TPU v7x, 32 devices: a whole 2x2x4 slice. The times are simulated.
32 devices in a mesh: seq: 4 (over x, core), res: 8 (over z, y).
Axes of the slice: x: 2, y: 2, z: 4, core: 2. Of those that a mesh axis runs over, the one named last changes fastest.
Arguments:
- homolog_embedding: bfloat16 [16, 512, 256], P('seq', 'res'), may hold values from -6 to 6
- pair_input_rows: bfloat16 [512, 512, 128], P('res', 'seq'), may hold values from -256 to 256
- incoming_slope: bfloat16 [16, 512, 256], P('seq', 'res'), may hold values from -6 to 6
- rescale_factor: float32 [256], replicated, may hold values from 0.25 to 1.75
- probe_weights: bfloat16 [256, 256], replicated, may hold values from -0.375 to 0.375
- lookup_weights: bfloat16 [256, 256], replicated, may hold values from -0.375 to 0.375
- content_weights: bfloat16 [256, 256], replicated, may hold values from -0.375 to 0.375
- sigmoid_weights: bfloat16 [256, 256], replicated, may hold values from -0.375 to 0.375
- final_projection: bfloat16 [256, 256], replicated, may hold values from -0.375 to 0.375
- pair_bias_matrix: bfloat16 [128, 8], replicated, may hold values from -1 to 1
Outputs:
- alignment_rows_gradient: bfloat16 [16, 512, 256], P('seq', 'res')
- pair_input_gradient: bfloat16 [512, 512, 128], P('res', 'seq')
- layer_gain_gradient: float32 [256], replicated
- query_matrix_gradient: float32 [256, 256], replicated
- key_matrix_gradient: float32 [256, 256], replicated
- value_matrix_gradient: float32 [256, 256], replicated
- gate_matrix_gradient: float32 [256, 256], replicated
- final_projection_slope: float32 [256, 256], replicated
- pair_bias_matrix_gradient: float32 [128, 8], replicated
All inputs are finite; a program needn't handle non-finite values.
Results may differ from a plain program's by a relative error of at most 0.0034.
The roundings to bfloat16 on the way count: a program that leaves them out, or rounds other values in their place, can miss the bound.
Values may be sent and summed in bfloat16 or wider, within the bound.
No kernel may reach another device: no remote copies, remote signals or barrier semaphores. Data moves between devices by JAX's collectives and lax.ppermute only.
A program may use at most 128 MiB of HBM per device.

v0:
```python
import functools
import math

import jax
import jax.numpy as jnp
from jax import lax
from jax.sharding import PartitionSpec as P


def layer_norm_rows(alignment_block):
    content_vectors = alignment_block.astype(jnp.float32)
    centered = content_vectors - jnp.mean(content_vectors, axis=-1, keepdims=True)
    inverse_deviation = lax.rsqrt(jnp.mean(centered * centered, axis=-1, keepdims=True) + 1e-05)
    return (centered * inverse_deviation, inverse_deviation)


def row_backward(bias_full, head_count, dbias_total, row_inputs):
    probe_vectors, keys_row, values_row, gate_row, derivative_modulated = row_inputs
    query_total, channel_width = probe_vectors.shape
    key_count = keys_row.shape[0]
    head_width = channel_width // head_count
    softmax_scale = 1.0 / math.sqrt(head_width)
    query_heads = probe_vectors.reshape(query_total, head_count, head_width)
    key_heads = keys_row.reshape(key_count, head_count, head_width)
    value_heads = values_row.reshape(key_count, head_count, head_width)
    scores = (
        jnp.einsum("ihd,jhd->hij", query_heads, key_heads, preferred_element_type=jnp.float32)
        * softmax_scale
    )
    scores = scores + bias_full.astype(jnp.float32)
    weights_soft = jax.nn.softmax(scores, axis=-1)
    weights_half = weights_soft.astype(jnp.bfloat16)
    attended = jnp.einsum(
        "hij,jhd->ihd", weights_half, value_heads, preferred_element_type=jnp.float32
    ).reshape(query_total, channel_width)
    modulated_result = (gate_row * attended).astype(jnp.bfloat16)
    grad_attended = (derivative_modulated * gate_row).astype(jnp.bfloat16)
    derivative_logits_sigmoid = (
        derivative_modulated * attended * gate_row * (1.0 - gate_row)
    ).astype(jnp.bfloat16)
    grad_heads = grad_attended.reshape(query_total, head_count, head_width)
    grad_weights = jnp.einsum(
        "ihd,jhd->hij", grad_heads, value_heads, preferred_element_type=jnp.float32
    )
    row_inner = jnp.sum(weights_soft * grad_weights, axis=-1, keepdims=True)
    grad_scores = weights_soft * (grad_weights - row_inner)
    scores_half = grad_scores.astype(jnp.bfloat16)
    derivative_probe_weights = (
        jnp.einsum("hij,jhd->ihd", scores_half, key_heads, preferred_element_type=jnp.float32)
        * softmax_scale
    ).astype(jnp.bfloat16)
    derivative_lookup_weights = (
        jnp.einsum("hij,ihd->jhd", scores_half, query_heads, preferred_element_type=jnp.float32)
        * softmax_scale
    )
    derivative_content_weights = jnp.einsum(
        "hij,ihd->jhd", weights_half, grad_heads, preferred_element_type=jnp.float32
    )
    outputs = (
        modulated_result,
        derivative_logits_sigmoid,
        derivative_probe_weights.reshape(query_total, channel_width),
        derivative_lookup_weights.reshape(key_count, channel_width),
        derivative_content_weights.reshape(key_count, channel_width),
    )
    return (dbias_total + grad_scores, outputs)


def body(
    homolog_embedding,
    pair_input_rows,
    incoming_slope,
    rescale_factor,
    probe_weights,
    lookup_weights,
    content_weights,
    sigmoid_weights,
    final_projection,
    pair_bias_matrix,
):
    highest = lax.Precision.HIGHEST
    head_count = pair_bias_matrix.shape[1]
    row_total, query_total, channel_width = homolog_embedding.shape
    standardized_rows, inverse_deviation = layer_norm_rows(homolog_embedding)
    rescaled_embedding = (standardized_rows * rescale_factor).astype(jnp.bfloat16)
    rescaled_plain = rescaled_embedding.reshape(-1, channel_width)
    probe_vectors = (
        jnp.dot(rescaled_plain, probe_weights, preferred_element_type=jnp.float32)
        .astype(jnp.bfloat16)
        .reshape(row_total, query_total, channel_width)
    )
    sigmoid_factors = jax.nn.sigmoid(
        jnp.dot(rescaled_plain, sigmoid_weights, preferred_element_type=jnp.float32)
    ).reshape(row_total, query_total, channel_width)
    incoming_slope_plain = incoming_slope.reshape(-1, channel_width)
    derivative_modulated = jnp.dot(
        incoming_slope_plain, final_projection.T, preferred_element_type=jnp.float32
    ).reshape(row_total, query_total, channel_width)
    bias_local = jnp.einsum(
        "ijc,ch->hij", pair_input_rows, pair_bias_matrix, preferred_element_type=jnp.float32
    ).astype(jnp.bfloat16)
    bias_full = lax.all_gather(bias_local, "seq", axis=2, tiled=True)
    normed_all = lax.all_gather(rescaled_embedding, "res", axis=1, tiled=True)
    key_count = normed_all.shape[1]
    all_flat = normed_all.reshape(-1, channel_width)
    lookup_vectors = (
        jnp.dot(all_flat, lookup_weights, preferred_element_type=jnp.float32)
        .astype(jnp.bfloat16)
        .reshape(row_total, key_count, channel_width)
    )
    content_vectors = (
        jnp.dot(all_flat, content_weights, preferred_element_type=jnp.float32)
        .astype(jnp.bfloat16)
        .reshape(row_total, key_count, channel_width)
    )
    dbias_init = jnp.zeros(bias_full.shape, jnp.float32)
    dbias_local, row_results = lax.scan(
        functools.partial(row_backward, bias_full, head_count),
        dbias_init,
        (probe_vectors, lookup_vectors, content_vectors, sigmoid_factors, derivative_modulated),
    )
    (
        modulated_result,
        derivative_logits_sigmoid,
        derivative_probe_weights,
        derivative_lookup_weights,
        derivative_content_weights,
    ) = row_results
    key_weight_wide = lookup_weights.astype(jnp.float32)
    value_weight_wide = content_weights.astype(jnp.float32)
    lookup_plain = derivative_lookup_weights.reshape(-1, channel_width)
    content_plain = derivative_content_weights.reshape(-1, channel_width)
    key_term = (
        jnp.dot(lookup_plain, key_weight_wide.T, precision=highest)
        + jnp.dot(content_plain, value_weight_wide.T, precision=highest)
    ).reshape(row_total, -1, channel_width)
    grad_from_keys = lax.psum_scatter(key_term, "res", scatter_dimension=1, tiled=True).reshape(
        -1, channel_width
    )
    all_wide = all_flat.astype(jnp.float32)
    part_key = jnp.dot(all_wide.T, lookup_plain, precision=highest)
    part_value = jnp.dot(all_wide.T, content_plain, precision=highest)
    probe_plain = derivative_probe_weights.reshape(-1, channel_width)
    sigmoid_factor_plain = derivative_logits_sigmoid.reshape(-1, channel_width)
    part_query = jnp.dot(rescaled_plain.T, probe_plain, preferred_element_type=jnp.float32)
    part_gate = jnp.dot(rescaled_plain.T, sigmoid_factor_plain, preferred_element_type=jnp.float32)
    part_out = jnp.dot(
        modulated_result.reshape(-1, channel_width).T,
        incoming_slope_plain,
        preferred_element_type=jnp.float32,
    )
    derivative_rescaled = (
        jnp.dot(probe_plain, probe_weights.T, preferred_element_type=jnp.float32)
        + jnp.dot(sigmoid_factor_plain, sigmoid_weights.T, preferred_element_type=jnp.float32)
        + grad_from_keys
    )
    derivative_rescaled = derivative_rescaled.reshape(row_total, query_total, channel_width)
    part_gain = jnp.sum(derivative_rescaled * standardized_rows, axis=(0, 1))
    centered_scaled_gradient = derivative_rescaled * rescale_factor
    alignment_rows_gradient = (
        inverse_deviation
        * (
            centered_scaled_gradient
            - jnp.mean(centered_scaled_gradient, axis=-1, keepdims=True)
            - standardized_rows
            * jnp.mean(centered_scaled_gradient * standardized_rows, axis=-1, keepdims=True)
        )
    ).astype(jnp.bfloat16)
    dbias_own = lax.psum_scatter(dbias_local, "seq", scatter_dimension=2, tiled=True).astype(
        jnp.bfloat16
    )
    pair_input_gradient = jnp.einsum(
        "hij,ch->ijc", dbias_own, pair_bias_matrix, preferred_element_type=jnp.float32
    ).astype(jnp.bfloat16)
    part_bias = jnp.einsum(
        "ijc,hij->ch", pair_input_rows, dbias_own, preferred_element_type=jnp.float32
    )
    totals = lax.psum(
        (part_gain, part_query, part_key, part_value, part_gate, part_out, part_bias),
        ("seq", "res"),
    )
    return (
        alignment_rows_gradient,
        pair_input_gradient,
        totals[0],
        totals[1],
        totals[2],
        totals[3],
        totals[4],
        totals[5],
        totals[6],
    )


def solution(mesh):
    in_specs = (
        P("seq", "res", None),
        P("res", "seq", None),
        P("seq", "res", None),
        P(),
        P(),
        P(),
        P(),
        P(),
        P(),
        P(),
    )
    out_specs = (P("seq", "res", None), P("res", "seq", None), P(), P(), P(), P(), P(), P(), P())
    return jax.shard_map(body, mesh=mesh, in_specs=in_specs, out_specs=out_specs, check_vma=False)
```

profile of v0, /device:TPU:0, one launch (start us, length us, event | category | flops | bytes accessed | tf_op | source)
XLA Modules:
  0.0 379.8 jit_solution(11783316702636671667)
XLA Ops:
  7.2 1.2 convert_reduce_fusion
  8.4 1.1 fusion.32
  9.5 1.7 fusion.26
  11.4 1.4 convolution_convert_fusion.3
  12.8 8.8 %all_gather.7 = bf16[8,64,512]{2,0,1:T(8,128)(2,1)S(1)} all-gather(bf16[8,64,128]{2,0,1:T(8,128)(2,1)S(1)} %convolution_convert_fusion.3), channel_id=1, replica_groups=mesh['seq'=4,'res'=8] {'seq'}, dimensions={2}, use_global_device_ids=true | all-gather | bytes 655360 | tf_op jit(solution)/shard_map/all_gather | solution.py:102
  24.0 30.3 %all-gather.2.cloned.1.call-done = bf16[4,512,256]{2,1,0:T(8,128)(2,1)} async-done(((bf16[4,64,256]{2,1,0:T(8,128)(2,1)}), bf16[4,512,256]{2,1,0:T(8,128)(2,1)}) %all-gather.2.cloned.1.call-update) | async-done | bytes 1048592 | tf_op jit(solution)/shard_map/all_gather | solution.py:103
  54.3 2.7 convolution_convert_fusion
  57.0 1.4 convolution_convert_fusion.1
  58.4 71.3 %while.21 = (s32[]{:T(128)}, f32[8,64,512]{2,1,0:T(8,128)}, bf16[4,64,256]{1,2,0:T(8,128)(2,1)}, bf16[4,64,256]{1,2,0:T(8,128)(2,1)}, bf16[4,64,256]{1,2,0:T(8,1...) while((s32[]{:T(128)}, f32[8,64,512]{2,1,0:T(8,128)}, ...), condition=%wide.region_6.7_spmd.clone, body=%wide.region_2.6_spmd.clone.sunk | while | flops 141346816 | bytes 32225668 | solution.py:117
  62.8 1.6 fusion.123
  64.4 2.5 fusion.124
  66.9 1.7 fusion.125
  69.2 2.6 fusion.128
  71.8 1.5 multiply_reduce_fusion.3
  80.6 1.6 fusion.123
  82.2 2.5 fusion.124
  84.7 1.7 fusion.125
  87.1 2.6 fusion.128
  89.7 1.5 multiply_reduce_fusion.3
  98.5 1.6 fusion.123
  100.1 2.5 fusion.124
  102.5 1.7 fusion.125
  104.9 2.6 fusion.128
  107.5 1.5 multiply_reduce_fusion.3
  116.3 1.6 fusion.123
  117.9 2.5 fusion.124
  120.4 1.7 fusion.125
  122.7 2.6 fusion.128
  125.3 1.5 multiply_reduce_fusion.3
  129.8 2.9 copy.40
  132.8 3.1 copy.41
  135.8 2.9 fusion.41
  138.7 2.4 convolution_add_fusion
  141.5 1.9 copy.39
  144.1 2.1 convolution_bitcast_fusion.1
  147.2 1.9 convolution_bitcast_fusion
  149.2 1.3 fusion.40
  150.5 2.2 convolution_bitcast_fusion.3
  152.7 2.2 convolution_bitcast_fusion.4
  156.4 2.2 convolution_convert_fusion.2
  158.6 67.0 %reduce-scatter.3.cloned.1.call-done = f32[4,64,256]{2,1,0:T(8,128)} async-done(((f32[4,512,256]{2,1,0:T(8,128)}), f32[4,64,256]{2,1,0:T(8,128)}) %reduce-scatter.3.cloned.1.call-update) | async-done | bytes 262160 | tf_op jit(solution)/shard_map/reduce_scatter | solution.py:137
  225.6 1.3 multiply_reduce_fusion.1
  227.2 39.8 %all-reduce = (f32[256]{0:T(256)}, f32[128,8]{0,1:T(8,128)}) all-reduce(f32[256]{0:T(256)S(1)} %get-tuple-element.155, f32[128,8]{0,1:T(8,128)S(1)} %convolution_bitcast_fusion.5), channel_id=1, replica_groups=mesh['seq'=4,'res'=8] {'seq','res'}, use_global_device_ids=true, to_apply=%region_12.13 | all-reduce | flops 1280 | bytes 10240 | tf_op jit(solution)/shard_map/psum | solution.py:178
  267.9 98.0 %all-reduce.4.cloned.1.call-done = (f32[256,256]{1,0:T(8,128)}, f32[256,256]{1,0:T(8,128)}, f32[256,256]{1,0:T(8,128)}, f32[256,256]{1,0:T(8,128)}, f32[256,256]{1,0:T(8,128)}) async-done(((f32[256,256]{1,0:T(8,128)}, f32[256,256]{1,0:T(8,128)}, f32[256,256]{1,0:T(8,128)}, f32[256,256]{1,0:T(8,128)}, f32[256,256]{1,0:T(8,128)}), (f32[256,256]{1,0:T(8,128)}, f32[256,256]{1,0:T(8,128)}, f32[256,256]{1,0:T(8,128)}, ...) | async-done | bytes 1310736 | tf_op jit(solution)/shard_map/psum | solution.py:178
  365.9 1.7 copy.102
  367.6 1.7 copy.103
  369.2 1.7 copy.104
  370.9 1.7 copy.105
  (189 shorter events, 39.3 us)
Async XLA Ops:
  7.2 4.2 %copy-start = (bf16[64,128,128]{2,1,0:T(8,128)(2,1)S(1)}, bf16[64,128,128]{2,1,0:T(8,128)(2,1)}, u32[]{:S(2)}) copy-start(bf16[64,128,128]{2,1,0:T(8,128)(2,1)} %param.13) | copy-start | bytes 6291460
  7.2 47.1 %all-gather.2.cloned.1.call-start = ((), (), s32[]{:S(2)}) async-start(), calls=%async_computation.2 | async-start | bytes 1179648 | tf_op jit(solution)/shard_map/all_gather | solution.py:103
  11.2 11.2 %copy-start.9 = (bf16[4,64,256]{2,1,0:T(8,128)(2,1)S(1)}, bf16[4,64,256]{2,1,0:T(8,128)(2,1)}, u32[]{:S(2)}) copy-start(bf16[4,64,256]{2,1,0:T(8,128)(2,1)} %fusion.26) | copy-start | bytes 393220
  11.2 11.2 %copy-start.20 = (bf16[256,256]{1,0:T(8,128)(2,1)S(1)}, bf16[256,256]{1,0:T(8,128)(2,1)}, u32[]{:S(2)}) copy-start(bf16[256,256]{1,0:T(8,128)(2,1)} %param.16) | copy-start | bytes 393220
  11.2 143.7 %reduce-scatter.5.cloned.1.call-start = ((), (), s32[]{:S(2)}) async-start(), calls=%async_computation.4 | async-start | bytes 1310720 | tf_op jit(solution)/shard_map/reduce_scatter | solution.py:169
  11.4 11.3 %copy-start.26 = (bf16[256,256]{1,0:T(8,128)(2,1)S(1)}, bf16[256,256]{1,0:T(8,128)(2,1)}, u32[]{:S(2)}) copy-start(bf16[256,256]{1,0:T(8,128)(2,1)} %param.19) | copy-start | bytes 393220
  12.7 10.2 %copy-start.19 = (bf16[4,64,256]{2,1,0:T(8,128)(2,1)S(1)}, bf16[4,64,256]{2,1,0:T(8,128)(2,1)}, u32[]{:S(2)}) copy-start(bf16[4,64,256]{2,1,0:T(8,128)(2,1)} %param.14) | copy-start | bytes 393220
  12.7 10.2 %copy-start.25 = (bf16[256,256]{1,0:T(8,128)(2,1)S(1)}, bf16[256,256]{1,0:T(8,128)(2,1)}, u32[]{:S(2)}) copy-start(bf16[256,256]{1,0:T(8,128)(2,1)} %param.20) | copy-start | bytes 393220
  12.7 41.5 %copy-start.17 = (bf16[256,256]{1,0:T(8,128)(2,1)S(1)}, bf16[256,256]{1,0:T(8,128)(2,1)}, u32[]{:S(2)}) copy-start(bf16[256,256]{1,0:T(8,128)(2,1)} %param.18) | copy-start | bytes 393220
  22.7 34.4 %copy-start.15 = (bf16[256,256]{1,0:T(8,128)(2,1)S(1)}, bf16[256,256]{1,0:T(8,128)(2,1)}, u32[]{:S(2)}) copy-start(bf16[256,256]{1,0:T(8,128)(2,1)} %param.17) | copy-start | bytes 393220
  54.3 2.8 copy-start.3
  58.4 3.2 copy-start.22
  71.8 1.5 copy-start.1
  73.8 2.5 copy-start.2
  73.8 1.4 copy-start.5
  73.8 2.5 copy-start.23
  74.1 2.2 copy-start.14
  76.3 3.2 copy-start.22
  89.7 1.5 copy-start.1
  91.6 2.5 copy-start.2
  91.6 2.5 copy-start.23
  91.9 2.2 copy-start.14
  94.1 3.2 copy-start.22
  107.5 1.5 copy-start.1
  109.4 2.5 copy-start.2
  109.5 2.5 copy-start.23
  109.7 2.2 copy-start.14
  111.9 3.2 copy-start.22
  125.3 1.5 copy-start.1
  127.3 2.5 copy-start.2
  127.3 2.5 copy-start.23
  127.6 2.2 copy-start.14
  129.8 95.8 %reduce-scatter.3.cloned.1.call-start = ((), (), s32[]{:S(2)}) async-start(), calls=%async_computation.3 | async-start | bytes 2359296 | tf_op jit(solution)/shard_map/reduce_scatter | solution.py:137
  132.8 3.1 copy-start.16
  135.8 2.9 copy-start.6
  135.8 2.9 copy-start.18
  141.2 2.2 copy-start.12
  141.2 2.9 copy-start.10
  141.2 9.3 %copy-start.4 = (bf16[4,512,256]{2,1,0:T(8,128)(2,1)S(1)}, bf16[4,512,256]{2,1,0:T(8,128)(2,1)}, u32[]{:S(2)}) copy-start(bf16[4,512,256]{2,1,0:T(8,128)(2,1)} %all-gather.2.cloned.1.call-done) | copy-start | bytes 3145732
  141.2 224.6 %all-reduce.4.cloned.1.call-start = ((), (), s32[]{:S(2)}) async-start(), calls=%async_computation.5 | async-start | bytes 2621440 | tf_op jit(solution)/shard_map/psum | solution.py:178
  144.1 6.4 %copy-start.7 = (f32[4,512,256]{1,2,0:T(8,128)S(1)}, f32[4,512,256]{1,2,0:T(8,128)}, u32[]{:S(2)}) copy-start(f32[4,512,256]{1,2,0:T(8,128)} %get-tuple-element.84) | copy-start | bytes 6291460
  149.2 3.5 copy-start.8
  154.9 1.5 copy-start.29
  155.9 69.7 %copy-start.21 = (bf16[4,64,256]{2,1,0:T(8,128)(2,1)S(1)}, bf16[4,64,256]{2,1,0:T(8,128)(2,1)}, u32[]{:S(2)}) copy-start(bf16[4,64,256]{2,1,0:T(8,128)(2,1)} %copy.39) | copy-start | bytes 393220
  155.9 69.7 %copy-start.27 = (bf16[256,256]{1,0:T(8,128)(2,1)S(1)}, bf16[256,256]{1,0:T(8,128)(2,1)}, u32[]{:S(2)}) copy-start(bf16[256,256]{1,0:T(8,128)(2,1)} %param.19) | copy-start | bytes 393220
  155.9 69.7 %copy-start.28 = (f32[256]{0:T(256)S(1)}, f32[256]{0:T(256)}, u32[]{:S(2)}) copy-start(f32[256]{0:T(256)} %param.15) | copy-start | bytes 3076
  156.4 70.6 %copy-start.11 = (bf16[4,64,256]{2,1,0:T(8,128)(2,1)S(1)}, bf16[4,64,256]{2,1,0:T(8,128)(2,1)}, u32[]{:S(2)}) copy-start(bf16[4,64,256]{2,1,0:T(8,128)(2,1)} %param.12) | copy-start | bytes 393220
  365.9 6.7 %copy-start.24 = (f32[256,256]{1,0:T(8,128)S(1)}, f32[256,256]{1,0:T(8,128)}, u32[]{:S(2)}) copy-start(f32[256,256]{1,0:T(8,128)} %get-tuple-element.362) | copy-start | bytes 786436
  (7 other events, 6.9 us)
Sparse Core Ops, SparseCore 0:
  11.4 42.8 all-gather.1
  129.9 23.6 reduce-scatter.4
  157.5 68.0 reduce-scatter.2
  233.3 132.4 all-reduce.3
where the time goes:
time: 381 us; the launch traced here: 380 us
  waiting for transfers between devices  195 us (51%)
  matrix products  61.6 us (16%)
  blocking collectives  48.6 us (13%)
  local copies, waits for them, and re-layouts  44.9 us (12%)
  other arithmetic  14.6 us (4%)
  between operations  14.1 us (4%)
    psum x1, waiting for transfers between devices, body(): lax.psum((part_gain, part_query, part_key, part_value, part_gate, part_ou...  98 us
    reduce_scatter x1, waiting for transfers between devices, body(): lax.psum_scatter(key_term, 'res', scatter_dimension=1, tiled=True)  67 us
    psum x1, blocking collectives, body(): lax.psum((part_gain, part_query, part_key, part_value, part_gate, part_ou...  39.8 us
    all_gather x1, waiting for transfers between devices, body(): normed_all = lax.all_gather(rescaled_embedding, 'res', axis=1, tiled=True)  30.3 us
    dynamic_slice x32, local copies, waits for them, and re-layouts, body(): lax.scan(functools.partial(row_backward, bias_full, head_count), dbias_in...  15.3 us
    dot_general x4, matrix products, row_backward(): jnp.einsum('hij,ihd->jhd', weights_half, grad_heads, preferred_element_ty...  10.5 us
    dot_general x4, matrix products, row_backward(): jnp.einsum('hij,jhd->ihd', weights_half, value_heads, preferred_element_t...  9.9 us
    dynamic_update_slice x12, local copies, waits for them, and re-layouts, body(): lax.scan(functools.partial(row_backward, bias_full, head_count), dbias_in...  9.33 us
  transfers between devices with their start and end apart: 4, of which 3 were waited for; matrix products, arithmetic and copies ran while one was open for 9% of the time, Pallas kernels for 0%

commit v1 on v0

--- a/solution.py
+++ b/solution.py
@@ -4,7 +4,332 @@
 import jax
 import jax.numpy as jnp
 from jax import lax
+from jax.experimental import pallas as pl
+from jax.experimental.pallas import tpu as pltpu
 from jax.sharding import PartitionSpec as P
+
+F32 = jnp.float32
+BF16 = jnp.bfloat16
+
+
+def exchange(value, axis, size, offset):
+    return lax.ppermute(value, axis, [(i, i ^ offset) for i in range(size)])
+
+
+def dot(a, b, dims=((1,), (0,))):
+    return lax.dot_general(a, b, (dims, ((), ())), preferred_element_type=F32)
+
+
+def norm_rows(block):
+    wide = block.astype(F32)
+    centered = wide - jnp.mean(wide, axis=-1, keepdims=True)
+    inverse = lax.rsqrt(jnp.mean(centered * centered, axis=-1, keepdims=True) + 1e-05)
+    return centered * inverse, inverse
+
+
+def attention_kernel(
+    n_res,
+    n_seq,
+    width,
+    span,
+    where,
+    *refs,
+):
+    tokens = refs[:n_res]
+    biases = refs[n_res : n_res + n_seq]
+    head_w, out_w, gain_w = refs[n_res + n_seq : n_res + n_seq + 3]
+    refs = refs[n_res + n_seq + 3 :]
+    grads, (pair_keep, pair_send, sums_keep, sums_send) = refs[:n_res], refs[n_res : n_res + 4]
+    hat_s, normed_s, slope_s, bias_s, dbias_s, grad_s, sums_s = refs[n_res + 4 :]
+    row, last = pl.program_id(0), pl.num_programs(0) - 1
+    r, s = where[0], where[1]
+    own = tokens[0].shape[2]
+    total = own * n_res
+    part = total // n_seq
+    channels = normed_s.shape[1]
+    scale = 1.0 / math.sqrt(width)
+
+    @pl.when(row == 0)
+    def _():
+        for m in range(n_seq):
+            lane = pl.multiple_of(jnp.bitwise_xor(s, m) * part, part)
+            for k in range(n_res):
+                at = pl.multiple_of(jnp.bitwise_xor(r, k) * own, own)
+                bias_s[pl.ds(at, own), pl.ds(lane, part)] = biases[m][k]
+        dbias_s[...] = jnp.zeros_like(dbias_s)
+        sums_s[...] = jnp.zeros_like(sums_s)
+
+    for k in range(n_res):
+        at = pl.multiple_of(jnp.bitwise_xor(r, k) * own, own)
+        hat, _ = norm_rows(tokens[k][0, 0])
+        hat_s[pl.ds(at, own), :] = hat
+        normed_s[pl.ds(at, own), :] = (hat * gain_w[...]).astype(BF16)
+        slope_s[pl.ds(at, own), :] = tokens[k][1, 0]
+
+    normed = normed_s[...]
+    slope = slope_s[...]
+    weights = head_w[0]
+    wq, wk, wv, wg = (weights[n * width : (n + 1) * width] for n in range(4))
+    rows = ((1,), (1,))
+    q = dot(normed, wq, rows).astype(BF16)
+    k_ = dot(normed, wk, rows).astype(BF16)
+    v = dot(normed, wv, rows).astype(BF16)
+    gate = jax.nn.sigmoid(dot(normed, wg, rows))
+    dgated = dot(slope, out_w[0], rows)
+    datt = (dgated * gate).astype(BF16)
+    q_t, k_t, v_t, datt_t = (jnp.transpose(x) for x in (q, k_, v, datt))
+
+    gk_t = jnp.zeros((width, total), F32)
+    gv_t = jnp.zeros((width, total), F32)
+    gqs, atts = [], []
+    for c in range(total // span):
+        lo, hi = c * span, (c + 1) * span
+        scores = dot(q[lo:hi], k_t) * scale + bias_s[lo:hi, :].astype(F32)
+        top = jnp.max(scores, axis=-1, keepdims=True)
+        e = jnp.exp(scores - top)
+        soft = e * (1.0 / jnp.sum(e, axis=-1, keepdims=True))
+        half = soft.astype(BF16)
+        atts.append(dot(half, v))
+        gv_t += dot(datt_t[:, lo:hi], half)
+        dsoft = dot(datt[lo:hi], v_t)
+        inner = jnp.sum(soft * dsoft, axis=-1, keepdims=True)
+        dscores = soft * (dsoft - inner)
+        dbias_s[lo:hi, :] += dscores
+        dhalf = dscores.astype(BF16)
+        gqs.append(dot(dhalf, k_) * scale)
+        gk_t += dot(q_t[:, lo:hi], dhalf)
+    att = jnp.concatenate(atts, axis=0)
+    gated = (gate * att).astype(BF16)
+    dgate = dgated * att * gate * (1.0 - gate)
+    gq = jnp.concatenate(gqs, axis=0)
+    grad_t = jnp.concatenate([jnp.transpose(gq), gk_t * scale, gv_t, jnp.transpose(dgate)], axis=0)
+    grad_s[...] = jnp.transpose(grad_t)
+    high_t = grad_t.astype(BF16)
+    part_row = lax.broadcasted_iota(jnp.int32, grad_t.shape, 0)
+    wide_rows = (part_row >= width) & (part_row < 3 * width)
+    low_t = jnp.where(wide_rows, grad_t - high_t.astype(F32), 0.0).astype(BF16)
+    sums_s[: 4 * width, :] += dot(high_t, normed) + dot(low_t, normed)
+    sums_s[4 * width : 5 * width, :] += dot(jnp.transpose(gated), slope)
+    grad_normed = dot(jnp.transpose(high_t), weights) + dot(jnp.transpose(low_t), weights)
+    sums_s[5 * width : 5 * width + 1, :] += jnp.sum(grad_normed * hat_s[...], axis=0, keepdims=True)
+    for k in range(n_res):
+        at = pl.multiple_of(jnp.bitwise_xor(r, k) * own, own)
+        grads[k][0] = grad_s[pl.ds(at, own), :].astype(BF16)
+
+    @pl.when(row == last)
+    def _():
+        for m in range(n_seq):
+            lane = pl.multiple_of(jnp.bitwise_xor(s, m) * part, part)
+            (pair_send if m % 2 else pair_keep)[m // 2] = dbias_s[:, pl.ds(lane, part)]
+        side = channels // 2
+        core = jnp.bitwise_and(s, 1)
+        sums_keep[...] = sums_s[:, pl.ds(pl.multiple_of(core * side, side), side)]
+        sums_send[...] = sums_s[:, pl.ds(pl.multiple_of((1 - core) * side, side), side)]
+
+
+def tail_kernel(n_res, where, *refs):
+    grads = refs[:n_res]
+    own_ref, weights, gain_w, out_ref = refs[n_res:]
+    r = where[0]
+    own = own_ref[...].reshape(-1, own_ref.shape[-1])
+    total = jnp.zeros(own.shape, F32)
+    for k in range(n_res):
+        block = grads[k][...].reshape(own.shape[0], -1)
+        total += dot(block, weights[jnp.bitwise_xor(r, k)])
+    hat, inverse = norm_rows(own)
+    g = total * gain_w[...]
+    mean = jnp.mean(g, axis=-1, keepdims=True)
+    cross = jnp.mean(g * hat, axis=-1, keepdims=True)
+    out_ref[...] = (inverse * (g - mean - hat * cross)).astype(BF16).reshape(out_ref.shape)
+
+
+def sums_kernel(n_res, width, where, mine, other, gain_ref, *outs):
+    r, s = where[0], where[1]
+    wide = outs[-1]
+    outs = outs[:-1]
+    side = mine.shape[2]
+    core = jnp.bitwise_and(s, 1)
+    here = pl.ds(pl.multiple_of(core * side, side), side)
+    there = pl.ds(pl.multiple_of((1 - core) * side, side), side)
+    gain = jnp.zeros((1, 2 * side), F32)
+    for k in range(n_res):
+        h = jnp.bitwise_xor(r, k)
+        for ref, lanes in ((mine, here), (other, there)):
+            block = ref[k].astype(F32)
+            for n in range(5):
+                rows = pl.ds(pl.multiple_of(h * width, width), width)
+                wide[n, rows, lanes] = block[n * width : (n + 1) * width]
+            wide[5, pl.ds(k, 1), lanes] = block[5 * width : 5 * width + 1] + block[5 * width + 1 : 5 * width + 2]
+    gain = jnp.sum(wide[5, :n_res, :], axis=0, keepdims=True)
+    gain_ref[...] = gain
+    for n in range(4):
+        outs[n][...] = jnp.transpose(wide[n])
+    outs[4][...] = wide[4]
+
+
+def whole(shape):
+    return pl.BlockSpec(shape, lambda *_: (0,) * len(shape))
+
+
+def by_head(
+    n_res,
+    n_seq,
+    homolog_embedding,
+    pair_input_rows,
+    incoming_slope,
+    rescale_factor,
+    probe_weights,
+    lookup_weights,
+    content_weights,
+    sigmoid_weights,
+    final_projection,
+    pair_bias_matrix,
+):
+    heads = pair_bias_matrix.shape[1]
+    rows, own, channels = homolog_embedding.shape
+    width = channels // heads
+    total = own * n_res
+    part = total // n_seq
+    r, s = lax.axis_index("res"), lax.axis_index("seq")
+    where = jnp.stack([r, s]).astype(jnp.int32)
+    gain_row = rescale_factor.reshape(1, channels)
+
+    both = jnp.stack([homolog_embedding, incoming_slope])
+    tokens = [None] * n_res
+    tokens[0] = both
+    for k in range(2, n_res, 2):
+        tokens[k] = exchange(both, "res", n_res, k)
+    for k in range(0, n_res, 2):
+        tokens[k + 1] = exchange(tokens[k], "res", n_res, 1)
+
+    bias_local = jnp.einsum(
+        "ijc,ch->hij", pair_input_rows, pair_bias_matrix, preferred_element_type=F32
+    ).astype(BF16)
+    bias_parts = [lax.dynamic_index_in_dim(bias_local, r ^ k, 0, keepdims=False) for k in range(n_res)]
+    bias_parts = [bias_parts[0]] + [exchange(bias_parts[k], "res", n_res, k) for k in range(1, n_res)]
+    bias_head = jnp.stack(bias_parts)
+    biases = [bias_head] + [exchange(bias_head, "seq", n_seq, m) for m in range(1, n_seq)]
+
+    by = [
+        w.T.reshape(heads, 1, width, channels)
+        for w in (probe_weights, lookup_weights, content_weights, sigmoid_weights)
+    ]
+    head_weights = jnp.concatenate(by, axis=1).reshape(heads, 4 * width, channels)
+    out_weights = final_projection.reshape(heads, width, channels)
+
+    token_spec = pl.BlockSpec((2, 1, own, channels), lambda i, w: (0, i, 0, 0))
+    grad_spec = pl.BlockSpec((1, own, 4 * width), lambda i, w: (i, 0, 0))
+    sum_rows = 5 * width + 16
+    side = channels // 2
+    span = min(total, 256)
+    outs = pl.pallas_call(
+        functools.partial(attention_kernel, n_res, n_seq, width, span),
+        grid_spec=pltpu.PrefetchScalarGridSpec(
+            num_scalar_prefetch=1,
+            grid=(rows,),
+            in_specs=[token_spec] * n_res
+            + [whole((n_res, own, part))] * n_seq
+            + [
+                pl.BlockSpec((1, 4 * width, channels), lambda i, w: (w[0], 0, 0)),
+                pl.BlockSpec((1, width, channels), lambda i, w: (w[0], 0, 0)),
+                whole((1, channels)),
+            ],
+            out_specs=[grad_spec] * n_res
+            + [whole((n_seq // 2, total, part))] * 2
+            + [whole((sum_rows, side))] * 2,
+            scratch_shapes=[
+                pltpu.VMEM((total, channels), F32),
+                pltpu.VMEM((total, channels), BF16),
+                pltpu.VMEM((total, channels), BF16),
+                pltpu.VMEM((total, total), BF16),
+                pltpu.VMEM((total, total), F32),
+                pltpu.VMEM((total, 4 * width), F32),
+                pltpu.VMEM((sum_rows, channels), F32),
+            ],
+        ),
+        out_shape=[jax.ShapeDtypeStruct((rows, own, 4 * width), BF16)] * n_res
+        + [jax.ShapeDtypeStruct((n_seq // 2, total, part), F32)] * 2
+        + [jax.ShapeDtypeStruct((sum_rows, side), F32)] * 2,
+        compiler_params=pltpu.CompilerParams(vmem_limit_bytes=48 * 1024 * 1024),
+        name="attention",
+    )(where, *tokens, *biases, head_weights, out_weights, gain_row)
+    grads, (pair_keep, pair_send, sums_keep, sums_send) = outs[:n_res], outs[n_res:]
+
+    pair_sum = pair_keep + exchange(pair_send, "seq", n_seq, 1)
+    sums = sums_keep + exchange(sums_send, "seq", n_seq, 1)
+    step = 2
+    while step < n_seq:
+        half = pair_sum.shape[0] // 2
+        pair_sum = pair_sum.reshape(half, 2, total, part)
+        pair_sum = pair_sum[:, 0] + exchange(pair_sum[:, 1], "seq", n_seq, step)
+        sums = sums + exchange(sums, "seq", n_seq, step)
+        step *= 2
+    pair_half = pair_sum.reshape(n_res, own, part).astype(BF16)
+    sums_half = sums.astype(BF16)
+    gain_at = 5 * width
+    rest = (sums[gain_at : gain_at + 1] - sums_half[gain_at : gain_at + 1].astype(F32)).astype(BF16)
+    sums_half = jnp.concatenate([sums_half[: gain_at + 1], rest, sums_half[gain_at + 2 :]], axis=0)
+
+    pair_parts = [lax.dynamic_index_in_dim(pair_half, r ^ k, 0, keepdims=False) for k in range(n_res)]
+    pair_parts = [pair_parts[0]] + [exchange(pair_parts[k], "res", n_res, k) for k in range(1, n_res)]
+    grads = [grads[0]] + [exchange(grads[k], "res", n_res, k) for k in range(1, n_res)]
+    sums_all = jnp.stack([sums_half] + [exchange(sums_half, "res", n_res, k) for k in range(1, n_res)])
+    sums_other = exchange(sums_all, "seq", n_seq, 1)
+
+    dbias_own = jnp.stack([lax.dynamic_index_in_dim(jnp.stack(pair_parts), r ^ h, 0, keepdims=False) for h in range(n_res)])
+    pair_input_gradient = jnp.einsum(
+        "hij,ch->ijc", dbias_own, pair_bias_matrix, preferred_element_type=F32
+    ).astype(BF16)
+    part_bias = jnp.einsum("ijc,hij->ch", pair_input_rows, dbias_own, preferred_element_type=F32)
+    for axis, size in (("seq", n_seq), ("res", n_res)):
+        step = 1
+        while step < size:
+            part_bias = part_bias + exchange(part_bias, axis, size, step)
+            step *= 2
+
+    alignment_rows_gradient = pl.pallas_call(
+        functools.partial(tail_kernel, n_res),
+        grid_spec=pltpu.PrefetchScalarGridSpec(
+            num_scalar_prefetch=1,
+            grid=(rows,),
+            in_specs=[grad_spec] * n_res
+            + [
+                pl.BlockSpec((1, own, channels), lambda i, w: (i, 0, 0)),
+                whole((heads, 4 * width, channels)),
+                whole((1, channels)),
+            ],
+            out_specs=pl.BlockSpec((1, own, channels), lambda i, w: (i, 0, 0)),
+        ),
+        out_shape=jax.ShapeDtypeStruct(homolog_embedding.shape, BF16),
+        compiler_params=pltpu.CompilerParams(vmem_limit_bytes=32 * 1024 * 1024),
+        name="tail",
+    )(where, *grads, homolog_embedding, head_weights, gain_row)
+
+    square = jax.ShapeDtypeStruct((channels, channels), F32)
+    gain, dq, dk, dv, dg, dout = pl.pallas_call(
+        functools.partial(sums_kernel, n_res, width),
+        grid_spec=pltpu.PrefetchScalarGridSpec(
+            num_scalar_prefetch=1,
+            grid=(1,),
+            in_specs=[whole((n_res, sum_rows, side))] * 2,
+            out_specs=[whole((1, channels))] + [whole((channels, channels))] * 5,
+            scratch_shapes=[pltpu.VMEM((6, channels, channels), F32)],
+        ),
+        out_shape=[jax.ShapeDtypeStruct((1, channels), F32)] + [square] * 5,
+        compiler_params=pltpu.CompilerParams(vmem_limit_bytes=32 * 1024 * 1024),
+        name="sums",
+    )(where, sums_all, sums_other)
+    return (
+        alignment_rows_gradient,
+        pair_input_gradient,
+        gain.reshape(channels),
+        dq,
+        dk,
+        dv,
+        dg,
+        dout,
+        part_bias,
+    )
 
 
 def layer_norm_rows(alignment_block):
@@ -206,4 +531,11 @@
         P(),
     )
     out_specs = (P("seq", "res", None), P("res", "seq", None), P(), P(), P(), P(), P(), P(), P())
-    return jax.shard_map(body, mesh=mesh, in_specs=in_specs, out_specs=out_specs, check_vma=False)
+    n_res, n_seq = mesh.shape["res"], mesh.shape["seq"]
+
+    def run(*args):
+        if n_res == args[-1].shape[1] and n_res & (n_res - 1) == 0 and n_seq > 1 and n_seq & (n_seq - 1) == 0:
+            return by_head(n_res, n_seq, *args)
+        return body(*args)
+
+    return jax.shard_map(run, mesh=mesh, in_specs=in_specs, out_specs=out_specs, check_vma=False)

time: 381 us -> 187 us (0.49)
  waiting for transfers between devices: 195 us -> 73.5 us
  starting transfers between devices: 0.34 us -> 58.5 us
  matrix products: 61.6 us -> 4.89 us
  blocking collectives: 48.6 us -> 0 us
  Pallas kernels: 0 us -> 20.3 us
  local copies, waits for them, and re-layouts: 44.9 us -> 25.9 us
  between operations: 14.1 us -> 1.08 us
  other arithmetic: 14.6 us -> 2.72 us
    psum x1 -> x0, waiting for transfers between devices: 98 us -> none  [body(): lax.psum((part_gain, part_query, part_key, part_value, part_gate, part_ou...]
    ppermute x0 -> x48, waiting for transfers between devices: none -> 73.5 us  [exchange(): return lax.ppermute(value, axis, [(i, i ^ offset) for i in range(size)])]
    reduce_scatter x2 -> x0, waiting for transfers between devices: 67 us -> none  [the longest x1 67 us: body(): lax.psum_scatter(key_term, 'res', scatter_dimension=1, tiled=True)]
    ppermute x0 -> x48, starting transfers between devices: none -> 58.5 us  [exchange(): return lax.ppermute(value, axis, [(i, i ^ offset) for i in range(size)])]
    dot_general x37 -> x3, matrix products: 55.2 us -> 4.89 us  [the longest x1 2.24 us: by_head(): jnp.einsum('hij,ch->ijc', dbias_own, pair_bias_matrix, preferred_element_...]
    psum x1 -> x0, blocking collectives: 39.8 us -> none  [body(): lax.psum((part_gain, part_query, part_key, part_value, part_gate, part_ou...]
    all_gather x1 -> x0, waiting for transfers between devices: 30.3 us -> none  [body(): normed_all = lax.all_gather(rescaled_embedding, 'res', axis=1, tiled=True)]
    pallas_call x0 -> x3, Pallas kernels: none -> 20.3 us  [the longest x1 14.6 us: by_head(): pl.pallas_call(functools.partial(attention_kernel, n_res, n_seq, width, s...]
  transfers between devices with their start and end apart: 4 -> 48, of which waited for: 3 -> 19; matrix products, arithmetic and copies ran while one was open for 9% -> 14% of each run, Pallas kernels for 0% -> 3%
where the time goes in v1:
time: 187 us
  waiting for transfers between devices  73.5 us (39%)
  starting transfers between devices  58.5 us (31%)
  local copies, waits for them, and re-layouts  25.9 us (14%)
  Pallas kernels  20.3 us (11%)
  matrix products  4.89 us (3%)
  other arithmetic  2.72 us (1%)
    ppermute x48, waiting for transfers between devices, exchange(): return lax.ppermute(value, axis, [(i, i ^ offset) for i in range(size)])  73.5 us
    ppermute x48, starting transfers between devices, exchange(): return lax.ppermute(value, axis, [(i, i ^ offset) for i in range(size)])  58.5 us
    pallas_call x1, Pallas kernels, by_head(): pl.pallas_call(functools.partial(attention_kernel, n_res, n_seq, width, s...  14.6 us
    unnamed x61, local copies, waits for them, and re-layouts  12.5 us
    another operation x8, local copies, waits for them, and re-layouts, by_head(): jnp.stack(pair_parts)  6.34 us
  transfers between devices with their start and end apart: 48, of which 19 were waited for; matrix products, arithmetic and copies ran while one was open for 14% of the time, Pallas kernels for 3%

profile of v1, /device:TPU:0, one launch (start us, length us, event | category | flops | bytes accessed | tf_op | source)
XLA Modules:
  0.0 186.9 jit_solution(11829142018059370970)
XLA Ops:
  0.7 1.5 copy-done
  2.2 1.3 fusion.3
  4.3 3.0 %collective-permute-start.7 = (bf16[64,128]{1,0:T(8,128)(2,1)S(1)}, bf16[64,128]{1,0:T(8,128)(2,1)S(1)}, u32[]{:S(2)}, u32[]{:S(2)}) collective-permute-start(bf16[64,128]{1,0:T(8,128)(2,1)S(1)} %get-tuple-element.71), channel_id=1, source_target_pairs={{0,1},{1,0},{2,3},{3,2},{4,5},{5,4},{6,7},{7,6},{8,9},{9,8},{10,11... | collective-permute-start | bytes 49160 | tf_op jit(solution)/shard_map/ppermute | solution.py:16
  7.3 3.7 %collective-permute-start.5 = (bf16[2,4,64,256]{3,2,1,0:T(8,128)(2,1)S(1)}, bf16[2,4,64,256]{3,2,1,0:T(8,128)(2,1)S(1)}, u32[]{:S(2)}, u32[]{:S(2)}) collective-permute-start(bf16[2,4,64,256]{3,2,1,0:T(8,128)(2,1)S(1)} %pad_maximum_fusion.1.refs_0_), channel_id=1, source_target_pairs={{0,6},{1,7},{2,4},{3,5},{4,2},{5,3},{6,0},{7,1},{8,14},{9,15},{10,... | collective-permute-start | bytes 786440 | tf_op jit(solution)/shard_map/ppermute | solution.py:16
  11.7 3.5 %collective-permute-start.13 = (bf16[64,128]{1,0:T(8,128)(2,1)S(1)}, bf16[64,128]{1,0:T(8,128)(2,1)S(1)}, u32[]{:S(2)}, u32[]{:S(2)}) collective-permute-start(bf16[64,128]{1,0:T(8,128)(2,1)S(1)} %get-tuple-element.65), channel_id=1, source_target_pairs={{0,7},{1,6},{2,5},{3,4},{4,3},{5,2},{6,1},{7,0},{8,15},{9,14},{10,... | collective-permute-start | bytes 49160 | tf_op jit(solution)/shard_map/ppermute | solution.py:16
  15.9 12.4 %collective-permute-done.8 = bf16[64,128]{1,0:T(8,128)(2,1)S(1)} collective-permute-done((bf16[64,128]{1,0:T(8,128)(2,1)S(1)}, bf16[64,128]{1,0:T(8,128)(2,1)S(1)}, u32[]{:S(2)}, u32[]{:S(2)}) %collective-permute-start.8) | collective-permute-done | bytes 16416 | tf_op jit(solution)/shard_map/ppermute | solution.py:16
  28.3 2.4 %collective-permute-start.9 = (bf16[64,128]{1,0:T(8,128)(2,1)S(1)}, bf16[64,128]{1,0:T(8,128)(2,1)S(1)}, u32[]{:S(2)}, u32[]{:S(2)}) collective-permute-start(bf16[64,128]{1,0:T(8,128)(2,1)S(1)} %get-tuple-element.69), channel_id=1, source_target_pairs={{0,3},{1,2},{2,1},{3,0},{4,7},{5,6},{6,5},{7,4},{8,11},{9,10},{10,... | collective-permute-start | bytes 49160 | tf_op jit(solution)/shard_map/ppermute | solution.py:16
  31.3 2.4 %collective-permute-done.9 = bf16[64,128]{1,0:T(8,128)(2,1)S(1)} collective-permute-done((bf16[64,128]{1,0:T(8,128)(2,1)S(1)}, bf16[64,128]{1,0:T(8,128)(2,1)S(1)}, u32[]{:S(2)}, u32[]{:S(2)}) %collective-permute-start.9) | collective-permute-done | bytes 16416 | tf_op jit(solution)/shard_map/ppermute | solution.py:16
  34.8 3.5 %collective-permute-done.10 = bf16[64,128]{1,0:T(8,128)(2,1)S(1)} collective-permute-done((bf16[64,128]{1,0:T(8,128)(2,1)S(1)}, bf16[64,128]{1,0:T(8,128)(2,1)S(1)}, u32[]{:S(2)}, u32[]{:S(2)}) %collective-permute-start.10) | collective-permute-done | bytes 16416 | tf_op jit(solution)/shard_map/ppermute | solution.py:16
  39.8 4.1 %collective-permute-done.11 = bf16[64,128]{1,0:T(8,128)(2,1)S(1)} collective-permute-done((bf16[64,128]{1,0:T(8,128)(2,1)S(1)}, bf16[64,128]{1,0:T(8,128)(2,1)S(1)}, u32[]{:S(2)}, u32[]{:S(2)}) %collective-permute-start.11) | collective-permute-done | bytes 16416 | tf_op jit(solution)/shard_map/ppermute | solution.py:16
  45.6 3.9 %collective-permute-done.12 = bf16[64,128]{1,0:T(8,128)(2,1)S(1)} collective-permute-done((bf16[64,128]{1,0:T(8,128)(2,1)S(1)}, bf16[64,128]{1,0:T(8,128)(2,1)S(1)}, u32[]{:S(2)}, u32[]{:S(2)}) %collective-permute-start.12) | collective-permute-done | bytes 16416 | tf_op jit(solution)/shard_map/ppermute | solution.py:16
  50.7 1.5 collective-permute-start.15
  52.3 4.4 %collective-permute-done.16.refs_11_ = bf16[8,64,128]{2,1,0:T(8,128)(2,1)S(1)} collective-permute-done((bf16[8,64,128]{2,1,0:T(8,128)(2,1)}, bf16[8,64,128]{2,1,0:T(8,128)(2,1)S(1)}, u32[]{:S(2)}, u32[]{:S(2)}) %collective-permute-start.16) | collective-permute-done | bytes 131104 | tf_op jit(solution)/shard_map/ppermute | solution.py:16
  56.7 1.4 collective-permute-start
  58.7 1.4 collective-permute-start.4
  61.9 1.7 copy.28
  63.5 1.7 copy.29
  65.2 1.9 %pad_maximum_fusion = bf16[8,4,32,256]{3,2,0,1:T(8,128)(2,1)} fusion(bf16[8,1,32,256]{3,2,0,1:T(8,128)(2,1)} %bitcast.119, bf16[8,1,32,256]{3,2,0,1:T(8,128)(2,1)} %bitcast.118, bf16[8,1,32,256]{3,2,0,1:T(8,128)(2,1)S(1)} %bitcast.117, bf16[8,1,32,256]{3,2,0,1:T(8,128)(2,1)S(1)} %bitcast.116), kind=kLoop, calls=%fused_computation.2 | loop fusion | flops 786432 | bytes 1048576 | tf_op jit(solution)/shard_map/concatenate | solution.py:217
  68.3 3.3 %collective-permute-done.6.refs_7_ = bf16[2,4,64,256]{3,2,1,0:T(8,128)(2,1)} collective-permute-done((bf16[2,4,64,256]{3,2,1,0:T(8,128)(2,1)S(1)}, bf16[2,4,64,256]{3,2,1,0:T(8,128)(2,1)}, u32[]{:S(2)}, u32[]{:S(2)}) %collective-permute-start.6) | collective-permute-done | bytes 262176 | tf_op jit(solution)/shard_map/ppermute | solution.py:16
  71.6 5.6 %collective-permute-done.4.refs_5_ = bf16[2,4,64,256]{3,2,1,0:T(8,128)(2,1)} collective-permute-done((bf16[2,4,64,256]{3,2,1,0:T(8,128)(2,1)S(1)}, bf16[2,4,64,256]{3,2,1,0:T(8,128)(2,1)}, u32[]{:S(2)}, u32[]{:S(2)}) %collective-permute-start.4) | collective-permute-done | bytes 262176 | tf_op jit(solution)/shard_map/ppermute | solution.py:16
  77.2 4.8 %collective-permute-done.2.refs_3_ = bf16[2,4,64,256]{3,2,1,0:T(8,128)(2,1)} collective-permute-done((bf16[2,4,64,256]{3,2,1,0:T(8,128)(2,1)}, bf16[2,4,64,256]{3,2,1,0:T(8,128)(2,1)}, u32[]{:S(2)}, u32[]{:S(2)}) %collective-permute-start.2) | collective-permute-done | bytes 262176 | tf_op jit(solution)/shard_map/ppermute | solution.py:16
  84.7 14.6 %attention.1 = (bf16[4,64,128]{2,1,0:T(8,128)(2,1)S(1)}, bf16[4,64,128]{2,1,0:T(8,128)(2,1)}, bf16[4,64,128]{2,1,0:T(8,128)(2,1)}, bf16[4,64,128]{2,1,0:T(8,128)...) custom-call(s32[2]{0:T(128)S(1)} %pad_add_fusion.where, ...), custom_call_target="tpu_custom_call" | custom-call | tf_op jit(solution)/shard_map/attention/pallas_call | solution.py:225
  100.8 4.7 %collective-permute-done.34 = f32[176,128]{1,0:T(8,128)S(1)} collective-permute-done((f32[176,128]{1,0:T(8,128)S(1)}, f32[176,128]{1,0:T(8,128)S(1)}, u32[]{:S(2)}, u32[]{:S(2)}) %collective-permute-start.34) | collective-permute-done | bytes 90144 | tf_op jit(solution)/shard_map/ppermute | solution.py:16
  105.6 1.4 collective-permute-start.35
  108.4 2.6 %collective-permute-start.38 = (bf16[176,128]{1,0:T(8,128)(2,1)S(1)}, bf16[176,128]{1,0:T(8,128)(2,1)S(1)}, u32[]{:S(2)}, u32[]{:S(2)}) collective-permute-start(bf16[176,128]{1,0:T(8,128)(2,1)S(1)} %get-tuple-element.46), channel_id=1, source_target_pairs={{0,4},{1,5},{2,6},{3,7},{4,0},{5,1},{6,2},{7,3},{8,12},{9,13},{10,... | collective-permute-start | bytes 135176 | tf_op jit(solution)/shard_map/ppermute | solution.py:16
  111.5 4.0 %collective-permute-done.36 = bf16[176,128]{1,0:T(8,128)(2,1)S(1)} collective-permute-done((bf16[176,128]{1,0:T(8,128)(2,1)S(1)}, bf16[176,128]{1,0:T(8,128)(2,1)S(1)}, u32[]{:S(2)}, u32[]{:S(2)}) %collective-permute-start.36) | collective-permute-done | bytes 45088 | tf_op jit(solution)/shard_map/ppermute | solution.py:16
  116.4 4.0 %collective-permute-done.37 = bf16[176,128]{1,0:T(8,128)(2,1)S(1)} collective-permute-done((bf16[176,128]{1,0:T(8,128)(2,1)S(1)}, bf16[176,128]{1,0:T(8,128)(2,1)S(1)}, u32[]{:S(2)}, u32[]{:S(2)}) %collective-permute-start.37) | collective-permute-done | bytes 45088 | tf_op jit(solution)/shard_map/ppermute | solution.py:16
  120.5 3.2 %collective-permute-start.41 = (bf16[176,128]{1,0:T(8,128)(2,1)S(1)}, bf16[176,128]{1,0:T(8,128)(2,1)S(1)}, u32[]{:S(2)}, u32[]{:S(2)}) collective-permute-start(bf16[176,128]{1,0:T(8,128)(2,1)S(1)} %get-tuple-element.46), channel_id=1, source_target_pairs={{0,7},{1,6},{2,5},{3,4},{4,3},{5,2},{6,1},{7,0},{8,15},{9,14},{10,... | collective-permute-start | bytes 135176 | tf_op jit(solution)/shard_map/ppermute | solution.py:16
  124.2 6.0 %collective-permute-done.25 = f32[1,512,128]{2,1,0:T(8,128)S(1)} collective-permute-done((f32[1,512,128]{2,1,0:T(8,128)S(1)}, f32[1,512,128]{2,1,0:T(8,128)S(1)}, u32[]{:S(2)}, u32[]{:S(2)}) %collective-permute-start.25) | collective-permute-done | bytes 262176 | tf_op jit(solution)/shard_map/ppermute | solution.py:16
  130.4 1.5 collective-permute-start.32
  131.9 2.8 %collective-permute-start.31 = (bf16[64,128]{1,0:T(8,128)(2,1)S(1)}, bf16[64,128]{1,0:T(8,128)(2,1)S(1)}, u32[]{:S(2)}, u32[]{:S(2)}) collective-permute-start(bf16[64,128]{1,0:T(8,128)(2,1)S(1)} %get-tuple-element.58), channel_id=1, source_target_pairs={{0,6},{1,7},{2,4},{3,5},{4,2},{5,3},{6,0},{7,1},{8,14},{9,15},{10,... | collective-permute-start | bytes 49160 | tf_op jit(solution)/shard_map/ppermute | solution.py:16
  134.8 3.4 %collective-permute-start.29 = (bf16[64,128]{1,0:T(8,128)(2,1)S(1)}, bf16[64,128]{1,0:T(8,128)(2,1)S(1)}, u32[]{:S(2)}, u32[]{:S(2)}) collective-permute-start(bf16[64,128]{1,0:T(8,128)(2,1)S(1)} %get-tuple-element.60), channel_id=1, source_target_pairs={{0,4},{1,5},{2,6},{3,7},{4,0},{5,1},{6,2},{7,3},{8,12},{9,13},{10,... | collective-permute-start | bytes 49160 | tf_op jit(solution)/shard_map/ppermute | solution.py:16
  138.2 2.4 %collective-permute-start.27 = (bf16[64,128]{1,0:T(8,128)(2,1)S(1)}, bf16[64,128]{1,0:T(8,128)(2,1)S(1)}, u32[]{:S(2)}, u32[]{:S(2)}) collective-permute-start(bf16[64,128]{1,0:T(8,128)(2,1)S(1)} %get-tuple-element.62), channel_id=1, source_target_pairs={{0,2},{1,3},{2,0},{3,1},{4,6},{5,7},{6,4},{7,5},{8,10},{9,11},{10,... | collective-permute-start | bytes 49160 | tf_op jit(solution)/shard_map/ppermute | solution.py:16
  145.3 2.5 %collective-permute-start.19 = (bf16[4,64,128]{2,1,0:T(8,128)(2,1)}, bf16[4,64,128]{2,1,0:T(8,128)(2,1)S(1)}, u32[]{:S(2)}, u32[]{:S(2)}) collective-permute-start(bf16[4,64,128]{2,1,0:T(8,128)(2,1)} %get-tuple-element.30), channel_id=1, source_target_pairs={{0,3},{1,2},{2,1},{3,0},{4,7},{5,6},{6,5},{7,4},{8,11},{9,10},{10,... | collective-permute-start | bytes 196616 | tf_op jit(solution)/shard_map/ppermute | solution.py:16
  149.7 1.9 %stack.85 = bf16[8,64,128]{2,0,1:T(8,128)(2,1)} concatenate(bf16[1,64,128]{2,0,1:T(2,128)(2,1)S(1)} %copy.39, bf16[1,64,128]{2,0,1:T(2,128)(2,1)} %copy.32, bf16[1,64,128]{2,0,1:T(2,128)(2,1)} %copy.33, bf16[1,64,128]{2,0,1:T(2,128)(2,1)} %copy.34, bf16[1,64,128]{2,0,1:T(2,128)(2,1)} %copy.35, bf16[1,64,128]{2,0,1:T(2,128)(2,1)} %copy.36, bf16[1,64,128]{2,0,1:T(2,128)(2,1)} %copy.37, ...), dimensions={0} | concatenate | bytes 262144 | tf_op jit(solution)/shard_map/stack | solution.py:279
  151.6 2.8 %constant_dynamic-slice_fusion = (bf16[1,64,128]{2,0,1:T(2,128)(2,1)S(1)}, bf16[1,64,128]{2,0,1:T(2,128)(2,1)}, bf16[1,64,128]{2,0,1:T(2,128)(2,1)}, bf16[1,64,1...) fusion(bf16[8,64,128]{2,0,1:T(8,128)(2,1)} %stack.85, ...), kind=kLoop, calls=%fused_computation.41 | loop fusion | bytes 262176 | tf_op jit(solution)/shard_map/jit(dynamic_index_in_dim)/dynamic_slice | solution.py:279
  154.4 1.9 %stack.86 = bf16[8,64,128]{2,0,1:T(8,128)(2,1)} concatenate(bf16[1,64,128]{2,0,1:T(2,128)(2,1)} %get-tuple-element.56, bf16[1,64,128]{2,0,1:T(2,128)(2,1)} %get-tuple-element.55, bf16[1,64,128]{2,0,1:T(2,128)(2,1)} %get-tuple-element.54, bf16[1,64,128]{2,0,1:T(2,128)(2,1)} %get-tuple-element.53, bf16[1,64,128]{2,0,1:T(2,128)(2,1)} %get-tuple-element.52, ...), dimensions={0} | concatenate | bytes 262144 | tf_op jit(solution)/shard_map/stack | solution.py:279
  156.3 1.3 convolution_bitcast_fusion
  159.3 3.3 %collective-permute-done.44 = f32[128,8]{0,1:T(8,128)S(1)} collective-permute-done((f32[128,8]{0,1:T(8,128)S(1)}, f32[128,8]{0,1:T(8,128)S(1)}, u32[]{:S(2)}, u32[]{:S(2)}) %collective-permute-start.44) | collective-permute-done | bytes 4128 | tf_op jit(solution)/shard_map/ppermute | solution.py:16
  163.7 3.3 %collective-permute-start.21 = (bf16[4,64,128]{2,1,0:T(8,128)(2,1)S(1)}, bf16[4,64,128]{2,1,0:T(8,128)(2,1)S(1)}, u32[]{:S(2)}, u32[]{:S(2)}) collective-permute-start(bf16[4,64,128]{2,1,0:T(8,128)(2,1)S(1)} %copy-done.15), channel_id=1, source_target_pairs={{0,5},{1,4},{2,7},{3,6},{4,1},{5,0},{6,3},{7,2},{8,13},{9,12},{10,... | collective-permute-start | bytes 196616 | tf_op jit(solution)/shard_map/ppermute | solution.py:16
  167.0 1.9 %collective-permute-start.22 = (bf16[4,64,128]{2,1,0:T(8,128)(2,1)S(1)}, bf16[4,64,128]{2,1,0:T(8,128)(2,1)S(1)}, u32[]{:S(2)}, u32[]{:S(2)}) collective-permute-start(bf16[4,64,128]{2,1,0:T(8,128)(2,1)S(1)} %copy-done.13), channel_id=1, source_target_pairs={{0,6},{1,7},{2,4},{3,5},{4,2},{5,3},{6,0},{7,1},{8,14},{9,15},{10,... | collective-permute-start | bytes 196616 | tf_op jit(solution)/shard_map/ppermute | solution.py:16
  168.9 2.3 %collective-permute-start.23 = (bf16[4,64,128]{2,1,0:T(8,128)(2,1)S(1)}, bf16[4,64,128]{2,1,0:T(8,128)(2,1)S(1)}, u32[]{:S(2)}, u32[]{:S(2)}) collective-permute-start(bf16[4,64,128]{2,1,0:T(8,128)(2,1)S(1)} %copy-done.11), channel_id=1, source_target_pairs={{0,7},{1,6},{2,5},{3,4},{4,3},{5,2},{6,1},{7,0},{8,15},{9,14},{10,... | collective-permute-start | bytes 196616 | tf_op jit(solution)/shard_map/ppermute | solution.py:16
  171.2 2.1 %collective-permute-done.20.refs_4_ = bf16[4,64,128]{2,1,0:T(8,128)(2,1)S(1)} collective-permute-done((bf16[4,64,128]{2,1,0:T(8,128)(2,1)S(1)}, bf16[4,64,128]{2,1,0:T(8,128)(2,1)S(1)}, u32[]{:S(2)}, u32[]{:S(2)}) %collective-permute-start.20) | collective-permute-done | bytes 65568 | tf_op jit(solution)/shard_map/ppermute | solution.py:16
  173.3 1.8 collective-permute-done.21.refs_5_
  176.0 2.8 %tail.1 = bf16[4,64,256]{2,1,0:T(8,128)(2,1)} custom-call(s32[2]{0:T(128)S(1)} %pad_add_fusion.where, bf16[4,64,128]{2,1,0:T(8,128)(2,1)S(1)} %copy-done.8, bf16[4,64,128]{2,1,0:T(8,128)(2,1)S(1)} %collective-permute-done.17.refs_1_, bf16[4,64,128]{2,1,0:T(8,128)(2,1)S(1)} %collective-permute-done.18.refs_2_, ...), custom_call_target="tpu_custom_call" | custom-call | tf_op jit(solution)/shard_map/tail/pallas_call | solution.py:290
  178.8 2.9 %sums.1 = (f32[1,256]{1,0:T(1,128)}, f32[256,256]{1,0:T(8,128)}, f32[256,256]{1,0:T(8,128)}, f32[256,256]{1,0:T(8,128)}, f32[256,256]{1,0:T(8,128)}, /*index=5*/f32[256,256]{1,0:T(8,128)}) custom-call(s32[2]{0:T(128)S(1)} %pad_add_fusion.where, bf16[8,176,128]{2,1,0:T(8,128)(2,1)S(1)} %bitcast_dynamic-update-slice_fusion.mine, ...), custom_call_target="tpu_custom_call" | custom-call | tf_op jit(solution)/shard_map/sums/pallas_call | solution.py:309
  181.7 2.3 %collective-permute-start.47 = (f32[128,8]{0,1:T(8,128)S(1)}, f32[128,8]{0,1:T(8,128)S(1)}, u32[]{:S(2)}, u32[]{:S(2)}) collective-permute-start(f32[128,8]{0,1:T(8,128)S(1)} %add.83), channel_id=1, source_target_pairs={{0,4},{1,5},{2,6},{3,7},{4,0},{5,1},{6,2},{7,3},{8,12},{9,13},{10,... | collective-permute-start | bytes 12296 | tf_op jit(solution)/shard_map/ppermute | solution.py:16
  184.0 2.2 %convolution_convert_fusion = bf16[64,128,128]{2,1,0:T(8,128)(2,1)} fusion(bf16[8,64,128]{2,0,1:T(8,128)(2,1)S(1)} %copy-done.18, bf16[128,8]{0,1:T(8,128)(2,1)S(1)} %copy-done.21), kind=kOutput, calls=%fused_computation | convolution fusion | flops 17825792 | bytes 2230272 | tf_op jit(solution)/shard_map/hij,ch->ijc/dot_general | solution.py:280
  (148 shorter events, 30.6 us)
Async XLA Ops:
  4.3 11.0 %collective-permute-start.7 = (bf16[64,128]{1,0:T(8,128)(2,1)S(1)}, bf16[64,128]{1,0:T(8,128)(2,1)S(1)}, u32[]{:S(2)}, u32[]{:S(2)}) collective-permute-start(bf16[64,128]{1,0:T(8,128)(2,1)S(1)} %get-tuple-element.71), channel_id=1, source_target_pairs={{0,1},{1,0},{2,3},{3,2},{4,5},{5,4},{6,7},{7,6},{8,9},{9,8},{10,11... | collective-permute-start | bytes 49160 | tf_op jit(solution)/shard_map/ppermute | solution.py:16
  7.3 50.8 %collective-permute-start.5 = (bf16[2,4,64,256]{3,2,1,0:T(8,128)(2,1)S(1)}, bf16[2,4,64,256]{3,2,1,0:T(8,128)(2,1)S(1)}, u32[]{:S(2)}, u32[]{:S(2)}) collective-permute-start(bf16[2,4,64,256]{3,2,1,0:T(8,128)(2,1)S(1)} %pad_maximum_fusion.1.refs_0_), channel_id=1, source_target_pairs={{0,6},{1,7},{2,4},{3,5},{4,2},{5,3},{6,0},{7,1},{8,14},{9,15},{10,... | collective-permute-start | bytes 786440 | tf_op jit(solution)/shard_map/ppermute | solution.py:16
  11.0 47.8 %collective-permute-start.3 = (bf16[2,4,64,256]{3,2,1,0:T(8,128)(2,1)S(1)}, bf16[2,4,64,256]{3,2,1,0:T(8,128)(2,1)S(1)}, u32[]{:S(2)}, u32[]{:S(2)}) collective-permute-start(bf16[2,4,64,256]{3,2,1,0:T(8,128)(2,1)S(1)} %pad_maximum_fusion.1.refs_0_), channel_id=1, source_target_pairs={{0,4},{1,5},{2,6},{3,7},{4,0},{5,1},{6,2},{7,3},{8,12},{9,13},{10,... | collective-permute-start | bytes 786440 | tf_op jit(solution)/shard_map/ppermute | solution.py:16
  11.0 49.1 %collective-permute-start.1 = (bf16[2,4,64,256]{3,2,1,0:T(8,128)(2,1)S(1)}, bf16[2,4,64,256]{3,2,1,0:T(8,128)(2,1)}, u32[]{:S(2)}, u32[]{:S(2)}) collective-permute-start(bf16[2,4,64,256]{3,2,1,0:T(8,128)(2,1)S(1)} %pad_maximum_fusion.1.refs_0_), channel_id=1, source_target_pairs={{0,2},{1,3},{2,0},{3,1},{4,6},{5,7},{6,4},{7,5},{8,10},{9,11},{10,... | collective-permute-start | bytes 786440 | tf_op jit(solution)/shard_map/ppermute | solution.py:16
  11.7 38.4 %collective-permute-start.13 = (bf16[64,128]{1,0:T(8,128)(2,1)S(1)}, bf16[64,128]{1,0:T(8,128)(2,1)S(1)}, u32[]{:S(2)}, u32[]{:S(2)}) collective-permute-start(bf16[64,128]{1,0:T(8,128)(2,1)S(1)} %get-tuple-element.65), channel_id=1, source_target_pairs={{0,7},{1,6},{2,5},{3,4},{4,3},{5,2},{6,1},{7,0},{8,15},{9,14},{10,... | collective-permute-start | bytes 49160 | tf_op jit(solution)/shard_map/ppermute | solution.py:16
  15.3 13.0 %collective-permute-start.8 = (bf16[64,128]{1,0:T(8,128)(2,1)S(1)}, bf16[64,128]{1,0:T(8,128)(2,1)S(1)}, u32[]{:S(2)}, u32[]{:S(2)}) collective-permute-start(bf16[64,128]{1,0:T(8,128)(2,1)S(1)} %get-tuple-element.70), channel_id=1, source_target_pairs={{0,2},{1,3},{2,0},{3,1},{4,6},{5,7},{6,4},{7,5},{8,10},{9,11},{10,... | collective-permute-start | bytes 49160 | tf_op jit(solution)/shard_map/ppermute | solution.py:16
  28.3 5.4 %collective-permute-start.9 = (bf16[64,128]{1,0:T(8,128)(2,1)S(1)}, bf16[64,128]{1,0:T(8,128)(2,1)S(1)}, u32[]{:S(2)}, u32[]{:S(2)}) collective-permute-start(bf16[64,128]{1,0:T(8,128)(2,1)S(1)} %get-tuple-element.69), channel_id=1, source_target_pairs={{0,3},{1,2},{2,1},{3,0},{4,7},{5,6},{6,5},{7,4},{8,11},{9,10},{10,... | collective-permute-start | bytes 49160 | tf_op jit(solution)/shard_map/ppermute | solution.py:16
  33.7 4.6 %collective-permute-start.10 = (bf16[64,128]{1,0:T(8,128)(2,1)S(1)}, bf16[64,128]{1,0:T(8,128)(2,1)S(1)}, u32[]{:S(2)}, u32[]{:S(2)}) collective-permute-start(bf16[64,128]{1,0:T(8,128)(2,1)S(1)} %get-tuple-element.68), channel_id=1, source_target_pairs={{0,4},{1,5},{2,6},{3,7},{4,0},{5,1},{6,2},{7,3},{8,12},{9,13},{10,... | collective-permute-start | bytes 49160 | tf_op jit(solution)/shard_map/ppermute | solution.py:16
  38.3 5.7 %collective-permute-start.11 = (bf16[64,128]{1,0:T(8,128)(2,1)S(1)}, bf16[64,128]{1,0:T(8,128)(2,1)S(1)}, u32[]{:S(2)}, u32[]{:S(2)}) collective-permute-start(bf16[64,128]{1,0:T(8,128)(2,1)S(1)} %get-tuple-element.67), channel_id=1, source_target_pairs={{0,5},{1,4},{2,7},{3,6},{4,1},{5,0},{6,3},{7,2},{8,13},{9,12},{10,... | collective-permute-start | bytes 49160 | tf_op jit(solution)/shard_map/ppermute | solution.py:16
  44.0 5.5 %collective-permute-start.12 = (bf16[64,128]{1,0:T(8,128)(2,1)S(1)}, bf16[64,128]{1,0:T(8,128)(2,1)S(1)}, u32[]{:S(2)}, u32[]{:S(2)}) collective-permute-start(bf16[64,128]{1,0:T(8,128)(2,1)S(1)} %get-tuple-element.66), channel_id=1, source_target_pairs={{0,6},{1,7},{2,4},{3,5},{4,2},{5,3},{6,0},{7,1},{8,14},{9,15},{10,... | collective-permute-start | bytes 49160 | tf_op jit(solution)/shard_map/ppermute | solution.py:16
  50.7 6.0 %collective-permute-start.16 = (bf16[8,64,128]{2,1,0:T(8,128)(2,1)}, bf16[8,64,128]{2,1,0:T(8,128)(2,1)S(1)}, u32[]{:S(2)}, u32[]{:S(2)}) collective-permute-start(bf16[8,64,128]{2,1,0:T(8,128)(2,1)} %constant_dynamic-update-slice_fusion.refs_8_), channel_id=1, source_target_pairs={{0,24},{8,16},{16,8},{24,0},{1,25},{9,17},{17,9},{25,1},{2,26},{10... | collective-permute-start | bytes 393224 | tf_op jit(solution)/shard_map/ppermute | solution.py:16
  50.7 14.5 %collective-permute-start.15 = (bf16[8,64,128]{2,1,0:T(8,128)(2,1)}, bf16[8,64,128]{2,1,0:T(8,128)(2,1)S(1)}, u32[]{:S(2)}, u32[]{:S(2)}) collective-permute-start(bf16[8,64,128]{2,1,0:T(8,128)(2,1)} %constant_dynamic-update-slice_fusion.refs_8_), channel_id=1, source_target_pairs={{0,16},{8,24},{16,0},{24,8},{1,17},{9,25},{17,1},{25,9},{2,18},{10... | collective-permute-start | bytes 393224 | tf_op jit(solution)/shard_map/ppermute | solution.py:16
  56.7 11.6 %collective-permute-start = (bf16[2,4,64,256]{3,2,1,0:T(8,128)(2,1)S(1)}, bf16[2,4,64,256]{3,2,1,0:T(8,128)(2,1)}, u32[]{:S(2)}, u32[]{:S(2)}) collective-permute-start(bf16[2,4,64,256]{3,2,1,0:T(8,128)(2,1)S(1)} %pad_maximum_fusion.1.refs_0_), channel_id=1, source_target_pairs={{0,1},{1,0},{2,3},{3,2},{4,5},{5,4},{6,7},{7,6},{8,9},{9,8},{10,11... | collective-permute-start | bytes 786440 | tf_op jit(solution)/shard_map/ppermute | solution.py:16
  58.1 13.5 %collective-permute-start.6 = (bf16[2,4,64,256]{3,2,1,0:T(8,128)(2,1)S(1)}, bf16[2,4,64,256]{3,2,1,0:T(8,128)(2,1)}, u32[]{:S(2)}, u32[]{:S(2)}) collective-permute-start(bf16[2,4,64,256]{3,2,1,0:T(8,128)(2,1)S(1)} %collective-permute-done.5.refs_6_), channel_id=1, source_target_pairs={{0,1},{1,0},{2,3},{3,2},{4,5},{5,4},{6,7},{7,6},{8,9},{9,8},{10,11... | collective-permute-start | bytes 786440 | tf_op jit(solution)/shard_map/ppermute | solution.py:16
  58.7 18.5 %collective-permute-start.4 = (bf16[2,4,64,256]{3,2,1,0:T(8,128)(2,1)S(1)}, bf16[2,4,64,256]{3,2,1,0:T(8,128)(2,1)}, u32[]{:S(2)}, u32[]{:S(2)}) collective-permute-start(bf16[2,4,64,256]{3,2,1,0:T(8,128)(2,1)S(1)} %collective-permute-done.3.refs_4_), channel_id=1, source_target_pairs={{0,1},{1,0},{2,3},{3,2},{4,5},{5,4},{6,7},{7,6},{8,9},{9,8},{10,11... | collective-permute-start | bytes 786440 | tf_op jit(solution)/shard_map/ppermute | solution.py:16
  60.1 21.9 %collective-permute-start.2 = (bf16[2,4,64,256]{3,2,1,0:T(8,128)(2,1)}, bf16[2,4,64,256]{3,2,1,0:T(8,128)(2,1)}, u32[]{:S(2)}, u32[]{:S(2)}) collective-permute-start(bf16[2,4,64,256]{3,2,1,0:T(8,128)(2,1)} %collective-permute-done.1.refs_2_), channel_id=1, source_target_pairs={{0,1},{1,0},{2,3},{3,2},{4,5},{5,4},{6,7},{7,6},{8,9},{9,8},{10,11... | collective-permute-start | bytes 786440 | tf_op jit(solution)/shard_map/ppermute | solution.py:16
  65.2 3.1 %collective-permute-start.14 = (bf16[8,64,128]{2,1,0:T(8,128)(2,1)}, bf16[8,64,128]{2,1,0:T(8,128)(2,1)}, u32[]{:S(2)}, u32[]{:S(2)}) collective-permute-start(bf16[8,64,128]{2,1,0:T(8,128)(2,1)} %constant_dynamic-update-slice_fusion.refs_8_), channel_id=1, source_target_pairs={{0,8},{8,0},{16,24},{24,16},{1,9},{9,1},{17,25},{25,17},{2,10},{10... | collective-permute-start | bytes 393224 | tf_op jit(solution)/shard_map/ppermute | solution.py:16
  99.4 1.4 collective-permute-start.33
  100.7 4.7 %collective-permute-start.34 = (f32[176,128]{1,0:T(8,128)S(1)}, f32[176,128]{1,0:T(8,128)S(1)}, u32[]{:S(2)}, u32[]{:S(2)}) collective-permute-start(f32[176,128]{1,0:T(8,128)S(1)} %add.78), channel_id=1, source_target_pairs={{0,16},{8,24},{16,0},{24,8},{1,17},{9,25},{17,1},{25,9},{2,18},{10... | collective-permute-start | bytes 270344 | tf_op jit(solution)/shard_map/ppermute | solution.py:16
  105.6 5.5 %collective-permute-start.35 = (bf16[176,128]{1,0:T(8,128)(2,1)S(1)}, bf16[176,128]{1,0:T(8,128)(2,1)S(1)}, u32[]{:S(2)}, u32[]{:S(2)}) collective-permute-start(bf16[176,128]{1,0:T(8,128)(2,1)S(1)} %get-tuple-element.46), channel_id=1, source_target_pairs={{0,1},{1,0},{2,3},{3,2},{4,5},{5,4},{6,7},{7,6},{8,9},{9,8},{10,11... | collective-permute-start | bytes 135176 | tf_op jit(solution)/shard_map/ppermute | solution.py:16
  107.0 16.8 %collective-permute-start.24 = (f32[2,512,128]{2,1,0:T(8,128)S(1)}, f32[2,512,128]{2,1,0:T(8,128)S(1)}, u32[]{:S(2)}, u32[]{:S(2)}) collective-permute-start(f32[2,512,128]{2,1,0:T(8,128)S(1)} %get-tuple-element.36), channel_id=1, source_target_pairs={{0,8},{8,0},{16,24},{24,16},{1,9},{9,1},{17,25},{25,17},{2,10},{10... | collective-permute-start | bytes 1572872 | tf_op jit(solution)/shard_map/ppermute | solution.py:16
  107.0 27.7 %collective-permute-start.40 = (bf16[176,128]{1,0:T(8,128)(2,1)S(1)}, bf16[176,128]{1,0:T(8,128)(2,1)S(1)}, u32[]{:S(2)}, u32[]{:S(2)}) collective-permute-start(bf16[176,128]{1,0:T(8,128)(2,1)S(1)} %get-tuple-element.46), channel_id=1, source_target_pairs={{0,6},{1,7},{2,4},{3,5},{4,2},{5,3},{6,0},{7,1},{8,14},{9,15},{10,... | collective-permute-start | bytes 135176 | tf_op jit(solution)/shard_map/ppermute | solution.py:16
  108.1 16.1 %collective-permute-start.39 = (bf16[176,128]{1,0:T(8,128)(2,1)S(1)}, bf16[176,128]{1,0:T(8,128)(2,1)S(1)}, u32[]{:S(2)}, u32[]{:S(2)}) collective-permute-start(bf16[176,128]{1,0:T(8,128)(2,1)S(1)} %get-tuple-element.46), channel_id=1, source_target_pairs={{0,5},{1,4},{2,7},{3,6},{4,1},{5,0},{6,3},{7,2},{8,13},{9,12},{10,... | collective-permute-start | bytes 135176 | tf_op jit(solution)/shard_map/ppermute | solution.py:16
  108.4 15.8 %collective-permute-start.38 = (bf16[176,128]{1,0:T(8,128)(2,1)S(1)}, bf16[176,128]{1,0:T(8,128)(2,1)S(1)}, u32[]{:S(2)}, u32[]{:S(2)}) collective-permute-start(bf16[176,128]{1,0:T(8,128)(2,1)S(1)} %get-tuple-element.46), channel_id=1, source_target_pairs={{0,4},{1,5},{2,6},{3,7},{4,0},{5,1},{6,2},{7,3},{8,12},{9,13},{10,... | collective-permute-start | bytes 135176 | tf_op jit(solution)/shard_map/ppermute | solution.py:16
  111.0 4.5 %collective-permute-start.36 = (bf16[176,128]{1,0:T(8,128)(2,1)S(1)}, bf16[176,128]{1,0:T(8,128)(2,1)S(1)}, u32[]{:S(2)}, u32[]{:S(2)}) collective-permute-start(bf16[176,128]{1,0:T(8,128)(2,1)S(1)} %get-tuple-element.46), channel_id=1, source_target_pairs={{0,2},{1,3},{2,0},{3,1},{4,6},{5,7},{6,4},{7,5},{8,10},{9,11},{10,... | collective-permute-start | bytes 135176 | tf_op jit(solution)/shard_map/ppermute | solution.py:16
  115.5 4.9 %collective-permute-start.37 = (bf16[176,128]{1,0:T(8,128)(2,1)S(1)}, bf16[176,128]{1,0:T(8,128)(2,1)S(1)}, u32[]{:S(2)}, u32[]{:S(2)}) collective-permute-start(bf16[176,128]{1,0:T(8,128)(2,1)S(1)} %get-tuple-element.46), channel_id=1, source_target_pairs={{0,3},{1,2},{2,1},{3,0},{4,7},{5,6},{6,5},{7,4},{8,11},{9,10},{10,... | collective-permute-start | bytes 135176 | tf_op jit(solution)/shard_map/ppermute | solution.py:16
  120.5 17.7 %collective-permute-start.41 = (bf16[176,128]{1,0:T(8,128)(2,1)S(1)}, bf16[176,128]{1,0:T(8,128)(2,1)S(1)}, u32[]{:S(2)}, u32[]{:S(2)}) collective-permute-start(bf16[176,128]{1,0:T(8,128)(2,1)S(1)} %get-tuple-element.46), channel_id=1, source_target_pairs={{0,7},{1,6},{2,5},{3,4},{4,3},{5,2},{6,1},{7,0},{8,15},{9,14},{10,... | collective-permute-start | bytes 135176 | tf_op jit(solution)/shard_map/ppermute | solution.py:16
  123.8 6.4 %collective-permute-start.25 = (f32[1,512,128]{2,1,0:T(8,128)S(1)}, f32[1,512,128]{2,1,0:T(8,128)S(1)}, u32[]{:S(2)}, u32[]{:S(2)}) collective-permute-start(f32[1,512,128]{2,1,0:T(8,128)S(1)} %slice_bitcast_fusion), channel_id=1, source_target_pairs={{0,16},{8,24},{16,0},{24,8},{1,17},{9,25},{17,1},{25,9},{2,18},{10... | collective-permute-start | bytes 786440 | tf_op jit(solution)/shard_map/ppermute | solution.py:16
  130.4 7.8 %collective-permute-start.32 = (bf16[64,128]{1,0:T(8,128)(2,1)S(1)}, bf16[64,128]{1,0:T(8,128)(2,1)S(1)}, u32[]{:S(2)}, u32[]{:S(2)}) collective-permute-start(bf16[64,128]{1,0:T(8,128)(2,1)S(1)} %get-tuple-element.57), channel_id=1, source_target_pairs={{0,7},{1,6},{2,5},{3,4},{4,3},{5,2},{6,1},{7,0},{8,15},{9,14},{10,... | collective-permute-start | bytes 49160 | tf_op jit(solution)/shard_map/ppermute | solution.py:16
  131.9 8.7 %collective-permute-start.31 = (bf16[64,128]{1,0:T(8,128)(2,1)S(1)}, bf16[64,128]{1,0:T(8,128)(2,1)S(1)}, u32[]{:S(2)}, u32[]{:S(2)}) collective-permute-start(bf16[64,128]{1,0:T(8,128)(2,1)S(1)} %get-tuple-element.58), channel_id=1, source_target_pairs={{0,6},{1,7},{2,4},{3,5},{4,2},{5,3},{6,0},{7,1},{8,14},{9,15},{10,... | collective-permute-start | bytes 49160 | tf_op jit(solution)/shard_map/ppermute | solution.py:16
  134.7 8.3 %collective-permute-start.30 = (bf16[64,128]{1,0:T(8,128)(2,1)S(1)}, bf16[64,128]{1,0:T(8,128)(2,1)S(1)}, u32[]{:S(2)}, u32[]{:S(2)}) collective-permute-start(bf16[64,128]{1,0:T(8,128)(2,1)S(1)} %get-tuple-element.59), channel_id=1, source_target_pairs={{0,5},{1,4},{2,7},{3,6},{4,1},{5,0},{6,3},{7,2},{8,13},{9,12},{10,... | collective-permute-start | bytes 49160 | tf_op jit(solution)/shard_map/ppermute | solution.py:16
  134.8 9.8 %collective-permute-start.29 = (bf16[64,128]{1,0:T(8,128)(2,1)S(1)}, bf16[64,128]{1,0:T(8,128)(2,1)S(1)}, u32[]{:S(2)}, u32[]{:S(2)}) collective-permute-start(bf16[64,128]{1,0:T(8,128)(2,1)S(1)} %get-tuple-element.60), channel_id=1, source_target_pairs={{0,4},{1,5},{2,6},{3,7},{4,0},{5,1},{6,2},{7,3},{8,12},{9,13},{10,... | collective-permute-start | bytes 49160 | tf_op jit(solution)/shard_map/ppermute | solution.py:16
  138.2 7.1 %collective-permute-start.28 = (bf16[64,128]{1,0:T(8,128)(2,1)S(1)}, bf16[64,128]{1,0:T(8,128)(2,1)S(1)}, u32[]{:S(2)}, u32[]{:S(2)}) collective-permute-start(bf16[64,128]{1,0:T(8,128)(2,1)S(1)} %get-tuple-element.61), channel_id=1, source_target_pairs={{0,3},{1,2},{2,1},{3,0},{4,7},{5,6},{6,5},{7,4},{8,11},{9,10},{10,... | collective-permute-start | bytes 49160 | tf_op jit(solution)/shard_map/ppermute | solution.py:16
  138.2 10.2 %collective-permute-start.27 = (bf16[64,128]{1,0:T(8,128)(2,1)S(1)}, bf16[64,128]{1,0:T(8,128)(2,1)S(1)}, u32[]{:S(2)}, u32[]{:S(2)}) collective-permute-start(bf16[64,128]{1,0:T(8,128)(2,1)S(1)} %get-tuple-element.62), channel_id=1, source_target_pairs={{0,2},{1,3},{2,0},{3,1},{4,6},{5,7},{6,4},{7,5},{8,10},{9,11},{10,... | collective-permute-start | bytes 49160 | tf_op jit(solution)/shard_map/ppermute | solution.py:16
  140.6 8.4 %collective-permute-start.26 = (bf16[64,128]{1,0:T(8,128)(2,1)S(1)}, bf16[64,128]{1,0:T(8,128)(2,1)S(1)}, u32[]{:S(2)}, u32[]{:S(2)}) collective-permute-start(bf16[64,128]{1,0:T(8,128)(2,1)S(1)} %get-tuple-element.63), channel_id=1, source_target_pairs={{0,1},{1,0},{2,3},{3,2},{4,5},{5,4},{6,7},{7,6},{8,9},{9,8},{10,11... | collective-permute-start | bytes 49160 | tf_op jit(solution)/shard_map/ppermute | solution.py:16
  143.0 20.5 %collective-permute-start.17 = (bf16[4,64,128]{2,1,0:T(8,128)(2,1)}, bf16[4,64,128]{2,1,0:T(8,128)(2,1)S(1)}, u32[]{:S(2)}, u32[]{:S(2)}) collective-permute-start(bf16[4,64,128]{2,1,0:T(8,128)(2,1)} %get-tuple-element.28), channel_id=1, source_target_pairs={{0,1},{1,0},{2,3},{3,2},{4,5},{5,4},{6,7},{7,6},{8,9},{9,8},{10,11... | collective-permute-start | bytes 196616 | tf_op jit(solution)/shard_map/ppermute | solution.py:16
  144.6 19.1 %collective-permute-start.18 = (bf16[4,64,128]{2,1,0:T(8,128)(2,1)}, bf16[4,64,128]{2,1,0:T(8,128)(2,1)S(1)}, u32[]{:S(2)}, u32[]{:S(2)}) collective-permute-start(bf16[4,64,128]{2,1,0:T(8,128)(2,1)} %get-tuple-element.29), channel_id=1, source_target_pairs={{0,2},{1,3},{2,0},{3,1},{4,6},{5,7},{6,4},{7,5},{8,10},{9,11},{10,... | collective-permute-start | bytes 196616 | tf_op jit(solution)/shard_map/ppermute | solution.py:16
  145.3 21.6 %collective-permute-start.19 = (bf16[4,64,128]{2,1,0:T(8,128)(2,1)}, bf16[4,64,128]{2,1,0:T(8,128)(2,1)S(1)}, u32[]{:S(2)}, u32[]{:S(2)}) collective-permute-start(bf16[4,64,128]{2,1,0:T(8,128)(2,1)} %get-tuple-element.30), channel_id=1, source_target_pairs={{0,3},{1,2},{2,1},{3,0},{4,7},{5,6},{6,5},{7,4},{8,11},{9,10},{10,... | collective-permute-start | bytes 196616 | tf_op jit(solution)/shard_map/ppermute | solution.py:16
  148.4 30.4 %collective-permute-start.42 = (bf16[8,176,128]{2,1,0:T(8,128)(2,1)S(1)}, bf16[8,176,128]{2,1,0:T(8,128)(2,1)}, u32[]{:S(2)}, u32[]{:S(2)}) collective-permute-start(bf16[8,176,128]{2,1,0:T(8,128)(2,1)S(1)} %bitcast_dynamic-update-slice_fusion.mine), channel_id=1, source_target_pairs={{0,8},{8,0},{16,24},{24,16},{1,9},{9,1},{17,25},{25,17},{2,10},{10... | collective-permute-start | bytes 1081352 | tf_op jit(solution)/shard_map/ppermute | solution.py:16
  157.6 1.4 collective-permute-start.43
  159.0 3.6 %collective-permute-start.44 = (f32[128,8]{0,1:T(8,128)S(1)}, f32[128,8]{0,1:T(8,128)S(1)}, u32[]{:S(2)}, u32[]{:S(2)}) collective-permute-start(f32[128,8]{0,1:T(8,128)S(1)} %add.80), channel_id=1, source_target_pairs={{0,16},{8,24},{16,0},{24,8},{1,17},{9,25},{17,1},{25,9},{2,18},{10... | collective-permute-start | bytes 12296 | tf_op jit(solution)/shard_map/ppermute | solution.py:16
  162.6 6.4 %collective-permute-start.45 = (f32[128,8]{0,1:T(8,128)S(1)}, f32[128,8]{0,1:T(8,128)S(1)}, u32[]{:S(2)}, u32[]{:S(2)}) collective-permute-start(f32[128,8]{0,1:T(8,128)S(1)} %add.81), channel_id=1, source_target_pairs={{0,1},{1,0},{2,3},{3,2},{4,5},{5,4},{6,7},{7,6},{8,9},{9,8},{10,11... | collective-permute-start | bytes 12296 | tf_op jit(solution)/shard_map/ppermute | solution.py:16
  163.6 9.7 %collective-permute-start.20 = (bf16[4,64,128]{2,1,0:T(8,128)(2,1)S(1)}, bf16[4,64,128]{2,1,0:T(8,128)(2,1)S(1)}, u32[]{:S(2)}, u32[]{:S(2)}) collective-permute-start(bf16[4,64,128]{2,1,0:T(8,128)(2,1)S(1)} %copy-done.17), channel_id=1, source_target_pairs={{0,4},{1,5},{2,6},{3,7},{4,0},{5,1},{6,2},{7,3},{8,12},{9,13},{10,... | collective-permute-start | bytes 196616 | tf_op jit(solution)/shard_map/ppermute | solution.py:16
  163.7 11.4 %collective-permute-start.21 = (bf16[4,64,128]{2,1,0:T(8,128)(2,1)S(1)}, bf16[4,64,128]{2,1,0:T(8,128)(2,1)S(1)}, u32[]{:S(2)}, u32[]{:S(2)}) collective-permute-start(bf16[4,64,128]{2,1,0:T(8,128)(2,1)S(1)} %copy-done.15), channel_id=1, source_target_pairs={{0,5},{1,4},{2,7},{3,6},{4,1},{5,0},{6,3},{7,2},{8,13},{9,12},{10,... | collective-permute-start | bytes 196616 | tf_op jit(solution)/shard_map/ppermute | solution.py:16
  167.0 8.1 %collective-permute-start.22 = (bf16[4,64,128]{2,1,0:T(8,128)(2,1)S(1)}, bf16[4,64,128]{2,1,0:T(8,128)(2,1)S(1)}, u32[]{:S(2)}, u32[]{:S(2)}) collective-permute-start(bf16[4,64,128]{2,1,0:T(8,128)(2,1)S(1)} %copy-done.13), channel_id=1, source_target_pairs={{0,6},{1,7},{2,4},{3,5},{4,2},{5,3},{6,0},{7,1},{8,14},{9,15},{10,... | collective-permute-start | bytes 196616 | tf_op jit(solution)/shard_map/ppermute | solution.py:16
  168.9 7.1 %collective-permute-start.23 = (bf16[4,64,128]{2,1,0:T(8,128)(2,1)S(1)}, bf16[4,64,128]{2,1,0:T(8,128)(2,1)S(1)}, u32[]{:S(2)}, u32[]{:S(2)}) collective-permute-start(bf16[4,64,128]{2,1,0:T(8,128)(2,1)S(1)} %copy-done.11), channel_id=1, source_target_pairs={{0,7},{1,6},{2,5},{3,4},{4,3},{5,2},{6,1},{7,0},{8,15},{9,14},{10,... | collective-permute-start | bytes 196616 | tf_op jit(solution)/shard_map/ppermute | solution.py:16
  173.3 8.4 %collective-permute-start.46 = (f32[128,8]{0,1:T(8,128)S(1)}, f32[128,8]{0,1:T(8,128)S(1)}, u32[]{:S(2)}, u32[]{:S(2)}) collective-permute-start(f32[128,8]{0,1:T(8,128)S(1)} %add.82), channel_id=1, source_target_pairs={{0,2},{1,3},{2,0},{3,1},{4,6},{5,7},{6,4},{7,5},{8,10},{9,11},{10,... | collective-permute-start | bytes 12296 | tf_op jit(solution)/shard_map/ppermute | solution.py:16
  181.7 4.6 %collective-permute-start.47 = (f32[128,8]{0,1:T(8,128)S(1)}, f32[128,8]{0,1:T(8,128)S(1)}, u32[]{:S(2)}, u32[]{:S(2)}) collective-permute-start(f32[128,8]{0,1:T(8,128)S(1)} %add.83), channel_id=1, source_target_pairs={{0,4},{1,5},{2,6},{3,7},{4,0},{5,1},{6,2},{7,3},{8,12},{9,13},{10,... | collective-permute-start | bytes 12296 | tf_op jit(solution)/shard_map/ppermute | solution.py:16
  (22 other events, 509.8 us)

commit v2 on v0

--- a/solution.py
+++ b/solution.py
@@ -4,7 +4,430 @@
 import jax
 import jax.numpy as jnp
 from jax import lax
+from jax.experimental import pallas as pl
+from jax.experimental.pallas import tpu as pltpu
 from jax.sharding import PartitionSpec as P
+
+F32 = jnp.float32
+BF16 = jnp.bfloat16
+
+
+def exchange(value, axis, size, offset):
+    return lax.ppermute(value, axis, [(i, i ^ offset) for i in range(size)])
+
+
+def dot(a, b, dims=((1,), (0,))):
+    return lax.dot_general(a, b, (dims, ((), ())), preferred_element_type=F32)
+
+
+def norm_rows(block):
+    wide = block.astype(F32)
+    centered = wide - jnp.mean(wide, axis=-1, keepdims=True)
+    inverse = lax.rsqrt(jnp.mean(centered * centered, axis=-1, keepdims=True) + 1e-05)
+    return centered * inverse, inverse
+
+
+def place(r, k, own):
+    return pl.ds(pl.multiple_of(jnp.bitwise_xor(r, k) * own, own), own)
+
+
+def ready_kernel(own_ref, slope_ref, bias_ref, gate_w, out_w, gain_w, out_ref):
+    heads, bias_rows, lanes = bias_ref.shape
+    channels = gain_w.shape[1]
+    width = channels // heads
+    hat, _ = norm_rows(own_ref[...].reshape(-1, channels))
+    normed = (hat * gain_w[...]).astype(BF16)
+    gate = jax.nn.sigmoid(dot(normed, gate_w[...]))
+    dgated = dot(slope_ref[...].reshape(-1, channels), out_w[...], ((1,), (1,)))
+    datt = jnp.transpose((dgated * gate).astype(BF16).astype(F32)).astype(BF16)
+    out_ref[:, :bias_rows, :] = bias_ref[...]
+    for h in range(heads):
+        for n in range(datt.shape[1] // lanes):
+            at = bias_rows + n * width
+            out_ref[h, at : at + width, :] = datt[h * width : (h + 1) * width, n * lanes : (n + 1) * lanes]
+
+
+def attention_kernel(n_res, n_seq, width, span, where, *refs):
+    tokens = refs[:n_res]
+    biases, datts, head_w, gain_w, flow_ref, keep_ref, send_ref = refs[n_res:][:7]
+    normed_s, datt_s, bias_s, dbias_s = refs[-4:]
+    row, last = pl.program_id(0), pl.num_programs(0) - 1
+    r, s = where[0], where[1]
+    own = tokens[0].shape[1]
+    total = own * n_res
+    part = total // n_seq
+    scale = 1.0 / math.sqrt(width)
+
+    @pl.when(row == 0)
+    def _():
+        for m in range(n_seq):
+            bias_s[:, m * part : (m + 1) * part] = biases[m]
+        for k in range(n_res):
+            for n in range(datts.shape[1] // width):
+                block = jnp.transpose(datts[k, n * width : (n + 1) * width, :].astype(F32)).astype(BF16)
+                for m in range(block.shape[0] // own):
+                    at = n * (block.shape[0] // own) + m
+                    datt_s[at, k * own : (k + 1) * own, :] = block[m * own : (m + 1) * own]
+        dbias_s[...] = jnp.zeros_like(dbias_s)
+
+    for k in range(n_res):
+        hat, _ = norm_rows(tokens[k][0])
+        normed_s[place(r, k, own), :] = (hat * gain_w[...]).astype(BF16)
+
+    normed = normed_s[...]
+    weights = head_w[0]
+    wq, wk, wv = (weights[n * width : (n + 1) * width] for n in range(3))
+    rows = ((1,), (1,))
+    q = dot(normed, wq, rows).astype(BF16)
+    k_ = dot(normed, wk, rows).astype(BF16)
+    v = dot(normed, wv, rows).astype(BF16)
+    datt = datt_s[row]
+    q_t, k_t, v_t, datt_t = (jnp.transpose(x) for x in (q, k_, v, datt))
+
+    gk_t = jnp.zeros((width, total), F32)
+    gv_t = jnp.zeros((width, total), F32)
+    gqs, atts = [], []
+    for c in range(total // span):
+        lo, hi = c * span, (c + 1) * span
+        scores = dot(q[lo:hi], k_t) * scale + bias_s[lo:hi, :].astype(F32)
+        top = jnp.max(scores, axis=-1, keepdims=True)
+        e = jnp.exp(scores - top)
+        soft = e * (1.0 / jnp.sum(e, axis=-1, keepdims=True))
+        half = soft.astype(BF16)
+        atts.append(dot(half, v))
+        gv_t += dot(datt_t[:, lo:hi], half)
+        dsoft = dot(datt[lo:hi], v_t)
+        inner = jnp.sum(soft * dsoft, axis=-1, keepdims=True)
+        dscores = soft * (dsoft - inner)
+        dbias_s[lo:hi, :] += dscores
+        dhalf = dscores.astype(BF16)
+        gqs.append(dot(dhalf, k_) * scale)
+        gk_t += dot(q_t[:, lo:hi], dhalf)
+    flow_ref[0, :width, :] = jnp.transpose(jnp.concatenate(gqs, axis=0))
+    flow_ref[0, width : 2 * width, :] = gk_t * scale
+    flow_ref[0, 2 * width : 3 * width, :] = gv_t
+    flow_ref[0, 3 * width :, :] = jnp.transpose(jnp.concatenate(atts, axis=0))
+
+    @pl.when(row == last)
+    def _():
+        for m in range(n_seq):
+            lane = pl.multiple_of(jnp.bitwise_xor(s, m) * part, part)
+            at = m // 2 * total
+            (send_ref if m % 2 else keep_ref)[at : at + total, :] = dbias_s[:, pl.ds(lane, part)]
+
+
+def gradient_kernel(n_res, width, where, *refs):
+    tokens, slopes = refs[:n_res], refs[n_res : n_res + n_res // 2]
+    refs = refs[n_res + n_res // 2 :]
+    flow_ref, head_w, out_w, gain_w, pair_keep, pair_send, grad_ref, keep_ref, send_ref = refs[:9]
+    hat_s, normed_s, slope_s, sums_s = refs[-4:]
+    row, last = pl.program_id(0), pl.num_programs(0) - 1
+    r, s = where[0], where[1]
+    own, channels = tokens[0].shape[1:]
+
+    @pl.when(row == 0)
+    def _():
+        sums_s[...] = jnp.zeros_like(sums_s)
+
+    for k in range(n_res):
+        hat, _ = norm_rows(tokens[k][0])
+        hat_s[place(r, k, own), :] = hat
+        normed_s[place(r, k, own), :] = (hat * gain_w[...]).astype(BF16)
+        slope_s[place(r, k, own), :] = slopes[k // 2][k % 2, 0]
+    normed = normed_s[...]
+    slope = slope_s[...]
+    weights = head_w[0]
+    rows = ((1,), (1,))
+    gate = jax.nn.sigmoid(dot(weights[3 * width :], normed, rows))
+    dgated = dot(out_w[0], slope, rows)
+    att = flow_ref[0, 3 * width :, :]
+    gated = (gate * att).astype(BF16)
+    dgate = dgated * att * gate * (1.0 - gate)
+    grad_t = jnp.concatenate([flow_ref[0, : 3 * width, :], dgate], axis=0)
+    high_t = grad_t.astype(BF16)
+    at = lax.broadcasted_iota(jnp.int32, grad_t.shape, 0)
+    wide = (at >= width) & (at < 3 * width)
+    low_t = jnp.where(wide, grad_t - high_t.astype(F32), 0.0).astype(BF16)
+    high = jnp.transpose(grad_t).astype(BF16)
+    low = jnp.transpose(low_t.astype(F32)).astype(BF16)
+    sums_s[: 4 * width, :] += dot(high_t, normed) + dot(low_t, normed)
+    sums_s[4 * width : 5 * width, :] += dot(gated, slope)
+    grad_normed = dot(high, weights) + dot(low, weights)
+    sums_s[5 * width : 5 * width + 1, :] += jnp.sum(grad_normed * hat_s[...], axis=0, keepdims=True)
+    for k in range(n_res):
+        grad_ref[k, 0] = high[k * own : (k + 1) * own]
+
+    @pl.when(row == last)
+    def _():
+        side = channels // 2
+        core = jnp.bitwise_and(s, 1)
+        at = pair_keep.shape[0]
+        keep_ref[:at, :] = pair_keep[...]
+        send_ref[:at, :] = pair_send[...]
+        keep_ref[at:, :] = sums_s[:, pl.ds(pl.multiple_of(core * side, side), side)]
+        send_ref[at:, :] = sums_s[:, pl.ds(pl.multiple_of((1 - core) * side, side), side)]
+
+
+def weights_kernel(width, *refs):
+    out = refs[-1]
+    for n, ref in enumerate(refs[:-1]):
+        flipped = jnp.transpose(ref[...].astype(F32)).astype(BF16)
+        for h in range(out.shape[0]):
+            out[h, n * width : (n + 1) * width, :] = flipped[h * width : (h + 1) * width]
+
+
+def back_kernel(n_res, own, gain_at, where, keep, come, *outs):
+    total = n_res * own
+    sums = keep[total:, :] + come[total:, :]
+    half = sums.astype(BF16)
+    rest = (sums - half.astype(F32))[gain_at:].astype(BF16)
+    tail = jnp.concatenate([half[:gain_at], jnp.concatenate([half[gain_at:], rest], axis=0)], axis=0)
+    for k in range(n_res):
+        at = place(where[0], k, own)
+        outs[k][:own, :] = (keep[at, :] + come[at, :]).astype(BF16)
+        outs[k][own:, :] = tail
+
+
+def pair_kernel(n_res, where, *refs):
+    blocks = refs[:n_res]
+    rows_ref, out_ref, grad_ref, sums_ref, wide = refs[n_res:]
+    own = grad_ref.shape[1]
+    for k in range(n_res):
+        h = jnp.bitwise_xor(where[0], k)
+        grad_ref[h] = blocks[k][:own, :]
+        wide[h] = blocks[k][:own, :].astype(F32)
+        sums_ref[h] = blocks[k][own:, :]
+    total = jnp.zeros(out_ref.shape[1:], F32)
+    for i in range(own):
+        total += dot(wide[:, i, :].astype(BF16), rows_ref[i])
+    for n in range(out_ref.shape[0]):
+        out_ref[n] = total
+
+
+def tail_kernel(grads, own_ref, weights, gain_w, out_ref):
+    own = own_ref[0]
+    total = jnp.zeros(own.shape, F32)
+    for h in range(grads.shape[0]):
+        total += dot(grads[h, 0], weights[h])
+    hat, inverse = norm_rows(own)
+    g = total * gain_w[...]
+    mean = jnp.mean(g, axis=-1, keepdims=True)
+    cross = jnp.mean(g * hat, axis=-1, keepdims=True)
+    out_ref[0] = (inverse * (g - mean - hat * cross)).astype(BF16)
+
+
+def sums_kernel(width, where, mine, other, gain_ref, *refs):
+    outs, wide = refs[:-1], refs[-1]
+    heads, _, side = mine.shape
+    core = jnp.bitwise_and(where[1], 1)
+    here = pl.ds(pl.multiple_of(core * side, side), side)
+    there = pl.ds(pl.multiple_of((1 - core) * side, side), side)
+    for ref, lanes in ((mine, here), (other, there)):
+        extra = jnp.zeros((1, side), F32)
+        for h in range(heads):
+            block = ref[h].astype(F32)
+            for n in range(5):
+                wide[n, h * width : (h + 1) * width, lanes] = block[n * width : (n + 1) * width]
+            extra += block[5 * width : 5 * width + 1] + block[5 * width + 8 : 5 * width + 9]
+        gain_ref[:, lanes] = extra
+    for n in range(4):
+        outs[n][...] = jnp.transpose(wide[n])
+    outs[4][...] = wide[4]
+
+
+def whole(shape):
+    return pl.BlockSpec(shape, lambda *_: (0,) * len(shape))
+
+
+def by_head(
+    n_res,
+    n_seq,
+    homolog_embedding,
+    pair_input_rows,
+    incoming_slope,
+    rescale_factor,
+    probe_weights,
+    lookup_weights,
+    content_weights,
+    sigmoid_weights,
+    final_projection,
+    pair_bias_matrix,
+):
+    heads = pair_bias_matrix.shape[1]
+    rows, own, channels = homolog_embedding.shape
+    width = channels // heads
+    total = own * n_res
+    part = total // n_seq
+    r, s = lax.axis_index("res"), lax.axis_index("seq")
+    where = jnp.stack([r, s]).astype(jnp.int32)
+    gain_row = rescale_factor.reshape(1, channels)
+
+    def params(mib=48):
+        return pltpu.CompilerParams(vmem_limit_bytes=mib * 1024 * 1024)
+
+    bias_local = jnp.einsum(
+        "ijc,ch->hij", pair_input_rows, pair_bias_matrix, preferred_element_type=F32
+    ).astype(BF16)
+    flat = rows * own // part * width
+    ready = pl.pallas_call(
+        ready_kernel,
+        out_shape=jax.ShapeDtypeStruct((heads, own + flat, part), BF16),
+        compiler_params=params(),
+        name="ready",
+    )(homolog_embedding, incoming_slope, bias_local, sigmoid_weights, final_projection, gain_row)
+    ready = lax.all_to_all(ready, "res", 0, 0, tiled=True)
+    slope_pair = jnp.stack([incoming_slope, exchange(incoming_slope, "res", n_res, 1)])
+    ready, embedding = lax.optimization_barrier((ready, homolog_embedding))
+    datts = ready[:, own:]
+    tokens = [embedding] + [exchange(embedding, "res", n_res, k) for k in range(1, n_res) if k == 1 or k % 2 == 0]
+    bias_all = lax.all_gather(ready[:, :own].reshape(total, part), "seq", axis=0)
+    bias_all, slope_pair, *tokens = lax.optimization_barrier((bias_all, slope_pair, *tokens))
+    tokens = tokens[:2] + [b for block in tokens[2:] for b in (block, exchange(block, "res", n_res, 1))]
+    slopes = [slope_pair] + [exchange(slope_pair, "res", n_res, k) for k in range(2, n_res, 2)]
+
+    head_weights = pl.pallas_call(
+        functools.partial(weights_kernel, width),
+        out_shape=jax.ShapeDtypeStruct((heads, 4 * width, channels), BF16),
+        compiler_params=params(),
+        name="weights",
+    )(probe_weights, lookup_weights, content_weights, sigmoid_weights)
+    out_weights = final_projection.reshape(heads, width, channels)
+
+    token_spec = pl.BlockSpec((1, own, channels), lambda i, w: (i, 0, 0))
+    flow_spec = pl.BlockSpec((1, 4 * width, total), lambda i, w: (i, 0, 0))
+    weight_spec = pl.BlockSpec((1, 4 * width, channels), lambda i, w: (w[0], 0, 0))
+    out_spec = pl.BlockSpec((1, width, channels), lambda i, w: (w[0], 0, 0))
+    sum_rows = 5 * width + 8
+    side = channels // 2
+    pair_rows = n_seq // 2 * total
+    merged = jax.ShapeDtypeStruct((pair_rows + sum_rows, side), F32)
+    flow, pair_keep, pair_send = pl.pallas_call(
+        functools.partial(attention_kernel, n_res, n_seq, width, min(total, 256)),
+        grid_spec=pltpu.PrefetchScalarGridSpec(
+            num_scalar_prefetch=1,
+            grid=(rows,),
+            in_specs=[token_spec] * n_res
+            + [whole((n_seq, total, part)), whole((n_res, flat, part)), weight_spec, whole((1, channels))],
+            out_specs=[flow_spec] + [whole((pair_rows, part))] * 2,
+            scratch_shapes=[
+                pltpu.VMEM((total, channels), BF16),
+                pltpu.VMEM((rows, total, width), BF16),
+                pltpu.VMEM((total, total), BF16),
+                pltpu.VMEM((total, total), F32),
+            ],
+        ),
+        out_shape=[jax.ShapeDtypeStruct((rows, 4 * width, total), F32)]
+        + [jax.ShapeDtypeStruct((pair_rows, part), F32)] * 2,
+        compiler_params=params(60),
+        name="attention",
+    )(where, *tokens, bias_all, datts, head_weights, gain_row)
+
+    grads, keep, send = pl.pallas_call(
+        functools.partial(gradient_kernel, n_res, width),
+        grid_spec=pltpu.PrefetchScalarGridSpec(
+            num_scalar_prefetch=1,
+            grid=(rows,),
+            in_specs=[token_spec] * n_res
+            + [pl.BlockSpec((2, 1, own, channels), lambda i, w: (0, i, 0, 0))] * (n_res // 2)
+            + [flow_spec, weight_spec, out_spec, whole((1, channels))]
+            + [whole((pair_rows, part))] * 2,
+            out_specs=[pl.BlockSpec((n_res, 1, own, 4 * width), lambda i, w: (0, i, 0, 0))]
+            + [whole(merged.shape)] * 2,
+            scratch_shapes=[
+                pltpu.VMEM((total, channels), F32),
+                pltpu.VMEM((total, channels), BF16),
+                pltpu.VMEM((total, channels), BF16),
+                pltpu.VMEM((sum_rows, channels), F32),
+            ],
+        ),
+        out_shape=[jax.ShapeDtypeStruct((n_res, rows, own, 4 * width), BF16)]
+        + [merged, merged],
+        compiler_params=params(60),
+        name="gradients",
+    )(where, *tokens, *slopes, flow, head_weights, out_weights, gain_row, pair_keep, pair_send)
+
+    grads = lax.all_to_all(grads, "res", 0, 0, tiled=True)
+    step = 1
+    while True:
+        come = exchange(send, "seq", n_seq, step)
+        step *= 2
+        if step == n_seq:
+            break
+        summed = keep + come
+        half = (summed.shape[0] - sum_rows) // 2
+        keep = jnp.concatenate([summed[:half], summed[2 * half :]], axis=0)
+        send = summed[half:]
+    come, grads = lax.optimization_barrier((come, grads))
+    back_rows = own + sum_rows + 8
+    backs = pl.pallas_call(
+        functools.partial(back_kernel, n_res, own, 5 * width),
+        grid_spec=pltpu.PrefetchScalarGridSpec(
+            num_scalar_prefetch=1,
+            grid=(1,),
+            in_specs=[whole(keep.shape)] * 2,
+            out_specs=[whole((back_rows, side))] * n_res,
+        ),
+        out_shape=[jax.ShapeDtypeStruct((back_rows, side), BF16)] * n_res,
+        compiler_params=params(),
+        name="back",
+    )(where, keep, come)
+    backs = [backs[0]] + [exchange(backs[k], "res", n_res, k) for k in range(1, n_res)]
+    part_bias, dbias_own, sums = pl.pallas_call(
+        functools.partial(pair_kernel, n_res),
+        grid_spec=pltpu.PrefetchScalarGridSpec(
+            num_scalar_prefetch=1,
+            grid=(1,),
+            in_specs=[whole((back_rows, side))] * n_res + [whole(pair_input_rows.shape)],
+            out_specs=[whole((n_seq * n_res, heads, pair_input_rows.shape[2])), whole((heads, own, part)), whole((heads, sum_rows + 8, side))],
+            scratch_shapes=[pltpu.VMEM((n_res, own, part), F32)],
+        ),
+        out_shape=[
+            jax.ShapeDtypeStruct((n_seq * n_res, heads, pair_input_rows.shape[2]), F32),
+            jax.ShapeDtypeStruct((heads, own, part), BF16),
+            jax.ShapeDtypeStruct((heads, sum_rows + 8, side), BF16),
+        ],
+        compiler_params=params(),
+        name="pair",
+    )(where, *backs, pair_input_rows)
+    part_bias, own_rows = lax.optimization_barrier((part_bias, homolog_embedding))
+    other = exchange(sums, "seq", n_seq, 1)
+    part_bias = lax.all_to_all(part_bias, ("seq", "res"), 0, 0, tiled=True)
+    pair_input_gradient = jnp.einsum(
+        "hij,ch->ijc", dbias_own, pair_bias_matrix, preferred_element_type=F32
+    ).astype(BF16)
+
+    alignment_rows_gradient = pl.pallas_call(
+        tail_kernel,
+        grid=(rows,),
+        in_specs=[
+            pl.BlockSpec((n_res, 1, own, 4 * width), lambda i: (0, i, 0, 0)),
+            pl.BlockSpec((1, own, channels), lambda i: (i, 0, 0)),
+            whole((heads, 4 * width, channels)),
+            whole((1, channels)),
+        ],
+        out_specs=pl.BlockSpec((1, own, channels), lambda i: (i, 0, 0)),
+        out_shape=jax.ShapeDtypeStruct(homolog_embedding.shape, BF16),
+        compiler_params=params(),
+        name="tail",
+    )(grads, own_rows, head_weights, gain_row)
+
+    square = jax.ShapeDtypeStruct((channels, channels), F32)
+    gain, *weight_sums = pl.pallas_call(
+        functools.partial(sums_kernel, width),
+        grid_spec=pltpu.PrefetchScalarGridSpec(
+            num_scalar_prefetch=1,
+            grid=(1,),
+            in_specs=[whole(sums.shape)] * 2,
+            out_specs=[whole((1, channels))] + [whole((channels, channels))] * 5,
+            scratch_shapes=[pltpu.VMEM((5, channels, channels), F32)],
+        ),
+        out_shape=[jax.ShapeDtypeStruct((1, channels), F32)] + [square] * 5,
+        compiler_params=params(),
+        name="sums",
+    )(where, sums, other)
+    part_bias, gain = lax.optimization_barrier((part_bias, gain))
+    part_bias = part_bias.sum(axis=0)
+    return (alignment_rows_gradient, pair_input_gradient, gain.reshape(channels), *weight_sums, part_bias.T)
 
 
 def layer_norm_rows(alignment_block):
@@ -206,4 +629,11 @@
         P(),
     )
     out_specs = (P("seq", "res", None), P("res", "seq", None), P(), P(), P(), P(), P(), P(), P())
-    return jax.shard_map(body, mesh=mesh, in_specs=in_specs, out_specs=out_specs, check_vma=False)
+    n_res, n_seq = mesh.shape["res"], mesh.shape["seq"]
+
+    def run(*args):
+        if n_res == args[-1].shape[1] and n_res & (n_res - 1) == 0 and n_seq > 1 and n_seq & (n_seq - 1) == 0:
+            return by_head(n_res, n_seq, *args)
+        return body(*args)
+
+    return jax.shard_map(run, mesh=mesh, in_specs=in_specs, out_specs=out_specs, check_vma=False)

time: 381 us -> 121 us (0.32)
  waiting for transfers between devices: 195 us -> 26.7 us
  matrix products: 61.6 us -> 4.47 us
  blocking collectives: 48.6 us -> 7.6 us
  starting transfers between devices: 0.34 us -> 40.6 us
  local copies, waits for them, and re-layouts: 44.9 us -> 6.25 us
  Pallas kernels: 0 us -> 30.4 us
  between operations: 14.1 us -> 1.04 us
  other arithmetic: 14.6 us -> 3.52 us
    psum x1 -> x0, waiting for transfers between devices: 98 us -> none  [body(): lax.psum((part_gain, part_query, part_key, part_value, part_gate, part_ou...]
    reduce_scatter x2 -> x0, waiting for transfers between devices: 67 us -> none  [the longest x1 67 us: body(): lax.psum_scatter(key_term, 'res', scatter_dimension=1, tiled=True)]
    dot_general x37 -> x2, matrix products: 55.2 us -> 4.47 us  [the longest x1 2.24 us: by_head(): jnp.einsum('hij,ch->ijc', dbias_own, pair_bias_matrix, preferred_element_...]
    psum x1 -> x0, blocking collectives: 39.8 us -> none  [body(): lax.psum((part_gain, part_query, part_key, part_value, part_gate, part_ou...]
    pallas_call x0 -> x8, Pallas kernels: none -> 30.4 us  [the longest x1 13.1 us: by_head(): pl.pallas_call(functools.partial(attention_kernel, n_res, n_seq, width, m...]
    all_gather x1 -> x0, waiting for transfers between devices: 30.3 us -> none  [body(): normed_all = lax.all_gather(rescaled_embedding, 'res', axis=1, tiled=True)]
    ppermute x0 -> x21, starting transfers between devices: none -> 27 us  [exchange(): return lax.ppermute(value, axis, [(i, i ^ offset) for i in range(size)])]
    dynamic_slice x32 -> x0, local copies, waits for them, and re-layouts: 15.3 us -> none  [body(): lax.scan(functools.partial(row_backward, bias_full, head_count), dbias_in...]
  transfers between devices with their start and end apart: 4 -> 24, of which waited for: 3 -> 9; matrix products, arithmetic and copies ran while one was open for 9% -> 5% of each run, Pallas kernels for 0% -> 15%
where the time goes in v2:
time: 121 us
  starting transfers between devices  40.6 us (34%)
  Pallas kernels  30.4 us (25%)
  waiting for transfers between devices  26.7 us (22%)
  blocking collectives  7.6 us (6%)
  local copies, waits for them, and re-layouts  6.25 us (5%)
  matrix products  4.47 us (4%)
  other arithmetic  3.52 us (3%)
    ppermute x21, starting transfers between devices, exchange(): return lax.ppermute(value, axis, [(i, i ^ offset) for i in range(size)])  27 us
    ppermute x21, waiting for transfers between devices, exchange(): return lax.ppermute(value, axis, [(i, i ^ offset) for i in range(size)])  14.6 us
    pallas_call x1, Pallas kernels, by_head(): pl.pallas_call(functools.partial(attention_kernel, n_res, n_seq, width, m...  13.1 us
    all_to_all x1, waiting for transfers between devices, by_head(): grads = lax.all_to_all(grads, 'res', 0, 0, tiled=True)  10.4 us
    all_gather x1, blocking collectives, by_head(): lax.all_gather(ready[:, :own].reshape(total, part), 'seq', axis=0)  7.6 us
    pallas_call x1, Pallas kernels, by_head(): pl.pallas_call(functools.partial(gradient_kernel, n_res, width), grid_spe...  7.36 us
    all_to_all x1, starting transfers between devices, by_head(): ready = lax.all_to_all(ready, 'res', 0, 0, tiled=True)  7.28 us
    unnamed x56, local copies, waits for them, and re-layouts  4.77 us
  transfers between devices with their start and end apart: 24, of which 9 were waited for; matrix products, arithmetic and copies ran while one was open for 5% of the time, Pallas kernels for 15%

profile of v2, /device:TPU:0, one launch (start us, length us, event | category | flops | bytes accessed | tf_op | source)
XLA Modules:
  0.0 120.6 jit_solution(13435150862201420488)
XLA Ops:
  0.7 0.6 copy-done
  1.3 2.2 %fusion.2 = bf16[8,64,128]{2,0,1:T(8,128)(2,1)S(1)} fusion(bf16[64,128,128]{2,1,0:T(8,128)(2,1)} %refs_8_.1, bf16[128,8]{0,1:T(8,128)(2,1)S(1)} %copy-done), kind=kOutput, calls=%fused_computation.6 | convolution fusion | flops 16777216 | bytes 2230272 | tf_op jit(solution)/shard_map/ijc,ch->hij/dot_general | solution.py:268
  3.7 1.2 ready.1
  4.9 7.3 %all-to-all-start = ((bf16[8,128,128]{2,1,0:T(8,128)(2,1)}), bf16[8,128,128]{2,1,0:T(8,128)(2,1)S(1)}, u32[]{:S(2)}, u32[]{:S(2)}) async-start(bf16[8,128,128]{2,1,0:T(8,128)(2,1)} %ready.1), calls=%async_computation | async-start | bytes 524288 | tf_op jit(solution)/shard_map/all_to_all | solution.py:278
  12.1 2.0 %collective-permute-start = (bf16[4,64,256]{2,1,0:T(8,128)(2,1)S(1)}, bf16[4,64,256]{2,1,0:T(8,128)(2,1)S(1)}, u32[]{:S(2)}, u32[]{:S(2)}) collective-permute-start(bf16[4,64,256]{2,1,0:T(8,128)(2,1)S(1)} %copy-done.8), channel_id=1, source_target_pairs={{0,1},{1,0},{2,3},{3,2},{4,5},{5,4},{6,7},{7,6},{8,9},{9,8},{10,11... | collective-permute-start | bytes 393224 | tf_op jit(solution)/shard_map/ppermute | solution.py:16
  14.2 5.6 %collective-permute-done = bf16[4,64,256]{2,1,0:T(8,128)(2,1)S(1)} collective-permute-done((bf16[4,64,256]{2,1,0:T(8,128)(2,1)S(1)}, bf16[4,64,256]{2,1,0:T(8,128)(2,1)S(1)}, u32[]{:S(2)}, u32[]{:S(2)}) %collective-permute-start) | collective-permute-done | bytes 131104 | tf_op jit(solution)/shard_map/ppermute | solution.py:16
  19.8 1.3 %all-to-all-done = bf16[8,128,128]{2,1,0:T(8,128)(2,1)S(1)} async-done(((bf16[8,128,128]{2,1,0:T(8,128)(2,1)}), bf16[8,128,128]{2,1,0:T(8,128)(2,1)S(1)}, u32[]{:S(2)}, u32[]{:S(2)}) %all-to-all-start) | async-done | bytes 262176 | tf_op jit(solution)/shard_map/all_to_all | solution.py:278
  21.1 2.4 %collective-permute-start.4 = (bf16[4,64,256]{2,1,0:T(8,128)(2,1)S(1)}, bf16[4,64,256]{2,1,0:T(8,128)(2,1)S(1)}, u32[]{:S(2)}, u32[]{:S(2)}) collective-permute-start(bf16[4,64,256]{2,1,0:T(8,128)(2,1)S(1)} %copy-done.4), channel_id=1, source_target_pairs={{0,6},{1,7},{2,4},{3,5},{4,2},{5,3},{6,0},{7,1},{8,14},{9,15},{10,... | collective-permute-start | bytes 393224 | tf_op jit(solution)/shard_map/ppermute | solution.py:16
  23.6 1.9 %collective-permute-start.2 = (bf16[4,64,256]{2,1,0:T(8,128)(2,1)S(1)}, bf16[4,64,256]{2,1,0:T(8,128)(2,1)S(1)}, u32[]{:S(2)}, u32[]{:S(2)}) collective-permute-start(bf16[4,64,256]{2,1,0:T(8,128)(2,1)S(1)} %copy-done.4), channel_id=1, source_target_pairs={{0,2},{1,3},{2,0},{3,1},{4,6},{5,7},{6,4},{7,5},{8,10},{9,11},{10,... | collective-permute-start | bytes 393224 | tf_op jit(solution)/shard_map/ppermute | solution.py:16
  25.5 1.4 %collective-permute-start.1 = (bf16[4,64,256]{2,1,0:T(8,128)(2,1)S(1)}, bf16[4,64,256]{2,1,0:T(8,128)(2,1)S(1)}, u32[]{:S(2)}, u32[]{:S(2)}) collective-permute-start(bf16[4,64,256]{2,1,0:T(8,128)(2,1)S(1)} %copy-done.4), channel_id=1, source_target_pairs={{0,1},{1,0},{2,3},{3,2},{4,5},{5,4},{6,7},{7,6},{8,9},{9,8},{10,11... | collective-permute-start | bytes 393224 | tf_op jit(solution)/shard_map/ppermute | solution.py:16
  26.9 0.7 fusion.4
  27.5 7.6 %all_gather.3.refs_8_ = bf16[4,512,128]{2,1,0:T(8,128)(2,1)} all-gather(bf16[1,512,128]{2,1,0:T(8,128)(2,1)S(1)} %bitcast.21), channel_id=1, replica_groups=mesh['seq'=4,'res'=8] {'seq'}, dimensions={0}, use_global_device_ids=true | all-gather | bytes 655360 | tf_op jit(solution)/shard_map/all_gather | solution.py:283
  35.2 0.7 collective-permute-start.5
  35.9 2.4 %collective-permute-start.10 = (bf16[2,4,64,256]{3,2,1,0:T(8,128)(2,1)S(1)}, bf16[2,4,64,256]{3,2,1,0:T(8,128)(2,1)S(1)}, u32[]{:S(2)}, u32[]{:S(2)}) collective-permute-start(bf16[2,4,64,256]{3,2,1,0:T(8,128)(2,1)S(1)} %pad_maximum_fusion.1.refs_8_), channel_id=1, source_target_pairs={{0,6},{1,7},{2,4},{3,5},{4,2},{5,3},{6,0},{7,1},{8,14},{9,15},{10,... | collective-permute-start | bytes 786440 | tf_op jit(solution)/shard_map/ppermute | solution.py:16
  38.3 2.0 %collective-permute-start.8 = (bf16[2,4,64,256]{3,2,1,0:T(8,128)(2,1)S(1)}, bf16[2,4,64,256]{3,2,1,0:T(8,128)(2,1)S(1)}, u32[]{:S(2)}, u32[]{:S(2)}) collective-permute-start(bf16[2,4,64,256]{3,2,1,0:T(8,128)(2,1)S(1)} %pad_maximum_fusion.1.refs_8_), channel_id=1, source_target_pairs={{0,2},{1,3},{2,0},{3,1},{4,6},{5,7},{6,4},{7,5},{8,10},{9,11},{10,... | collective-permute-start | bytes 786440 | tf_op jit(solution)/shard_map/ppermute | solution.py:16
  40.3 1.4 %collective-permute-start.6 = (bf16[4,64,256]{2,1,0:T(8,128)(2,1)S(1)}, bf16[4,64,256]{2,1,0:T(8,128)(2,1)S(1)}, u32[]{:S(2)}, u32[]{:S(2)}) collective-permute-start(bf16[4,64,256]{2,1,0:T(8,128)(2,1)S(1)} %collective-permute-done.3.refs_4_), channel_id=1, source_target_pairs={{0,1},{1,0},{2,3},{3,2},{4,5},{5,4},{6,7},{7,6},{8,9},{9,8},{10,11... | collective-permute-start | bytes 393224 | tf_op jit(solution)/shard_map/ppermute | solution.py:16
  41.7 0.6 collective-permute-start.7
  42.6 0.8 copy-done.2
  43.3 0.7 pad_add_fusion.where
  44.0 2.3 %collective-permute-done.6.refs_5_ = bf16[4,64,256]{2,1,0:T(8,128)(2,1)S(1)} collective-permute-done((bf16[4,64,256]{2,1,0:T(8,128)(2,1)S(1)}, bf16[4,64,256]{2,1,0:T(8,128)(2,1)S(1)}, u32[]{:S(2)}, u32[]{:S(2)}) %collective-permute-start.6) | collective-permute-done | bytes 131104 | tf_op jit(solution)/shard_map/ppermute | solution.py:16
  46.3 1.4 %collective-permute-done.7.refs_7_ = bf16[4,64,256]{2,1,0:T(8,128)(2,1)S(1)} collective-permute-done((bf16[4,64,256]{2,1,0:T(8,128)(2,1)S(1)}, bf16[4,64,256]{2,1,0:T(8,128)(2,1)S(1)}, u32[]{:S(2)}, u32[]{:S(2)}) %collective-permute-start.7) | collective-permute-done | bytes 131104 | tf_op jit(solution)/shard_map/ppermute | solution.py:16
  48.4 13.1 %attention.1 = (f32[4,128,512]{2,1,0:T(8,128)}, f32[1024,128]{1,0:T(8,128)}, f32[1024,128]{1,0:T(8,128)}) custom-call(s32[2]{0:T(128)} %pad_add_fusion.where, bf16[4,64,256]{2,1,0:T(8,128)(2,1)} %own_ref.2, bf16[4,64,256]{2,1,0:T(8,128)(2,1)} %copy-done.21, bf16[4,64,256]{2,1,0:T(8,128)(2,1)} %copy-done.20, bf16[4,64,256]{2,1,0:T(8,128)(2,1)} %copy-done.22, ...), custom_call_target="tpu_custom_call" | custom-call | tf_op jit(solution)/shard_map/attention/pallas_call | solution.py:304
  61.5 0.6 copy-done.25
  62.3 7.4 %gradients.1 = (bf16[8,4,64,128]{3,2,1,0:T(8,128)(2,1)}, f32[1192,128]{1,0:T(8,128)}, f32[1192,128]{1,0:T(8,128)}) custom-call(s32[2]{0:T(128)} %pad_add_fusion.where, bf16[4,64,256]{2,1,0:T(8,128)(2,1)} %own_ref.2, bf16[4,64,256]{2,1,0:T(8,128)(2,1)} %copy-done.21, bf16[4,64,256]{2,1,0:T(8,128)(2,1)} %copy-done.20, bf16[4,64,256]{2,1,0:T(8,128)(2,1)} %copy-done.22, ...), custom_call_target="tpu_custom_call" | custom-call | tf_op jit(solution)/shard_map/gradients/pallas_call | solution.py:325
  69.8 3.7 %all-to-all-start.1 = ((bf16[8,4,64,128]{3,2,1,0:T(8,128)(2,1)}), bf16[8,4,64,128]{3,2,1,0:T(8,128)(2,1)S(1)}, u32[]{:S(2)}, u32[]{:S(2)}) async-start(bf16[8,4,64,128]{3,2,1,0:T(8,128)(2,1)} %get-tuple-element.61), calls=%async_computation.1 | async-start | bytes 1048576 | tf_op jit(solution)/shard_map/all_to_all | solution.py:349
  73.5 0.8 copy-done.17
  74.3 1.5 %add.3 = f32[1192,128]{1,0:T(8,128)S(1)} add(f32[1192,128]{1,0:T(8,128)} %get-tuple-element.59, f32[1192,128]{1,0:T(8,128)} %copy-done.17) | non-fusion elementwise | flops 152576 | bytes 1830912 | tf_op jit(solution)/shard_map/add | solution.py:356
  75.8 0.8 slice.20
  76.5 0.8 collective-permute-start.12
  77.4 0.8 pad_maximum_fusion.keep
  78.2 10.4 %all-to-all-done.1.grads = bf16[8,4,64,128]{3,2,1,0:T(8,128)(2,1)S(1)} async-done(((bf16[8,4,64,128]{3,2,1,0:T(8,128)(2,1)}), bf16[8,4,64,128]{3,2,1,0:T(8,128)(2,1)S(1)}, u32[]{:S(2)}, u32[]{:S(2)}) %all-to-all-start.1) | async-done | bytes 524320 | tf_op jit(solution)/shard_map/all_to_all | solution.py:349
  88.6 1.0 copy-done.6
  89.6 1.6 %back.1 = (bf16[240,128]{1,0:T(8,128)(2,1)S(1)}, bf16[240,128]{1,0:T(8,128)(2,1)S(1)}, bf16[240,128]{1,0:T(8,128)(2,1)S(1)}, bf16[240,128]{1,0:T(8,128)(2,1)S(1)...) custom-call(s32[2]{0:T(128)S(1)} %copy-done.15, ...), custom_call_target="tpu_custom_call" | custom-call | tf_op jit(solution)/shard_map/back/pallas_call | solution.py:362
  91.2 1.5 %collective-permute-start.13 = (bf16[240,128]{1,0:T(8,128)(2,1)S(1)}, bf16[240,128]{1,0:T(8,128)(2,1)S(1)}, u32[]{:S(2)}, u32[]{:S(2)}) collective-permute-start(bf16[240,128]{1,0:T(8,128)(2,1)S(1)} %get-tuple-element.65), channel_id=1, source_target_pairs={{0,1},{1,0},{2,3},{3,2},{4,5},{5,4},{6,7},{7,6},{8,9},{9,8},{10,11... | collective-permute-start | bytes 184328 | tf_op jit(solution)/shard_map/ppermute | solution.py:16
  92.9 1.8 %collective-permute-start.15 = (bf16[240,128]{1,0:T(8,128)(2,1)S(1)}, bf16[240,128]{1,0:T(8,128)(2,1)S(1)}, u32[]{:S(2)}, u32[]{:S(2)}) collective-permute-start(bf16[240,128]{1,0:T(8,128)(2,1)S(1)} %get-tuple-element.67), channel_id=1, source_target_pairs={{0,3},{1,2},{2,1},{3,0},{4,7},{5,6},{6,5},{7,4},{8,11},{9,10},{10,... | collective-permute-start | bytes 184328 | tf_op jit(solution)/shard_map/ppermute | solution.py:16
  94.7 1.1 collective-permute-start.16
  95.9 2.7 %collective-permute-start.17 = (bf16[240,128]{1,0:T(8,128)(2,1)S(1)}, bf16[240,128]{1,0:T(8,128)(2,1)S(1)}, u32[]{:S(2)}, u32[]{:S(2)}) collective-permute-start(bf16[240,128]{1,0:T(8,128)(2,1)S(1)} %get-tuple-element.69), channel_id=1, source_target_pairs={{0,5},{1,4},{2,7},{3,6},{4,1},{5,0},{6,3},{7,2},{8,13},{9,12},{10,... | collective-permute-start | bytes 184328 | tf_op jit(solution)/shard_map/ppermute | solution.py:16
  98.6 2.1 %collective-permute-start.18 = (bf16[240,128]{1,0:T(8,128)(2,1)S(1)}, bf16[240,128]{1,0:T(8,128)(2,1)S(1)}, u32[]{:S(2)}, u32[]{:S(2)}) collective-permute-start(bf16[240,128]{1,0:T(8,128)(2,1)S(1)} %get-tuple-element.70), channel_id=1, source_target_pairs={{0,6},{1,7},{2,4},{3,5},{4,2},{5,3},{6,0},{7,1},{8,14},{9,15},{10,... | collective-permute-start | bytes 184328 | tf_op jit(solution)/shard_map/ppermute | solution.py:16
  100.6 1.8 %collective-permute-start.19 = (bf16[240,128]{1,0:T(8,128)(2,1)S(1)}, bf16[240,128]{1,0:T(8,128)(2,1)S(1)}, u32[]{:S(2)}, u32[]{:S(2)}) collective-permute-start(bf16[240,128]{1,0:T(8,128)(2,1)S(1)} %get-tuple-element.71), channel_id=1, source_target_pairs={{0,7},{1,6},{2,5},{3,4},{4,3},{5,2},{6,1},{7,0},{8,15},{9,14},{10,... | collective-permute-start | bytes 184328 | tf_op jit(solution)/shard_map/ppermute | solution.py:16
  102.4 1.4 %collective-permute-done.16.refs_4_ = bf16[240,128]{1,0:T(8,128)(2,1)S(1)} collective-permute-done((bf16[240,128]{1,0:T(8,128)(2,1)S(1)}, bf16[240,128]{1,0:T(8,128)(2,1)S(1)}, u32[]{:S(2)}, u32[]{:S(2)}) %collective-permute-start.16) | collective-permute-done | bytes 61472 | tf_op jit(solution)/shard_map/ppermute | solution.py:16
  103.8 2.5 %collective-permute-done.17.refs_5_ = bf16[240,128]{1,0:T(8,128)(2,1)S(1)} collective-permute-done((bf16[240,128]{1,0:T(8,128)(2,1)S(1)}, bf16[240,128]{1,0:T(8,128)(2,1)S(1)}, u32[]{:S(2)}, u32[]{:S(2)}) %collective-permute-start.17) | collective-permute-done | bytes 61472 | tf_op jit(solution)/shard_map/ppermute | solution.py:16
  106.2 1.4 %collective-permute-done.19.refs_7_ = bf16[240,128]{1,0:T(8,128)(2,1)S(1)} collective-permute-done((bf16[240,128]{1,0:T(8,128)(2,1)S(1)}, bf16[240,128]{1,0:T(8,128)(2,1)S(1)}, u32[]{:S(2)}, u32[]{:S(2)}) %collective-permute-start.19) | collective-permute-done | bytes 61472 | tf_op jit(solution)/shard_map/ppermute | solution.py:16
  107.6 1.9 %pair.1 = (f32[32,8,128]{2,1,0:T(8,128)}, bf16[8,64,128]{2,1,0:T(8,128)(2,1)S(1)}, bf16[8,176,128]{2,1,0:T(8,128)(2,1)}) custom-call(s32[2]{0:T(128)S(1)} %copy-done.15, bf16[240,128]{1,0:T(8,128)(2,1)S(1)} %get-tuple-element.64.refs_0_, bf16[240,128]{1,0:T(8,128)(2,1)S(1)} %collective-permute-done.13.refs_1_, ...), custom_call_target="tpu_custom_call" | custom-call | tf_op jit(solution)/shard_map/pair/pallas_call | solution.py:375
  109.6 2.6 %all-to-all-start.2 = ((f32[32,8,128]{2,1,0:T(8,128)}), f32[32,8,128]{2,1,0:T(8,128)S(1)}, u32[]{:S(2)}, u32[]{:S(2)}) async-start(f32[32,8,128]{2,1,0:T(8,128)} %get-tuple-element.75), calls=%async_computation.2 | async-start | bytes 262144 | tf_op jit(solution)/shard_map/all_to_all | solution.py:394
  112.2 2.2 %tail.1 = bf16[4,64,256]{2,1,0:T(8,128)(2,1)} custom-call(bf16[8,4,64,128]{3,2,1,0:T(8,128)(2,1)S(1)} %all-to-all-done.1.grads, bf16[4,64,256]{2,1,0:T(8,128)(2,1)S(1)} %copy-done.5, bf16[8,128,256]{2,1,0:T(8,128)(2,1)S(1)} %copy-done.3, f32[1,256]{1,0:T(1,128)S(1)} %bitcast.20), custom_call_target="tpu_custom_call" | custom-call | tf_op jit(solution)/shard_map/tail/pallas_call | solution.py:399
  114.5 2.2 %convolution_convert_fusion = bf16[64,128,128]{2,1,0:T(8,128)(2,1)} fusion(bf16[8,64,128]{2,1,0:T(8,128)(2,1)S(1)} %get-tuple-element.74, bf16[128,8]{0,1:T(8,128)(2,1)S(1)} %copy-done), kind=kOutput, calls=%fused_computation | convolution fusion | flops 17825792 | bytes 2230272 | tf_op jit(solution)/shard_map/hij,ch->ijc/dot_general | solution.py:395
  116.7 2.9 %sums.1 = (f32[1,256]{1,0:T(1,128)}, f32[256,256]{1,0:T(8,128)}, f32[256,256]{1,0:T(8,128)}, f32[256,256]{1,0:T(8,128)}, f32[256,256]{1,0:T(8,128)}, /*index=5*/f32[256,256]{1,0:T(8,128)}) custom-call(s32[2]{0:T(128)S(1)} %copy-done.15, bf16[8,176,128]{2,1,0:T(8,128)(2,1)} %get-tuple-element.76.mine, bf16[8,176,128]{2,1,0:T(8,128)(2,1)S(1)} %collective-permute-done.20.other), custom_call_target="tpu_custom_call" | custom-call | tf_op jit(solution)/shard_map/sums/pallas_call | solution.py:415
  120.0 0.6 reduce_sum.9
  (77 shorter events, 2.0 us)
Async XLA Ops:
  0.7 3.0 %copy-start.8 = (bf16[4,64,256]{2,1,0:T(8,128)(2,1)S(1)}, bf16[4,64,256]{2,1,0:T(8,128)(2,1)}, u32[]{:S(2)}) copy-start(bf16[4,64,256]{2,1,0:T(8,128)(2,1)} %slope_ref.1) | copy-start | bytes 393220
  0.7 3.0 %copy-start.4 = (bf16[4,64,256]{2,1,0:T(8,128)(2,1)S(1)}, bf16[4,64,256]{2,1,0:T(8,128)(2,1)}, u32[]{:S(2)}) copy-start(bf16[4,64,256]{2,1,0:T(8,128)(2,1)} %own_ref.2) | copy-start | bytes 393220
  0.7 3.0 %copy-start.7 = (bf16[256,256]{1,0:T(8,128)(2,1)S(1)}, bf16[256,256]{1,0:T(8,128)(2,1)}, u32[]{:S(2)}) copy-start(bf16[256,256]{1,0:T(8,128)(2,1)} %out_w.1) | copy-start | bytes 393220
  0.7 3.0 %copy-start.9 = (bf16[256,256]{1,0:T(8,128)(2,1)S(1)}, bf16[256,256]{1,0:T(8,128)(2,1)}, u32[]{:S(2)}) copy-start(bf16[256,256]{1,0:T(8,128)(2,1)} %refs_3_.1) | copy-start | bytes 393220
  0.7 3.0 %copy-start.13 = (f32[256]{0:T(256)S(1)}, f32[256]{0:T(256)}, u32[]{:S(2)}) copy-start(f32[256]{0:T(256)} %param.13) | copy-start | bytes 3076
  3.6 38.8 %copy-start.10 = (bf16[256,256]{1,0:T(8,128)(2,1)S(1)}, bf16[256,256]{1,0:T(8,128)(2,1)}, u32[]{:S(2)}) copy-start(bf16[256,256]{1,0:T(8,128)(2,1)} %refs_0_.1) | copy-start | bytes 393220
  3.6 38.8 %copy-start.11 = (bf16[256,256]{1,0:T(8,128)(2,1)S(1)}, bf16[256,256]{1,0:T(8,128)(2,1)}, u32[]{:S(2)}) copy-start(bf16[256,256]{1,0:T(8,128)(2,1)} %refs_1_.1) | copy-start | bytes 393220
  3.6 38.8 %copy-start.12 = (bf16[256,256]{1,0:T(8,128)(2,1)S(1)}, bf16[256,256]{1,0:T(8,128)(2,1)}, u32[]{:S(2)}) copy-start(bf16[256,256]{1,0:T(8,128)(2,1)} %refs_2_.1) | copy-start | bytes 393220
  4.9 16.2 %all-to-all-start = ((bf16[8,128,128]{2,1,0:T(8,128)(2,1)}), bf16[8,128,128]{2,1,0:T(8,128)(2,1)S(1)}, u32[]{:S(2)}, u32[]{:S(2)}) async-start(bf16[8,128,128]{2,1,0:T(8,128)(2,1)} %ready.1), calls=%async_computation | async-start | bytes 524288 | tf_op jit(solution)/shard_map/all_to_all | solution.py:278
  12.1 7.6 %collective-permute-start = (bf16[4,64,256]{2,1,0:T(8,128)(2,1)S(1)}, bf16[4,64,256]{2,1,0:T(8,128)(2,1)S(1)}, u32[]{:S(2)}, u32[]{:S(2)}) collective-permute-start(bf16[4,64,256]{2,1,0:T(8,128)(2,1)S(1)} %copy-done.8), channel_id=1, source_target_pairs={{0,1},{1,0},{2,3},{3,2},{4,5},{5,4},{6,7},{7,6},{8,9},{9,8},{10,11... | collective-permute-start | bytes 393224 | tf_op jit(solution)/shard_map/ppermute | solution.py:16
  19.8 41.6 %copy-start.16 = (bf16[2,4,64,256]{3,2,1,0:T(8,128)(2,1)}, bf16[2,4,64,256]{3,2,1,0:T(8,128)(2,1)S(1)}, u32[]{:S(2)}) copy-start(bf16[2,4,64,256]{3,2,1,0:T(8,128)(2,1)S(1)} %pad_maximum_fusion.1.refs_8_) | copy-start | bytes 786436
  21.1 14.1 %collective-permute-start.4 = (bf16[4,64,256]{2,1,0:T(8,128)(2,1)S(1)}, bf16[4,64,256]{2,1,0:T(8,128)(2,1)S(1)}, u32[]{:S(2)}, u32[]{:S(2)}) collective-permute-start(bf16[4,64,256]{2,1,0:T(8,128)(2,1)S(1)} %copy-done.4), channel_id=1, source_target_pairs={{0,6},{1,7},{2,4},{3,5},{4,2},{5,3},{6,0},{7,1},{8,14},{9,15},{10,... | collective-permute-start | bytes 393224 | tf_op jit(solution)/shard_map/ppermute | solution.py:16
  23.5 11.7 %collective-permute-start.3 = (bf16[4,64,256]{2,1,0:T(8,128)(2,1)S(1)}, bf16[4,64,256]{2,1,0:T(8,128)(2,1)S(1)}, u32[]{:S(2)}, u32[]{:S(2)}) collective-permute-start(bf16[4,64,256]{2,1,0:T(8,128)(2,1)S(1)} %copy-done.4), channel_id=1, source_target_pairs={{0,4},{1,5},{2,6},{3,7},{4,0},{5,1},{6,2},{7,3},{8,12},{9,13},{10,... | collective-permute-start | bytes 393224 | tf_op jit(solution)/shard_map/ppermute | solution.py:16
  23.6 11.6 %collective-permute-start.2 = (bf16[4,64,256]{2,1,0:T(8,128)(2,1)S(1)}, bf16[4,64,256]{2,1,0:T(8,128)(2,1)S(1)}, u32[]{:S(2)}, u32[]{:S(2)}) collective-permute-start(bf16[4,64,256]{2,1,0:T(8,128)(2,1)S(1)} %copy-done.4), channel_id=1, source_target_pairs={{0,2},{1,3},{2,0},{3,1},{4,6},{5,7},{6,4},{7,5},{8,10},{9,11},{10,... | collective-permute-start | bytes 393224 | tf_op jit(solution)/shard_map/ppermute | solution.py:16
  25.5 9.7 %collective-permute-start.1 = (bf16[4,64,256]{2,1,0:T(8,128)(2,1)S(1)}, bf16[4,64,256]{2,1,0:T(8,128)(2,1)S(1)}, u32[]{:S(2)}, u32[]{:S(2)}) collective-permute-start(bf16[4,64,256]{2,1,0:T(8,128)(2,1)S(1)} %copy-done.4), channel_id=1, source_target_pairs={{0,1},{1,0},{2,3},{3,2},{4,5},{5,4},{6,7},{7,6},{8,9},{9,8},{10,11... | collective-permute-start | bytes 393224 | tf_op jit(solution)/shard_map/ppermute | solution.py:16
  35.1 12.6 %copy-start.18 = (bf16[4,64,256]{2,1,0:T(8,128)(2,1)}, bf16[4,64,256]{2,1,0:T(8,128)(2,1)S(1)}, u32[]{:S(2)}) copy-start(bf16[4,64,256]{2,1,0:T(8,128)(2,1)S(1)} %collective-permute-done.4.refs_6_) | copy-start | bytes 393220
  35.2 12.6 %copy-start.19 = (bf16[4,64,256]{2,1,0:T(8,128)(2,1)}, bf16[4,64,256]{2,1,0:T(8,128)(2,1)S(1)}, u32[]{:S(2)}) copy-start(bf16[4,64,256]{2,1,0:T(8,128)(2,1)S(1)} %collective-permute-done.3.refs_4_) | copy-start | bytes 393220
  35.2 12.6 %copy-start.20 = (bf16[4,64,256]{2,1,0:T(8,128)(2,1)}, bf16[4,64,256]{2,1,0:T(8,128)(2,1)S(1)}, u32[]{:S(2)}) copy-start(bf16[4,64,256]{2,1,0:T(8,128)(2,1)S(1)} %collective-permute-done.2.refs_2_) | copy-start | bytes 393220
  35.2 12.5 %copy-start.21 = (bf16[4,64,256]{2,1,0:T(8,128)(2,1)}, bf16[4,64,256]{2,1,0:T(8,128)(2,1)S(1)}, u32[]{:S(2)}) copy-start(bf16[4,64,256]{2,1,0:T(8,128)(2,1)S(1)} %collective-permute-done.1.refs_1_) | copy-start | bytes 393220
  35.2 6.5 %collective-permute-start.5 = (bf16[4,64,256]{2,1,0:T(8,128)(2,1)S(1)}, bf16[4,64,256]{2,1,0:T(8,128)(2,1)S(1)}, u32[]{:S(2)}, u32[]{:S(2)}) collective-permute-start(bf16[4,64,256]{2,1,0:T(8,128)(2,1)S(1)} %collective-permute-done.2.refs_2_), channel_id=1, source_target_pairs={{0,1},{1,0},{2,3},{3,2},{4,5},{5,4},{6,7},{7,6},{8,9},{9,8},{10,11... | collective-permute-start | bytes 393224 | tf_op jit(solution)/shard_map/ppermute | solution.py:16
  35.9 25.5 %collective-permute-start.10 = (bf16[2,4,64,256]{3,2,1,0:T(8,128)(2,1)S(1)}, bf16[2,4,64,256]{3,2,1,0:T(8,128)(2,1)S(1)}, u32[]{:S(2)}, u32[]{:S(2)}) collective-permute-start(bf16[2,4,64,256]{3,2,1,0:T(8,128)(2,1)S(1)} %pad_maximum_fusion.1.refs_8_), channel_id=1, source_target_pairs={{0,6},{1,7},{2,4},{3,5},{4,2},{5,3},{6,0},{7,1},{8,14},{9,15},{10,... | collective-permute-start | bytes 786440 | tf_op jit(solution)/shard_map/ppermute | solution.py:16
  38.3 23.1 %collective-permute-start.9 = (bf16[2,4,64,256]{3,2,1,0:T(8,128)(2,1)S(1)}, bf16[2,4,64,256]{3,2,1,0:T(8,128)(2,1)S(1)}, u32[]{:S(2)}, u32[]{:S(2)}) collective-permute-start(bf16[2,4,64,256]{3,2,1,0:T(8,128)(2,1)S(1)} %pad_maximum_fusion.1.refs_8_), channel_id=1, source_target_pairs={{0,4},{1,5},{2,6},{3,7},{4,0},{5,1},{6,2},{7,3},{8,12},{9,13},{10,... | collective-permute-start | bytes 786440 | tf_op jit(solution)/shard_map/ppermute | solution.py:16
  38.3 23.2 %collective-permute-start.8 = (bf16[2,4,64,256]{3,2,1,0:T(8,128)(2,1)S(1)}, bf16[2,4,64,256]{3,2,1,0:T(8,128)(2,1)S(1)}, u32[]{:S(2)}, u32[]{:S(2)}) collective-permute-start(bf16[2,4,64,256]{3,2,1,0:T(8,128)(2,1)S(1)} %pad_maximum_fusion.1.refs_8_), channel_id=1, source_target_pairs={{0,2},{1,3},{2,0},{3,1},{4,6},{5,7},{6,4},{7,5},{8,10},{9,11},{10,... | collective-permute-start | bytes 786440 | tf_op jit(solution)/shard_map/ppermute | solution.py:16
  40.3 6.0 %collective-permute-start.6 = (bf16[4,64,256]{2,1,0:T(8,128)(2,1)S(1)}, bf16[4,64,256]{2,1,0:T(8,128)(2,1)S(1)}, u32[]{:S(2)}, u32[]{:S(2)}) collective-permute-start(bf16[4,64,256]{2,1,0:T(8,128)(2,1)S(1)} %collective-permute-done.3.refs_4_), channel_id=1, source_target_pairs={{0,1},{1,0},{2,3},{3,2},{4,5},{5,4},{6,7},{7,6},{8,9},{9,8},{10,11... | collective-permute-start | bytes 393224 | tf_op jit(solution)/shard_map/ppermute | solution.py:16
  41.7 6.0 %copy-start.22 = (bf16[4,64,256]{2,1,0:T(8,128)(2,1)}, bf16[4,64,256]{2,1,0:T(8,128)(2,1)S(1)}, u32[]{:S(2)}) copy-start(bf16[4,64,256]{2,1,0:T(8,128)(2,1)S(1)} %collective-permute-done.5.refs_3_) | copy-start | bytes 393220
  41.7 6.0 %collective-permute-start.7 = (bf16[4,64,256]{2,1,0:T(8,128)(2,1)S(1)}, bf16[4,64,256]{2,1,0:T(8,128)(2,1)S(1)}, u32[]{:S(2)}, u32[]{:S(2)}) collective-permute-start(bf16[4,64,256]{2,1,0:T(8,128)(2,1)S(1)} %collective-permute-done.4.refs_6_), channel_id=1, source_target_pairs={{0,1},{1,0},{2,3},{3,2},{4,5},{5,4},{6,7},{7,6},{8,9},{9,8},{10,11... | collective-permute-start | bytes 393224 | tf_op jit(solution)/shard_map/ppermute | solution.py:16
  42.5 0.8 copy-start.2
  46.3 1.4 %copy-start.23 = (bf16[4,64,256]{2,1,0:T(8,128)(2,1)}, bf16[4,64,256]{2,1,0:T(8,128)(2,1)S(1)}, u32[]{:S(2)}) copy-start(bf16[4,64,256]{2,1,0:T(8,128)(2,1)S(1)} %collective-permute-done.6.refs_5_) | copy-start | bytes 393220
  61.5 0.8 copy-start.27
  69.7 3.8 %collective-permute-start.11 = (f32[1192,128]{1,0:T(8,128)}, f32[1192,128]{1,0:T(8,128)S(1)}, u32[]{:S(2)}, u32[]{:S(2)}) collective-permute-start(f32[1192,128]{1,0:T(8,128)} %get-tuple-element.60), channel_id=1, source_target_pairs={{0,8},{8,0},{16,24},{24,16},{1,9},{9,1},{17,25},{25,17},{2,10},{10... | collective-permute-start | bytes 1830920 | tf_op jit(solution)/shard_map/ppermute | solution.py:16
  69.8 18.8 %all-to-all-start.1 = ((bf16[8,4,64,128]{3,2,1,0:T(8,128)(2,1)}), bf16[8,4,64,128]{3,2,1,0:T(8,128)(2,1)S(1)}, u32[]{:S(2)}, u32[]{:S(2)}) async-start(bf16[8,4,64,128]{3,2,1,0:T(8,128)(2,1)} %get-tuple-element.61), calls=%async_computation.1 | async-start | bytes 1048576 | tf_op jit(solution)/shard_map/all_to_all | solution.py:349
  73.5 15.2 %copy-start.15 = (s32[2]{0:T(128)S(1)}, s32[2]{0:T(128)}, u32[]{:S(2)}) copy-start(s32[2]{0:T(128)} %pad_add_fusion.where) | copy-start | bytes 28
  73.5 0.8 copy-start.17
  74.3 33.3 %copy-start.1 = (bf16[64,128,128]{2,1,0:T(8,128)(2,1)S(1)}, bf16[64,128,128]{2,1,0:T(8,128)(2,1)}, u32[]{:S(2)}) copy-start(bf16[64,128,128]{2,1,0:T(8,128)(2,1)} %refs_8_.1) | copy-start | bytes 6291460
  76.5 12.1 %collective-permute-start.12 = (f32[680,128]{1,0:T(8,128)}, f32[680,128]{1,0:T(8,128)}, u32[]{:S(2)}, u32[]{:S(2)}) collective-permute-start(f32[680,128]{1,0:T(8,128)} %slice.20), channel_id=1, source_target_pairs={{0,16},{8,24},{16,0},{24,8},{1,17},{9,25},{17,1},{25,9},{2,18},{10... | collective-permute-start | bytes 1044488 | tf_op jit(solution)/shard_map/ppermute | solution.py:16
  77.4 34.8 %copy-start.3 = (bf16[8,128,256]{2,1,0:T(8,128)(2,1)S(1)}, bf16[8,128,256]{2,1,0:T(8,128)(2,1)}, u32[]{:S(2)}) copy-start(bf16[8,128,256]{2,1,0:T(8,128)(2,1)} %copy-done.2) | copy-start | bytes 1572868
  77.4 34.8 %copy-start.5 = (bf16[4,64,256]{2,1,0:T(8,128)(2,1)S(1)}, bf16[4,64,256]{2,1,0:T(8,128)(2,1)}, u32[]{:S(2)}) copy-start(bf16[4,64,256]{2,1,0:T(8,128)(2,1)} %own_ref.2) | copy-start | bytes 393220
  77.4 34.8 %copy-start.14 = (f32[256]{0:T(256)S(1)}, f32[256]{0:T(256)}, u32[]{:S(2)}) copy-start(f32[256]{0:T(256)} %param.13) | copy-start | bytes 3076
  88.6 1.0 copy-start.6
  91.2 7.4 %collective-permute-start.13 = (bf16[240,128]{1,0:T(8,128)(2,1)S(1)}, bf16[240,128]{1,0:T(8,128)(2,1)S(1)}, u32[]{:S(2)}, u32[]{:S(2)}) collective-permute-start(bf16[240,128]{1,0:T(8,128)(2,1)S(1)} %get-tuple-element.65), channel_id=1, source_target_pairs={{0,1},{1,0},{2,3},{3,2},{4,5},{5,4},{6,7},{7,6},{8,9},{9,8},{10,11... | collective-permute-start | bytes 184328 | tf_op jit(solution)/shard_map/ppermute | solution.py:16
  92.7 7.9 %collective-permute-start.14 = (bf16[240,128]{1,0:T(8,128)(2,1)S(1)}, bf16[240,128]{1,0:T(8,128)(2,1)S(1)}, u32[]{:S(2)}, u32[]{:S(2)}) collective-permute-start(bf16[240,128]{1,0:T(8,128)(2,1)S(1)} %get-tuple-element.66), channel_id=1, source_target_pairs={{0,2},{1,3},{2,0},{3,1},{4,6},{5,7},{6,4},{7,5},{8,10},{9,11},{10,... | collective-permute-start | bytes 184328 | tf_op jit(solution)/shard_map/ppermute | solution.py:16
  92.9 9.4 %collective-permute-start.15 = (bf16[240,128]{1,0:T(8,128)(2,1)S(1)}, bf16[240,128]{1,0:T(8,128)(2,1)S(1)}, u32[]{:S(2)}, u32[]{:S(2)}) collective-permute-start(bf16[240,128]{1,0:T(8,128)(2,1)S(1)} %get-tuple-element.67), channel_id=1, source_target_pairs={{0,3},{1,2},{2,1},{3,0},{4,7},{5,6},{6,5},{7,4},{8,11},{9,10},{10,... | collective-permute-start | bytes 184328 | tf_op jit(solution)/shard_map/ppermute | solution.py:16
  94.7 9.0 %collective-permute-start.16 = (bf16[240,128]{1,0:T(8,128)(2,1)S(1)}, bf16[240,128]{1,0:T(8,128)(2,1)S(1)}, u32[]{:S(2)}, u32[]{:S(2)}) collective-permute-start(bf16[240,128]{1,0:T(8,128)(2,1)S(1)} %get-tuple-element.68), channel_id=1, source_target_pairs={{0,4},{1,5},{2,6},{3,7},{4,0},{5,1},{6,2},{7,3},{8,12},{9,13},{10,... | collective-permute-start | bytes 184328 | tf_op jit(solution)/shard_map/ppermute | solution.py:16
  95.9 10.4 %collective-permute-start.17 = (bf16[240,128]{1,0:T(8,128)(2,1)S(1)}, bf16[240,128]{1,0:T(8,128)(2,1)S(1)}, u32[]{:S(2)}, u32[]{:S(2)}) collective-permute-start(bf16[240,128]{1,0:T(8,128)(2,1)S(1)} %get-tuple-element.69), channel_id=1, source_target_pairs={{0,5},{1,4},{2,7},{3,6},{4,1},{5,0},{6,3},{7,2},{8,13},{9,12},{10,... | collective-permute-start | bytes 184328 | tf_op jit(solution)/shard_map/ppermute | solution.py:16
  98.6 7.7 %collective-permute-start.18 = (bf16[240,128]{1,0:T(8,128)(2,1)S(1)}, bf16[240,128]{1,0:T(8,128)(2,1)S(1)}, u32[]{:S(2)}, u32[]{:S(2)}) collective-permute-start(bf16[240,128]{1,0:T(8,128)(2,1)S(1)} %get-tuple-element.70), channel_id=1, source_target_pairs={{0,6},{1,7},{2,4},{3,5},{4,2},{5,3},{6,0},{7,1},{8,14},{9,15},{10,... | collective-permute-start | bytes 184328 | tf_op jit(solution)/shard_map/ppermute | solution.py:16
  100.6 7.0 %collective-permute-start.19 = (bf16[240,128]{1,0:T(8,128)(2,1)S(1)}, bf16[240,128]{1,0:T(8,128)(2,1)S(1)}, u32[]{:S(2)}, u32[]{:S(2)}) collective-permute-start(bf16[240,128]{1,0:T(8,128)(2,1)S(1)} %get-tuple-element.71), channel_id=1, source_target_pairs={{0,7},{1,6},{2,5},{3,4},{4,3},{5,2},{6,1},{7,0},{8,15},{9,14},{10,... | collective-permute-start | bytes 184328 | tf_op jit(solution)/shard_map/ppermute | solution.py:16
  109.6 7.1 %collective-permute-start.20 = (bf16[8,176,128]{2,1,0:T(8,128)(2,1)}, bf16[8,176,128]{2,1,0:T(8,128)(2,1)S(1)}, u32[]{:S(2)}, u32[]{:S(2)}) collective-permute-start(bf16[8,176,128]{2,1,0:T(8,128)(2,1)} %get-tuple-element.76.mine), channel_id=1, source_target_pairs={{0,8},{8,0},{16,24},{24,16},{1,9},{9,1},{17,25},{25,17},{2,10},{10... | collective-permute-start | bytes 1081352 | tf_op jit(solution)/shard_map/ppermute | solution.py:16
  109.6 10.4 %all-to-all-start.2 = ((f32[32,8,128]{2,1,0:T(8,128)}), f32[32,8,128]{2,1,0:T(8,128)S(1)}, u32[]{:S(2)}, u32[]{:S(2)}) async-start(f32[32,8,128]{2,1,0:T(8,128)} %get-tuple-element.75), calls=%async_computation.2 | async-start | bytes 262144 | tf_op jit(solution)/shard_map/all_to_all | solution.py:394
  (4 other events, 2.8 us)

commit v3 on v0

--- a/solution.py
+++ b/solution.py
@@ -4,7 +4,411 @@
 import jax
 import jax.numpy as jnp
 from jax import lax
+from jax.experimental import pallas as pl
+from jax.experimental.pallas import tpu as pltpu
 from jax.sharding import PartitionSpec as P
+
+F32 = jnp.float32
+BF16 = jnp.bfloat16
+
+
+def exchange(value, axis, size, offset):
+    return lax.ppermute(value, axis, [(i, i ^ offset) for i in range(size)])
+
+
+def dot(a, b, dims=((1,), (0,))):
+    return lax.dot_general(a, b, (dims, ((), ())), preferred_element_type=F32)
+
+
+def norm_rows(block):
+    wide = block.astype(F32)
+    centered = wide - jnp.mean(wide, axis=-1, keepdims=True)
+    inverse = lax.rsqrt(jnp.mean(centered * centered, axis=-1, keepdims=True) + 1e-05)
+    return centered * inverse, inverse
+
+
+def place(r, k, own):
+    return pl.ds(pl.multiple_of(jnp.bitwise_xor(r, k) * own, own), own)
+
+
+def ready_kernel(own_ref, slope_ref, bias_ref, gate_w, out_w, gain_w, out_ref):
+    heads, bias_rows, lanes = bias_ref.shape
+    channels = gain_w.shape[1]
+    width = channels // heads
+    hat, _ = norm_rows(own_ref[...].reshape(-1, channels))
+    normed = (hat * gain_w[...]).astype(BF16)
+    gate = jax.nn.sigmoid(dot(normed, gate_w[...]))
+    dgated = dot(slope_ref[...].reshape(-1, channels), out_w[...], ((1,), (1,)))
+    datt = jnp.transpose((dgated * gate).astype(BF16).astype(F32)).astype(BF16)
+    out_ref[:, :bias_rows, :] = bias_ref[...]
+    for h in range(heads):
+        for n in range(datt.shape[1] // lanes):
+            at = bias_rows + n * width
+            out_ref[h, at : at + width, :] = datt[h * width : (h + 1) * width, n * lanes : (n + 1) * lanes]
+
+
+def pack(values, depth, own, out_ref):
+    group = out_ref.shape[2] // own
+    for b in range(out_ref.shape[0]):
+        for n in range(values.shape[0] // group):
+            block = [values[n * group + m, :depth, b * own : (b + 1) * own] for m in range(group)]
+            out_ref[b, n * depth : (n + 1) * depth, :] = jnp.concatenate(block, axis=1).astype(BF16)
+
+
+def attention_kernel(n_res, n_seq, width, span, where, *refs):
+    tokens = refs[:2]
+    biases, datts, head_w, gain_w, flow_ref, packed_ref, keep_ref, send_ref = refs[2:10]
+    normed_s, datt_s, bias_s, dbias_s = refs[-4:]
+    _, msa_rows, own, _ = tokens[0].shape
+    r, s = where[0], where[1]
+    total = own * n_res
+    part = total // n_seq
+    scale = 1.0 / math.sqrt(width)
+
+    for m in range(n_seq):
+        bias_s[:, m * part : (m + 1) * part] = biases[m]
+    for k in range(n_res):
+        for n in range(datts.shape[1] // width):
+            block = jnp.transpose(datts[k, n * width : (n + 1) * width, :].astype(F32)).astype(BF16)
+            for m in range(block.shape[0] // own):
+                at = n * (block.shape[0] // own) + m
+                datt_s[at, k * own : (k + 1) * own, :] = block[m * own : (m + 1) * own]
+    dbias_s[...] = jnp.zeros_like(dbias_s)
+
+    @pl.loop(0, msa_rows)
+    def _(row):
+        for k in range(n_res):
+            hat, _ = norm_rows(tokens[k % 2][k // 2, row])
+            normed_s[place(r & 1, k, own), :] = (hat * gain_w[...]).astype(BF16)
+
+        normed = normed_s[...]
+        weights = head_w[r]
+        wq, wk, wv = (weights[n * width : (n + 1) * width] for n in range(3))
+        rows = ((1,), (1,))
+        q = dot(normed, wq, rows).astype(BF16)
+        k_ = dot(normed, wk, rows).astype(BF16)
+        v = dot(normed, wv, rows).astype(BF16)
+        datt = datt_s[row]
+        q_t, k_t, v_t, datt_t = (jnp.transpose(x) for x in (q, k_, v, datt))
+
+        gk_t = jnp.zeros((width, total), F32)
+        gv_t = jnp.zeros((width, total), F32)
+        gqs, atts = [], []
+        for c in range(total // span):
+            lo, hi = c * span, (c + 1) * span
+            scores = dot(q[lo:hi], k_t) * scale + bias_s[lo:hi, :].astype(F32)
+            top = jnp.max(scores, axis=-1, keepdims=True)
+            e = jnp.exp(scores - top)
+            soft = e * (1.0 / jnp.sum(e, axis=-1, keepdims=True))
+            half = soft.astype(BF16)
+            atts.append(dot(half, v))
+            gv_t += dot(datt_t[:, lo:hi], half)
+            dsoft = dot(datt[lo:hi], v_t)
+            inner = jnp.sum(soft * dsoft, axis=-1, keepdims=True)
+            dscores = soft * (dsoft - inner)
+            dbias_s[lo:hi, :] += dscores
+            dhalf = dscores.astype(BF16)
+            gqs.append(dot(dhalf, k_) * scale)
+            gk_t += dot(q_t[:, lo:hi], dhalf)
+        flow_ref[row, :width, :] = jnp.transpose(jnp.concatenate(gqs, axis=0))
+        flow_ref[row, width : 2 * width, :] = gk_t * scale
+        flow_ref[row, 2 * width : 3 * width, :] = gv_t
+        flow_ref[row, 3 * width :, :] = jnp.transpose(jnp.concatenate(atts, axis=0))
+
+    for m in range(n_seq):
+        lane = pl.multiple_of(jnp.bitwise_xor(s, m) * part, part)
+        at = m // 2 * total
+        (send_ref if m % 2 else keep_ref)[at : at + total, :] = dbias_s[:, pl.ds(lane, part)]
+    pack(flow_ref, 3 * width, own, packed_ref)
+
+
+def gradient_kernel(n_res, width, where, *refs):
+    tokens, slopes = refs[:2], refs[2 : 2 + n_res // 2]
+    refs = refs[2 + n_res // 2 :]
+    flow_ref, head_w, out_w, gain_w, grad_ref, keep_ref, send_ref = refs[:7]
+    hat_s, normed_s, slope_s, gate_s, sums_s = refs[-5:]
+    _, msa_rows, own, channels = tokens[0].shape
+    r, s = where[0], where[1]
+
+    sums_s[...] = jnp.zeros_like(sums_s)
+
+    @pl.loop(0, msa_rows)
+    def _(row):
+        for k in range(n_res):
+            hat, _ = norm_rows(tokens[k % 2][k // 2, row])
+            hat_s[place(r & 1, k, own), :] = hat
+            normed_s[place(r & 1, k, own), :] = (hat * gain_w[...]).astype(BF16)
+            slope_s[place(r, k, own), :] = slopes[k // 2][k % 2, row]
+        normed = normed_s[...]
+        slope = slope_s[...]
+        weights = head_w[r]
+        rows = ((1,), (1,))
+        gate = jax.nn.sigmoid(dot(weights[3 * width :], normed, rows))
+        dgated = dot(out_w[r], slope, rows)
+        att = flow_ref[row, 3 * width :, :]
+        gated = (gate * att).astype(BF16)
+        dgate = dgated * att * gate * (1.0 - gate)
+        grad_t = jnp.concatenate([flow_ref[row, : 3 * width, :], dgate], axis=0)
+        high_t = grad_t.astype(BF16)
+        at = lax.broadcasted_iota(jnp.int32, grad_t.shape, 0)
+        wide = (at >= width) & (at < 3 * width)
+        low_t = jnp.where(wide, grad_t - high_t.astype(F32), 0.0).astype(BF16)
+        high = jnp.transpose(grad_t).astype(BF16)
+        low = jnp.transpose(low_t.astype(F32)).astype(BF16)
+        sums_s[: 4 * width, :] += dot(high_t, normed) + dot(low_t, normed)
+        sums_s[4 * width : 5 * width, :] += dot(gated, slope)
+        grad_normed = dot(high, weights) + dot(low, weights)
+        sums_s[5 * width : 5 * width + 1, :] += jnp.sum(grad_normed * hat_s[...], axis=0, keepdims=True)
+        gate_s[row] = dgate
+
+    side = channels // 2
+    core = jnp.bitwise_and(s, 1)
+    keep_ref[...] = sums_s[:, pl.ds(pl.multiple_of(core * side, side), side)]
+    send_ref[...] = sums_s[:, pl.ds(pl.multiple_of((1 - core) * side, side), side)]
+    pack(gate_s, width, own, grad_ref)
+
+
+def weights_kernel(width, *refs):
+    out = refs[-1]
+    for n, ref in enumerate(refs[:-1]):
+        flipped = jnp.transpose(ref[...].astype(F32)).astype(BF16)
+        for h in range(out.shape[0]):
+            out[h, n * width : (n + 1) * width, :] = flipped[h * width : (h + 1) * width]
+
+
+def back_kernel(gain_at, pair_sum, pair_come, gates, keep, come, out_ref):
+    n_res, first, _ = gates.shape
+    own = pair_sum.shape[0] // n_res
+    sums = keep[...] + come[...]
+    half = sums.astype(BF16)
+    rest = (sums - half.astype(F32))[gain_at:].astype(BF16)
+    tail = jnp.concatenate([half[:gain_at], jnp.concatenate([half[gain_at:], rest], axis=0)], axis=0)
+    for k in range(n_res):
+        at = pl.ds(k * own, own)
+        out_ref[k, :own, :] = (pair_sum[at, :] + pair_come[at, :]).astype(BF16)
+        out_ref[k, own : own + first, :] = gates[k]
+        out_ref[k, own + first :, :] = tail
+
+
+def pair_kernel(grad_ref, rows_ref, out_ref, wide):
+    wide[...] = grad_ref[:, : wide.shape[1], :].astype(F32)
+    total = jnp.zeros(out_ref.shape[1:], F32)
+    for i in range(rows_ref.shape[0]):
+        total += dot(wide[:, i, :].astype(BF16), rows_ref[i])
+    for n in range(out_ref.shape[0]):
+        out_ref[n] = total
+
+
+def tail_kernel(packed, back, own_ref, weights, gain_w, out_ref):
+    heads, depth, channels = weights.shape
+    width = depth // 4
+    msa_rows, own, _ = own_ref.shape
+    group = packed.shape[2] // own
+    count = msa_rows // group
+    first = own
+    for n in range(count):
+        total = jnp.zeros((group * own, channels), F32)
+        for h in range(heads):
+            block = [packed[h, n * 3 * width : (n + 1) * 3 * width], back[h, first + n * width : first + (n + 1) * width]]
+            total += dot(jnp.concatenate(block, axis=0), weights[h], ((0,), (0,)))
+        here = pl.ds(n * group, group)
+        hat, inverse = norm_rows(own_ref[here].reshape(group * own, channels))
+        g = total * gain_w[...]
+        mean = jnp.mean(g, axis=-1, keepdims=True)
+        cross = jnp.mean(g * hat, axis=-1, keepdims=True)
+        out_ref[here] = (inverse * (g - mean - hat * cross)).astype(BF16).reshape(group, own, channels)
+
+
+def sums_kernel(width, where, mine, other, gain_ref, *refs):
+    outs, wide = refs[:-1], refs[-1]
+    heads, _, side = mine.shape
+    core = jnp.bitwise_and(where[1], 1)
+    here = pl.ds(pl.multiple_of(core * side, side), side)
+    there = pl.ds(pl.multiple_of((1 - core) * side, side), side)
+    for ref, lanes in ((mine, here), (other, there)):
+        extra = jnp.zeros((1, side), F32)
+        for h in range(heads):
+            block = ref[h, ref.shape[1] - 5 * width - 16 :, :].astype(F32)
+            for n in range(5):
+                wide[n, h * width : (h + 1) * width, lanes] = block[n * width : (n + 1) * width]
+            extra += block[5 * width : 5 * width + 1] + block[5 * width + 8 : 5 * width + 9]
+        gain_ref[:, lanes] = extra
+    for n in range(4):
+        outs[n][...] = jnp.transpose(wide[n])
+    outs[4][...] = wide[4]
+
+
+def whole(shape):
+    return pl.BlockSpec(shape, lambda *_: (0,) * len(shape))
+
+
+def by_head(
+    n_res,
+    n_seq,
+    homolog_embedding,
+    pair_input_rows,
+    incoming_slope,
+    rescale_factor,
+    probe_weights,
+    lookup_weights,
+    content_weights,
+    sigmoid_weights,
+    final_projection,
+    pair_bias_matrix,
+):
+    heads = pair_bias_matrix.shape[1]
+    rows, own, channels = homolog_embedding.shape
+    width = channels // heads
+    total = own * n_res
+    part = total // n_seq
+    r, s = lax.axis_index("res"), lax.axis_index("seq")
+    where = jnp.stack([r, s]).astype(jnp.int32)
+    gain_row = rescale_factor.reshape(1, channels)
+
+    def params(mib=48):
+        return pltpu.CompilerParams(vmem_limit_bytes=mib * 1024 * 1024)
+
+    bias_local = jnp.einsum(
+        "ijc,ch->hij", pair_input_rows, pair_bias_matrix, preferred_element_type=F32
+    ).astype(BF16)
+    flat = rows * own // part * width
+    ready = pl.pallas_call(
+        ready_kernel,
+        out_shape=jax.ShapeDtypeStruct((heads, own + flat, part), BF16),
+        compiler_params=params(),
+        name="ready",
+    )(homolog_embedding, incoming_slope, bias_local, sigmoid_weights, final_projection, gain_row)
+    ready = lax.all_to_all(ready, "res", 0, 0, tiled=True)
+    lines = [list(range(n, n_res, 2)) for n in range(2)]
+    tokens = lax.all_gather(homolog_embedding, "res", axis=0, axis_index_groups=lines)
+    slope_pair = jnp.stack([incoming_slope, exchange(incoming_slope, "res", n_res, 1)])
+    tokens, slope_pair = lax.optimization_barrier((tokens, slope_pair))
+    tokens = [tokens, exchange(tokens, "res", n_res, 1)]
+    datts = ready[:, own:]
+    bias_all = lax.all_gather(ready[:, :own].reshape(total, part), "seq", axis=0)
+    slopes = [slope_pair] + [exchange(slope_pair, "res", n_res, k) for k in range(2, n_res, 2)]
+
+    head_weights = pl.pallas_call(
+        functools.partial(weights_kernel, width),
+        out_shape=jax.ShapeDtypeStruct((heads, 4 * width, channels), BF16),
+        compiler_params=params(),
+        name="weights",
+    )(probe_weights, lookup_weights, content_weights, sigmoid_weights)
+    out_weights = final_projection.reshape(heads, width, channels)
+
+    token_spec = pl.BlockSpec((1, own, channels), lambda i, w: (i, 0, 0))
+    flow_spec = pl.BlockSpec((1, 4 * width, total), lambda i, w: (i, 0, 0))
+    weight_spec = pl.BlockSpec((1, 4 * width, channels), lambda i, w: (w[0], 0, 0))
+    out_spec = pl.BlockSpec((1, width, channels), lambda i, w: (w[0], 0, 0))
+    in_smem = pl.BlockSpec(memory_space=pltpu.SMEM)
+    in_vmem = pl.BlockSpec(memory_space=pltpu.VMEM)
+    sum_rows = 5 * width + 8
+    side = channels // 2
+    pair_rows = n_seq // 2 * total
+    partial = jax.ShapeDtypeStruct((sum_rows, side), F32)
+    flow, packed, pair_keep, pair_send = pl.pallas_call(
+        functools.partial(attention_kernel, n_res, n_seq, width, total),
+        in_specs=[in_smem] + [in_vmem] * 6,
+        out_specs=[in_vmem] * 4,
+        scratch_shapes=[
+            pltpu.VMEM((total, channels), BF16),
+            pltpu.VMEM((rows, total, width), BF16),
+            pltpu.VMEM((total, total), BF16),
+            pltpu.VMEM((total, total), F32),
+        ],
+        out_shape=[
+            jax.ShapeDtypeStruct((rows, 4 * width, total), F32),
+            jax.ShapeDtypeStruct((n_res, 3 * flat, part), BF16),
+        ]
+        + [jax.ShapeDtypeStruct((pair_rows, part), F32)] * 2,
+        compiler_params=params(60),
+        name="attention",
+    )(where, *tokens, bias_all, datts, head_weights, gain_row)
+
+    pair_send, *slopes = lax.optimization_barrier((pair_send, *slopes))
+    keep, send, step = pair_keep, pair_send, 1
+    while step < n_seq:
+        pair_come = exchange(send, "seq", n_seq, step)
+        step *= 2
+        if step < n_seq:
+            half = keep.shape[0] // 2
+            send = keep[half:] + pair_come[half:]
+            keep = keep[:half] + pair_come[:half]
+            send, flow = lax.optimization_barrier((send, flow))
+    pair_sum = keep
+
+    grads, keep, send = pl.pallas_call(
+        functools.partial(gradient_kernel, n_res, width),
+        in_specs=[in_smem] + [in_vmem] * (n_res // 2 + 6),
+        out_specs=[in_vmem] * 3,
+        scratch_shapes=[
+            pltpu.VMEM((total, channels), F32),
+            pltpu.VMEM((total, channels), BF16),
+            pltpu.VMEM((total, channels), BF16),
+            pltpu.VMEM((rows, width, total), F32),
+            pltpu.VMEM((sum_rows, channels), F32),
+        ],
+        out_shape=[jax.ShapeDtypeStruct((n_res, flat, part), BF16), partial, partial],
+        compiler_params=params(60),
+        name="gradients",
+    )(where, *tokens, *slopes, flow, head_weights, out_weights, gain_row)
+
+    packed = lax.all_to_all(packed, "res", 0, 0, tiled=True)
+    pair_come, grads, send = lax.optimization_barrier((pair_come, grads, send))
+    step = 1
+    while step < n_seq:
+        come = exchange(send, "seq", n_seq, step)
+        step *= 2
+        if step < n_seq:
+            send, packed = lax.optimization_barrier((keep + come, packed))
+            keep = send
+    back_rows = own + flat + sum_rows + 8
+    back = pl.pallas_call(
+        functools.partial(back_kernel, 5 * width),
+        out_shape=jax.ShapeDtypeStruct((n_res, back_rows, part), BF16),
+        compiler_params=params(),
+        name="back",
+    )(pair_sum, pair_come, grads, keep, come)
+    back = lax.all_to_all(back, "res", 0, 0, tiled=True)
+    part_bias = pl.pallas_call(
+        pair_kernel,
+        out_shape=jax.ShapeDtypeStruct((n_seq * n_res, heads, pair_input_rows.shape[2]), F32),
+        scratch_shapes=[pltpu.VMEM((n_res, own, part), F32)],
+        compiler_params=params(),
+        name="pair",
+    )(back, pair_input_rows)
+
+    part_bias, own_rows = lax.optimization_barrier((part_bias, homolog_embedding))
+    other = exchange(back, "seq", n_seq, 1)
+    part_bias = lax.all_to_all(part_bias, ("seq", "res"), 0, 0, tiled=True)
+    pair_input_gradient = jnp.einsum(
+        "hij,ch->ijc", back[:, :own], pair_bias_matrix, preferred_element_type=F32
+    ).astype(BF16)
+
+    alignment_rows_gradient = pl.pallas_call(
+        tail_kernel,
+        out_shape=jax.ShapeDtypeStruct(homolog_embedding.shape, BF16),
+        compiler_params=params(),
+        name="tail",
+    )(packed, back, own_rows, head_weights, gain_row)
+
+    square = jax.ShapeDtypeStruct((channels, channels), F32)
+    gain, *weight_sums = pl.pallas_call(
+        functools.partial(sums_kernel, width),
+        grid_spec=pltpu.PrefetchScalarGridSpec(
+            num_scalar_prefetch=1,
+            grid=(1,),
+            in_specs=[whole(back.shape)] * 2,
+            out_specs=[whole((1, channels))] + [whole((channels, channels))] * 5,
+            scratch_shapes=[pltpu.VMEM((5, channels, channels), F32)],
+        ),
+        out_shape=[jax.ShapeDtypeStruct((1, channels), F32)] + [square] * 5,
+        compiler_params=params(),
+        name="sums",
+    )(where, back, other)
+    part_bias, gain = lax.optimization_barrier((part_bias, gain))
+    part_bias = part_bias.sum(axis=0)
+    return (alignment_rows_gradient, pair_input_gradient, gain.reshape(channels), *weight_sums, part_bias.T)
 
 
 def layer_norm_rows(alignment_block):
@@ -206,4 +610,11 @@
         P(),
     )
     out_specs = (P("seq", "res", None), P("res", "seq", None), P(), P(), P(), P(), P(), P(), P())
-    return jax.shard_map(body, mesh=mesh, in_specs=in_specs, out_specs=out_specs, check_vma=False)
+    n_res, n_seq = mesh.shape["res"], mesh.shape["seq"]
+
+    def run(*args):
+        if n_res == args[-1].shape[1] and n_res & (n_res - 1) == 0 and n_seq > 1 and n_seq & (n_seq - 1) == 0:
+            return by_head(n_res, n_seq, *args)
+        return body(*args)
+
+    return jax.shard_map(run, mesh=mesh, in_specs=in_specs, out_specs=out_specs, check_vma=False)

time: 381 us -> 117 us (0.31)
  waiting for transfers between devices: 195 us -> 6.73 us
  matrix products: 61.6 us -> 4.5 us
  local copies, waits for them, and re-layouts: 44.9 us -> 5.62 us
  Pallas kernels: 0 us -> 24.6 us
  starting transfers between devices: 0.34 us -> 24.6 us
  between operations: 14.1 us -> 0.92 us
  other arithmetic: 14.6 us -> 3.3 us
    psum x1 -> x0, waiting for transfers between devices: 98 us -> none  [body(): lax.psum((part_gain, part_query, part_key, part_value, part_gate, part_ou...]
    reduce_scatter x2 -> x0, waiting for transfers between devices: 67 us -> none  [the longest x1 67 us: body(): lax.psum_scatter(key_term, 'res', scatter_dimension=1, tiled=True)]
    dot_general x37 -> x2, matrix products: 55.2 us -> 4.5 us  [the longest x1 2.26 us: by_head(): jnp.einsum('ijc,ch->hij', pair_input_rows, pair_bias_matrix, preferred_el...]
    psum x1 -> x0, blocking collectives: 39.8 us -> none  [body(): lax.psum((part_gain, part_query, part_key, part_value, part_gate, part_ou...]
    all_gather x1 -> x0, waiting for transfers between devices: 30.3 us -> none  [body(): normed_all = lax.all_gather(rescaled_embedding, 'res', axis=1, tiled=True)]
    pallas_call x0 -> x8, Pallas kernels: none -> 24.6 us  [the longest x1 11.3 us: by_head(): pl.pallas_call(functools.partial(attention_kernel, n_res, n_seq, width, t...]
    all_to_all x0 -> x1, blocking collectives: none -> 22.1 us  [by_head(): back = lax.all_to_all(back, 'res', 0, 0, tiled=True)]
    dynamic_slice x32 -> x0, local copies, waits for them, and re-layouts: 15.3 us -> none  [body(): lax.scan(functools.partial(row_backward, bias_full, head_count), dbias_in...]
  transfers between devices with their start and end apart: 4 -> 13, of which waited for: 3 -> 5; matrix products, arithmetic and copies ran while one was open for 9% -> 5% of each run, Pallas kernels for 0% -> 20%
where the time goes in v3:
time: 117 us; the launch traced here: 116 us
  blocking collectives  45.8 us (39%)
  Pallas kernels  24.6 us (21%)
  starting transfers between devices  24.6 us (21%)
  waiting for transfers between devices  6.73 us (6%)
  local copies, waits for them, and re-layouts  5.62 us (5%)
  matrix products  4.5 us (4%)
  other arithmetic  3.3 us (3%)
    all_to_all x1, blocking collectives, by_head(): back = lax.all_to_all(back, 'res', 0, 0, tiled=True)  22.1 us
    all_gather x1, blocking collectives, by_head(): lax.all_gather(homolog_embedding, 'res', axis=0, axis_index_groups=lines)  16.1 us
    pallas_call x1, Pallas kernels, by_head(): pl.pallas_call(functools.partial(attention_kernel, n_res, n_seq, width, t...  11.3 us
    ppermute x10, starting transfers between devices, exchange(): return lax.ppermute(value, axis, [(i, i ^ offset) for i in range(size)])  10.3 us
    all_gather x1, blocking collectives, by_head(): lax.all_gather(ready[:, :own].reshape(total, part), 'seq', axis=0)  7.6 us
    all_to_all x1, starting transfers between devices, by_head(): ready = lax.all_to_all(ready, 'res', 0, 0, tiled=True)  7.28 us
    ppermute x10, waiting for transfers between devices, exchange(): return lax.ppermute(value, axis, [(i, i ^ offset) for i in range(size)])  6.28 us
    pallas_call x1, Pallas kernels, by_head(): pl.pallas_call(functools.partial(gradient_kernel, n_res, width), in_specs...  6.14 us
  transfers between devices with their start and end apart: 13, of which 5 were waited for; matrix products, arithmetic and copies ran while one was open for 5% of the time, Pallas kernels for 20%

profile of v3, /device:TPU:0, one launch (start us, length us, event | category | flops | bytes accessed | tf_op | source)
XLA Modules:
  0.0 116.1 jit_solution(7769377175731235956)
XLA Ops:
  0.6 0.0 copy-start
  0.7 0.0 copy-start.7
  0.7 0.0 copy-start.14
  0.7 0.6 copy-done
  1.3 2.3 %fusion.2 = bf16[8,64,128]{2,0,1:T(8,128)(2,1)S(1)} fusion(bf16[64,128,128]{2,1,0:T(8,128)(2,1)} %rows_ref.1, bf16[128,8]{0,1:T(8,128)(2,1)S(1)} %copy-done), kind=kOutput, calls=%fused_computation.7 | convolution fusion | flops 16777216 | bytes 2230272 | tf_op jit(solution)/shard_map/ijc,ch->hij/dot_general | solution.py:271
  3.7 1.2 %ready.1 = bf16[8,128,128]{2,1,0:T(8,128)(2,1)} custom-call(bf16[4,64,256]{2,1,0:T(8,128)(2,1)S(1)} %copy-done.6, bf16[4,64,256]{2,1,0:T(8,128)(2,1)S(1)} %copy-done.8, bf16[8,64,128]{2,1,0:T(8,128)(2,1)S(1)} %copy.26.bias_ref, bf16[256,256]{1,0:T(8,128)(2,1)S(1)} %copy-done.9, bf16[256,256]{1,0:T(8,128)(2,1)S(1)} %copy-done.7, f32[1,256]{1,0:T(1,128)S(1)} %bitcast.20), custom_call_target="tpu_custom_call" | custom-call | tf_op jit(solution)/shard_map/ready/pallas_call | solution.py:275
  4.9 7.3 %all-to-all-start = ((bf16[8,128,128]{2,1,0:T(8,128)(2,1)}), bf16[8,128,128]{2,1,0:T(8,128)(2,1)S(1)}, u32[]{:S(2)}, u32[]{:S(2)}) async-start(bf16[8,128,128]{2,1,0:T(8,128)(2,1)} %ready.1), calls=%async_computation | async-start | bytes 524288 | tf_op jit(solution)/shard_map/all_to_all | solution.py:281
  12.2 2.0 %collective-permute-start = (bf16[4,64,256]{2,1,0:T(8,128)(2,1)S(1)}, bf16[4,64,256]{2,1,0:T(8,128)(2,1)S(1)}, u32[]{:S(2)}, u32[]{:S(2)}) collective-permute-start(bf16[4,64,256]{2,1,0:T(8,128)(2,1)S(1)} %copy-done.8), channel_id=1, source_target_pairs={{0,1},{1,0},{2,3},{3,2},{4,5},{5,4},{6,7},{7,6},{8,9},{9,8},{10,11... | collective-permute-start | bytes 393224 | tf_op jit(solution)/shard_map/ppermute | solution.py:16
  14.2 0.2 weights.1.refs_4_.refs_7_
  14.4 0.8 copy-done.2
  15.2 16.1 %all-gather = bf16[16,64,256]{2,1,0:T(8,128)(2,1)S(1)} all-gather(bf16[4,64,256]{2,1,0:T(8,128)(2,1)S(1)} %copy-done.6), channel_id=2, replica_groups={{0,2,4,6},{1,3,5,7},{8,10,12,14},{9,11,13,15},{16,18,20,22},{17,19,21,2..., dimensions={0}, use_global_device_ids=true | all-gather | bytes 655360 | tf_op jit(solution)/shard_map/all_gather | solution.py:283
  31.4 0.0 copy-start.19
  31.4 1.8 %collective-permute-start.1 = (bf16[4,4,64,256]{3,2,1,0:T(8,128)(2,1)S(1)}, bf16[4,4,64,256]{3,2,1,0:T(8,128)(2,1)S(1)}, u32[]{:S(2)}, u32[]{:S(2)}) collective-permute-start(bf16[4,4,64,256]{3,2,1,0:T(8,128)(2,1)S(1)} %bitcast.22), channel_id=1, source_target_pairs={{0,1},{1,0},{2,3},{3,2},{4,5},{5,4},{6,7},{7,6},{8,9},{9,8},{10,11... | collective-permute-start | bytes 1572872 | tf_op jit(solution)/shard_map/ppermute | solution.py:16
  33.2 0.6 pad_add_fusion.where
  33.8 0.5 collective-permute-start.2
  34.2 2.6 %collective-permute-start.3 = (bf16[2,4,64,256]{3,2,1,0:T(8,128)(2,1)S(1)}, bf16[2,4,64,256]{3,2,1,0:T(8,128)(2,1)S(1)}, u32[]{:S(2)}, u32[]{:S(2)}) collective-permute-start(bf16[2,4,64,256]{3,2,1,0:T(8,128)(2,1)S(1)} %pad_maximum_fusion.refs_2_), channel_id=1, source_target_pairs={{0,4},{1,5},{2,6},{3,7},{4,0},{5,1},{6,2},{7,3},{8,12},{9,13},{10,... | collective-permute-start | bytes 786440 | tf_op jit(solution)/shard_map/ppermute | solution.py:16
  36.9 1.3 %collective-permute-start.4 = (bf16[2,4,64,256]{3,2,1,0:T(8,128)(2,1)S(1)}, bf16[2,4,64,256]{3,2,1,0:T(8,128)(2,1)S(1)}, u32[]{:S(2)}, u32[]{:S(2)}) collective-permute-start(bf16[2,4,64,256]{3,2,1,0:T(8,128)(2,1)S(1)} %pad_maximum_fusion.refs_2_), channel_id=1, source_target_pairs={{0,6},{1,7},{2,4},{3,5},{4,2},{5,3},{6,0},{7,1},{8,14},{9,15},{10,... | collective-permute-start | bytes 786440 | tf_op jit(solution)/shard_map/ppermute | solution.py:16
  38.2 0.7 fusion.4
  38.8 7.6 %all_gather.11.refs_2_ = bf16[4,512,128]{2,1,0:T(8,128)(2,1)} all-gather(bf16[1,512,128]{2,1,0:T(8,128)(2,1)S(1)} %bitcast.25), channel_id=1, replica_groups=mesh['seq'=4,'res'=8] {'seq'}, dimensions={0}, use_global_device_ids=true | all-gather | bytes 655360 | tf_op jit(solution)/shard_map/all_gather | solution.py:288
  46.4 0.8 copy-done.18
  47.2 11.3 %attention.1 = (f32[4,128,512]{2,1,0:T(8,128)}, bf16[8,192,128]{2,1,0:T(8,128)(2,1)}, f32[1024,128]{1,0:T(8,128)}, f32[1024,128]{1,0:T(8,128)}) custom-call(s32[2]{0:T(128)} %pad_add_fusion.where, bf16[4,4,64,256]{3,2,1,0:T(8,128)(2,1)} %bitcast.23, bf16[4,4,64,256]{3,2,1,0:T(8,128)(2,1)} %copy-done.18, bf16[4,512,128]{2,1,0:T(8,128)(2,1)} %all_gather.11.refs_2_, ...), custom_call_target="tpu_custom_call" | custom-call | tf_op jit(solution)/shard_map/attention/pallas_call | solution.py:309
  58.6 0.0 copy-start.21
  58.6 0.0 copy-start.22
  58.6 0.4 collective-permute-start.5
  59.0 4.4 %all-to-all-start.1 = ((bf16[8,192,128]{2,1,0:T(8,128)(2,1)}), bf16[8,192,128]{2,1,0:T(8,128)(2,1)S(1)}, u32[]{:S(2)}, u32[]{:S(2)}) async-start(bf16[8,192,128]{2,1,0:T(8,128)(2,1)} %get-tuple-element.56), calls=%async_computation.1 | async-start | bytes 786432 | tf_op jit(solution)/shard_map/all_to_all | solution.py:356
  63.5 1.1 slice_add_fusion
  64.6 0.9 collective-permute-start.6
  65.5 6.1 %gradients.1 = (bf16[8,64,128]{2,1,0:T(8,128)(2,1)}, f32[168,128]{1,0:T(8,128)}, f32[168,128]{1,0:T(8,128)}) custom-call(s32[2]{0:T(128)} %pad_add_fusion.where, bf16[4,4,64,256]{3,2,1,0:T(8,128)(2,1)} %bitcast.24, bf16[4,4,64,256]{3,2,1,0:T(8,128)(2,1)} %copy-done.18, bf16[2,4,64,256]{3,2,1,0:T(8,128)(2,1)} %copy-done.19, ...), custom_call_target="tpu_custom_call" | custom-call | tf_op jit(solution)/shard_map/gradients/pallas_call | solution.py:340
  71.6 1.1 collective-permute-done.6.pair_come
  72.8 1.5 %collective-permute-done.7 = f32[168,128]{1,0:T(8,128)S(1)} collective-permute-done((f32[168,128]{1,0:T(8,128)}, f32[168,128]{1,0:T(8,128)S(1)}, u32[]{:S(2)}, u32[]{:S(2)}) %collective-permute-start.7) | collective-permute-done | bytes 86048 | tf_op jit(solution)/shard_map/ppermute | solution.py:16
  74.2 0.9 add.10.keep
  75.2 0.3 all-to-all-done.1.packed
  75.5 0.7 copy-done.4
  76.2 0.8 collective-permute-start.8
  77.0 3.7 %collective-permute-done.8.come = f32[168,128]{1,0:T(8,128)S(1)} collective-permute-done((f32[168,128]{1,0:T(8,128)S(1)}, f32[168,128]{1,0:T(8,128)S(1)}, u32[]{:S(2)}, u32[]{:S(2)}) %collective-permute-start.8) | collective-permute-done | bytes 86048 | tf_op jit(solution)/shard_map/ppermute | solution.py:16
  80.7 0.9 copy-done.13
  81.6 0.1 back.1
  81.7 0.0 copy-start.15
  81.7 22.1 %all_to_all.20.grad_ref.back.mine = bf16[8,304,128]{2,1,0:T(8,128)(2,1)S(1)} all-to-all(bf16[8,304,128]{2,1,0:T(8,128)(2,1)S(1)} %back.1), channel_id=1, replica_groups=mesh['seq'=4,'res'=8] {'res'}, dimensions={0} | all-to-all | bytes 1245184 | tf_op jit(solution)/shard_map/all_to_all | solution.py:372
  103.8 1.4 %pair.1 = f32[32,8,128]{2,1,0:T(8,128)} custom-call(bf16[8,304,128]{2,1,0:T(8,128)(2,1)S(1)} %all_to_all.20.grad_ref.back.mine, bf16[64,128,128]{2,1,0:T(8,128)(2,1)S(1)} %copy-done.1), custom_call_target="tpu_custom_call" | custom-call | tf_op jit(solution)/shard_map/pair/pallas_call | solution.py:373
  105.1 2.6 %all-to-all-start.3 = ((f32[32,8,128]{2,1,0:T(8,128)}), f32[32,8,128]{2,1,0:T(8,128)S(1)}, u32[]{:S(2)}, u32[]{:S(2)}) async-start(f32[32,8,128]{2,1,0:T(8,128)} %pair.1), calls=%async_computation.3 | async-start | bytes 262144 | tf_op jit(solution)/shard_map/all_to_all | solution.py:383
  107.7 0.0 copy-start.5
  107.8 1.0 copy-done.5
  108.7 1.2 %tail.1 = bf16[4,64,256]{2,1,0:T(8,128)(2,1)} custom-call(bf16[8,192,128]{2,1,0:T(8,128)(2,1)S(1)} %copy-done.5, bf16[8,304,128]{2,1,0:T(8,128)(2,1)S(1)} %all_to_all.20.grad_ref.back.mine, bf16[4,64,256]{2,1,0:T(8,128)(2,1)S(1)} %copy-done.6, bf16[8,128,256]{2,1,0:T(8,128)(2,1)S(1)} %copy-done.3, f32[1,256]{1,0:T(1,128)S(1)} %bitcast.21), custom_call_target="tpu_custom_call" | custom-call | tf_op jit(solution)/shard_map/tail/pallas_call | solution.py:388
  110.0 2.2 %convolution_convert_fusion = bf16[64,128,128]{2,1,0:T(8,128)(2,1)} fusion(bf16[8,64,128]{2,1,0:T(8,128)(2,1)S(1)} %slice.32, bf16[128,8]{0,1:T(8,128)(2,1)S(1)} %copy-done), kind=kOutput, calls=%fused_computation | convolution fusion | flops 17825792 | bytes 2230272 | tf_op jit(solution)/shard_map/hij,ch->ijc/dot_general | solution.py:384
  112.2 3.1 %sums.1 = (f32[1,256]{1,0:T(1,128)}, f32[256,256]{1,0:T(8,128)}, f32[256,256]{1,0:T(8,128)}, f32[256,256]{1,0:T(8,128)}, f32[256,256]{1,0:T(8,128)}, /*index=5*/f32[256,256]{1,0:T(8,128)}) custom-call(s32[2]{0:T(128)S(1)} %copy-done.16, bf16[8,304,128]{2,1,0:T(8,128)(2,1)S(1)} %all_to_all.20.grad_ref.back.mine, bf16[8,304,128]{2,1,0:T(8,128)(2,1)} %collective-permute-done.9.other), custom_call_target="tpu_custom_call" | custom-call | tf_op jit(solution)/shard_map/sums/pallas_call | solution.py:396
  115.3 0.1 all-to-all-done.3
  115.4 0.6 reduce_sum.9
  (45 shorter events, 0.2 us)
Async XLA Ops:
  0.6 0.7 copy-start
  0.7 3.0 %copy-start.6 = (bf16[4,64,256]{2,1,0:T(8,128)(2,1)S(1)}, bf16[4,64,256]{2,1,0:T(8,128)(2,1)}, u32[]{:S(2)}) copy-start(bf16[4,64,256]{2,1,0:T(8,128)(2,1)} %own_ref.2) | copy-start | bytes 393220
  0.7 3.0 %copy-start.8 = (bf16[4,64,256]{2,1,0:T(8,128)(2,1)S(1)}, bf16[4,64,256]{2,1,0:T(8,128)(2,1)}, u32[]{:S(2)}) copy-start(bf16[4,64,256]{2,1,0:T(8,128)(2,1)} %slope_ref.1) | copy-start | bytes 393220
  0.7 3.0 %copy-start.9 = (bf16[256,256]{1,0:T(8,128)(2,1)S(1)}, bf16[256,256]{1,0:T(8,128)(2,1)}, u32[]{:S(2)}) copy-start(bf16[256,256]{1,0:T(8,128)(2,1)} %refs_3_.1) | copy-start | bytes 393220
  0.7 3.0 %copy-start.7 = (bf16[256,256]{1,0:T(8,128)(2,1)S(1)}, bf16[256,256]{1,0:T(8,128)(2,1)}, u32[]{:S(2)}) copy-start(bf16[256,256]{1,0:T(8,128)(2,1)} %out_w.1) | copy-start | bytes 393220
  0.7 3.0 %copy-start.14 = (f32[256]{0:T(256)S(1)}, f32[256]{0:T(256)}, u32[]{:S(2)}) copy-start(f32[256]{0:T(256)} %param.13) | copy-start | bytes 3076
  0.7 13.5 %copy-start.10 = (bf16[256,256]{1,0:T(8,128)(2,1)S(1)}, bf16[256,256]{1,0:T(8,128)(2,1)}, u32[]{:S(2)}) copy-start(bf16[256,256]{1,0:T(8,128)(2,1)} %refs_0_.1) | copy-start | bytes 393220
  0.7 13.5 %copy-start.11 = (bf16[256,256]{1,0:T(8,128)(2,1)S(1)}, bf16[256,256]{1,0:T(8,128)(2,1)}, u32[]{:S(2)}) copy-start(bf16[256,256]{1,0:T(8,128)(2,1)} %refs_1_.1) | copy-start | bytes 393220
  1.3 12.9 %copy-start.12 = (bf16[256,256]{1,0:T(8,128)(2,1)S(1)}, bf16[256,256]{1,0:T(8,128)(2,1)}, u32[]{:S(2)}) copy-start(bf16[256,256]{1,0:T(8,128)(2,1)} %refs_2_.1) | copy-start | bytes 393220
  4.9 33.3 %all-to-all-start = ((bf16[8,128,128]{2,1,0:T(8,128)(2,1)}), bf16[8,128,128]{2,1,0:T(8,128)(2,1)S(1)}, u32[]{:S(2)}, u32[]{:S(2)}) async-start(bf16[8,128,128]{2,1,0:T(8,128)(2,1)} %ready.1), calls=%async_computation | async-start | bytes 524288 | tf_op jit(solution)/shard_map/all_to_all | solution.py:281
  12.2 19.2 %collective-permute-start = (bf16[4,64,256]{2,1,0:T(8,128)(2,1)S(1)}, bf16[4,64,256]{2,1,0:T(8,128)(2,1)S(1)}, u32[]{:S(2)}, u32[]{:S(2)}) collective-permute-start(bf16[4,64,256]{2,1,0:T(8,128)(2,1)S(1)} %copy-done.8), channel_id=1, source_target_pairs={{0,1},{1,0},{2,3},{3,2},{4,5},{5,4},{6,7},{7,6},{8,9},{9,8},{10,11... | collective-permute-start | bytes 393224 | tf_op jit(solution)/shard_map/ppermute | solution.py:16
  14.4 0.8 copy-start.2
  31.3 15.1 %copy-start.17 = (bf16[16,64,256]{2,1,0:T(8,128)(2,1)}, bf16[16,64,256]{2,1,0:T(8,128)(2,1)S(1)}, u32[]{:S(2)}) copy-start(bf16[16,64,256]{2,1,0:T(8,128)(2,1)S(1)} %all-gather) | copy-start | bytes 1572868
  31.4 27.7 %copy-start.19 = (bf16[2,4,64,256]{3,2,1,0:T(8,128)(2,1)}, bf16[2,4,64,256]{3,2,1,0:T(8,128)(2,1)S(1)}, u32[]{:S(2)}) copy-start(bf16[2,4,64,256]{3,2,1,0:T(8,128)(2,1)S(1)} %pad_maximum_fusion.refs_2_) | copy-start | bytes 786436
  31.4 15.1 %collective-permute-start.1 = (bf16[4,4,64,256]{3,2,1,0:T(8,128)(2,1)S(1)}, bf16[4,4,64,256]{3,2,1,0:T(8,128)(2,1)S(1)}, u32[]{:S(2)}, u32[]{:S(2)}) collective-permute-start(bf16[4,4,64,256]{3,2,1,0:T(8,128)(2,1)S(1)} %bitcast.22), channel_id=1, source_target_pairs={{0,1},{1,0},{2,3},{3,2},{4,5},{5,4},{6,7},{7,6},{8,9},{9,8},{10,11... | collective-permute-start | bytes 1572872 | tf_op jit(solution)/shard_map/ppermute | solution.py:16
  33.8 24.8 %collective-permute-start.2 = (bf16[2,4,64,256]{3,2,1,0:T(8,128)(2,1)S(1)}, bf16[2,4,64,256]{3,2,1,0:T(8,128)(2,1)S(1)}, u32[]{:S(2)}, u32[]{:S(2)}) collective-permute-start(bf16[2,4,64,256]{3,2,1,0:T(8,128)(2,1)S(1)} %pad_maximum_fusion.refs_2_), channel_id=1, source_target_pairs={{0,2},{1,3},{2,0},{3,1},{4,6},{5,7},{6,4},{7,5},{8,10},{9,11},{10,... | collective-permute-start | bytes 786440 | tf_op jit(solution)/shard_map/ppermute | solution.py:16
  34.2 24.3 %collective-permute-start.3 = (bf16[2,4,64,256]{3,2,1,0:T(8,128)(2,1)S(1)}, bf16[2,4,64,256]{3,2,1,0:T(8,128)(2,1)S(1)}, u32[]{:S(2)}, u32[]{:S(2)}) collective-permute-start(bf16[2,4,64,256]{3,2,1,0:T(8,128)(2,1)S(1)} %pad_maximum_fusion.refs_2_), channel_id=1, source_target_pairs={{0,4},{1,5},{2,6},{3,7},{4,0},{5,1},{6,2},{7,3},{8,12},{9,13},{10,... | collective-permute-start | bytes 786440 | tf_op jit(solution)/shard_map/ppermute | solution.py:16
  36.9 21.7 %collective-permute-start.4 = (bf16[2,4,64,256]{3,2,1,0:T(8,128)(2,1)S(1)}, bf16[2,4,64,256]{3,2,1,0:T(8,128)(2,1)S(1)}, u32[]{:S(2)}, u32[]{:S(2)}) collective-permute-start(bf16[2,4,64,256]{3,2,1,0:T(8,128)(2,1)S(1)} %pad_maximum_fusion.refs_2_), channel_id=1, source_target_pairs={{0,6},{1,7},{2,4},{3,5},{4,2},{5,3},{6,0},{7,1},{8,14},{9,15},{10,... | collective-permute-start | bytes 786440 | tf_op jit(solution)/shard_map/ppermute | solution.py:16
  46.4 0.8 copy-start.18
  58.6 6.9 %copy-start.20 = (bf16[2,4,64,256]{3,2,1,0:T(8,128)(2,1)}, bf16[2,4,64,256]{3,2,1,0:T(8,128)(2,1)S(1)}, u32[]{:S(2)}) copy-start(bf16[2,4,64,256]{3,2,1,0:T(8,128)(2,1)S(1)} %collective-permute-done.2.refs_3_) | copy-start | bytes 786436
  58.6 6.9 %copy-start.21 = (bf16[2,4,64,256]{3,2,1,0:T(8,128)(2,1)}, bf16[2,4,64,256]{3,2,1,0:T(8,128)(2,1)S(1)}, u32[]{:S(2)}) copy-start(bf16[2,4,64,256]{3,2,1,0:T(8,128)(2,1)S(1)} %collective-permute-done.3.refs_4_) | copy-start | bytes 786436
  58.6 6.9 %copy-start.22 = (bf16[2,4,64,256]{3,2,1,0:T(8,128)(2,1)}, bf16[2,4,64,256]{3,2,1,0:T(8,128)(2,1)S(1)}, u32[]{:S(2)}) copy-start(bf16[2,4,64,256]{3,2,1,0:T(8,128)(2,1)S(1)} %collective-permute-done.4.refs_5_) | copy-start | bytes 786436
  58.6 4.8 %collective-permute-start.5 = (f32[1024,128]{1,0:T(8,128)}, f32[1024,128]{1,0:T(8,128)S(1)}, u32[]{:S(2)}, u32[]{:S(2)}) collective-permute-start(f32[1024,128]{1,0:T(8,128)} %get-tuple-element.48), channel_id=1, source_target_pairs={{0,8},{8,0},{16,24},{24,16},{1,9},{9,1},{17,25},{25,17},{2,10},{10... | collective-permute-start | bytes 1572872 | tf_op jit(solution)/shard_map/ppermute | solution.py:16
  59.0 16.4 %all-to-all-start.1 = ((bf16[8,192,128]{2,1,0:T(8,128)(2,1)}), bf16[8,192,128]{2,1,0:T(8,128)(2,1)S(1)}, u32[]{:S(2)}, u32[]{:S(2)}) async-start(bf16[8,192,128]{2,1,0:T(8,128)(2,1)} %get-tuple-element.56), calls=%async_computation.1 | async-start | bytes 786432 | tf_op jit(solution)/shard_map/all_to_all | solution.py:356
  64.6 8.2 %collective-permute-start.6 = (f32[512,128]{1,0:T(8,128)S(1)}, f32[512,128]{1,0:T(8,128)S(1)}, u32[]{:S(2)}, u32[]{:S(2)}) collective-permute-start(f32[512,128]{1,0:T(8,128)S(1)} %get-tuple-element.52), channel_id=1, source_target_pairs={{0,16},{8,24},{16,0},{24,8},{1,17},{9,25},{17,1},{25,9},{2,18},{10... | collective-permute-start | bytes 786440 | tf_op jit(solution)/shard_map/ppermute | solution.py:16
  71.6 32.1 %copy-start.1 = (bf16[64,128,128]{2,1,0:T(8,128)(2,1)S(1)}, bf16[64,128,128]{2,1,0:T(8,128)(2,1)}, u32[]{:S(2)}) copy-start(bf16[64,128,128]{2,1,0:T(8,128)(2,1)} %rows_ref.1) | copy-start | bytes 6291460
  72.8 1.5 %collective-permute-start.7 = (f32[168,128]{1,0:T(8,128)}, f32[168,128]{1,0:T(8,128)S(1)}, u32[]{:S(2)}, u32[]{:S(2)}) collective-permute-start(f32[168,128]{1,0:T(8,128)} %get-tuple-element.55), channel_id=1, source_target_pairs={{0,8},{8,0},{16,24},{24,16},{1,9},{9,1},{17,25},{25,17},{2,10},{10... | collective-permute-start | bytes 258056 | tf_op jit(solution)/shard_map/ppermute | solution.py:16
  75.5 0.7 copy-start.4
  76.2 4.5 %collective-permute-start.8 = (f32[168,128]{1,0:T(8,128)S(1)}, f32[168,128]{1,0:T(8,128)S(1)}, u32[]{:S(2)}, u32[]{:S(2)}) collective-permute-start(f32[168,128]{1,0:T(8,128)S(1)} %add.10.keep), channel_id=1, source_target_pairs={{0,16},{8,24},{16,0},{24,8},{1,17},{9,25},{17,1},{25,9},{2,18},{10... | collective-permute-start | bytes 258056 | tf_op jit(solution)/shard_map/ppermute | solution.py:16
  80.7 0.9 copy-start.13
  81.7 26.1 %copy-start.3 = (bf16[8,128,256]{2,1,0:T(8,128)(2,1)S(1)}, bf16[8,128,256]{2,1,0:T(8,128)(2,1)}, u32[]{:S(2)}) copy-start(bf16[8,128,256]{2,1,0:T(8,128)(2,1)} %copy-done.2) | copy-start | bytes 1572868
  81.7 26.1 %copy-start.15 = (f32[256]{0:T(256)S(1)}, f32[256]{0:T(256)}, u32[]{:S(2)}) copy-start(f32[256]{0:T(256)} %param.13) | copy-start | bytes 3076
  103.8 8.5 %collective-permute-start.9 = (bf16[8,304,128]{2,1,0:T(8,128)(2,1)S(1)}, bf16[8,304,128]{2,1,0:T(8,128)(2,1)}, u32[]{:S(2)}, u32[]{:S(2)}) collective-permute-start(bf16[8,304,128]{2,1,0:T(8,128)(2,1)S(1)} %all_to_all.20.grad_ref.back.mine), channel_id=1, source_target_pairs={{0,8},{8,0},{16,24},{24,16},{1,9},{9,1},{17,25},{25,17},{2,10},{10... | collective-permute-start | bytes 1867784 | tf_op jit(solution)/shard_map/ppermute | solution.py:16
  105.1 10.3 %all-to-all-start.3 = ((f32[32,8,128]{2,1,0:T(8,128)}), f32[32,8,128]{2,1,0:T(8,128)S(1)}, u32[]{:S(2)}, u32[]{:S(2)}) async-start(f32[32,8,128]{2,1,0:T(8,128)} %pair.1), calls=%async_computation.3 | async-start | bytes 262144 | tf_op jit(solution)/shard_map/all_to_all | solution.py:383
  107.7 4.5 %copy-start.16 = (s32[2]{0:T(128)S(1)}, s32[2]{0:T(128)}, u32[]{:S(2)}) copy-start(s32[2]{0:T(128)} %pad_add_fusion.where) | copy-start | bytes 28
  107.7 1.0 copy-start.5

commit v4 on v3

--- a/solution.py
+++ b/solution.py
@@ -321,7 +321,7 @@
             jax.ShapeDtypeStruct((n_res, 3 * flat, part), BF16),
         ]
         + [jax.ShapeDtypeStruct((pair_rows, part), F32)] * 2,
-        compiler_params=params(60),
+        compiler_params=params(32),
         name="attention",
     )(where, *tokens, bias_all, datts, head_weights, gain_row)
 
@@ -349,19 +349,19 @@
             pltpu.VMEM((sum_rows, channels), F32),
         ],
         out_shape=[jax.ShapeDtypeStruct((n_res, flat, part), BF16), partial, partial],
-        compiler_params=params(60),
+        compiler_params=params(32),
         name="gradients",
     )(where, *tokens, *slopes, flow, head_weights, out_weights, gain_row)
 
     packed = lax.all_to_all(packed, "res", 0, 0, tiled=True)
-    pair_come, grads, send = lax.optimization_barrier((pair_come, grads, send))
     step = 1
     while step < n_seq:
         come = exchange(send, "seq", n_seq, step)
         step *= 2
         if step < n_seq:
-            send, packed = lax.optimization_barrier((keep + come, packed))
+            send, pair_come = lax.optimization_barrier((keep + come, pair_come))
             keep = send
+    come, packed = lax.optimization_barrier((come, packed))
     back_rows = own + flat + sum_rows + 8
     back = pl.pallas_call(
         functools.partial(back_kernel, 5 * width),

time: 117 us -> 111 us (0.949)
  local copies, waits for them, and re-layouts: 5.62 us -> 3.33 us
  Pallas kernels: 24.6 us -> 22.5 us
    ppermute x10, waiting for transfers between devices: 6.28 us -> 4.44 us  [exchange(): return lax.ppermute(value, axis, [(i, i ^ offset) for i in range(size)])]
    unnamed x46 -> x26, local copies, waits for them, and re-layouts: 4.9 us -> 3.26 us
    pallas_call x1, Pallas kernels: 6.14 us -> 4.54 us  [by_head(): pl.pallas_call(functools.partial(gradient_kernel, n_res, width), in_specs...]
    pallas_call x1, Pallas kernels: 11.3 us -> 9.9 us  [by_head(): pl.pallas_call(functools.partial(attention_kernel, n_res, n_seq, width, t...]
  transfers between devices with their start and end apart: 13 -> 13, of which waited for: 5 -> 5; matrix products, arithmetic and copies ran while one was open for 5% -> 4% of each run, Pallas kernels for 20% -> 19%
where the time goes in v4:
time: 111 us
  blocking collectives  45.7 us (41%)
  starting transfers between devices  25.2 us (23%)
  Pallas kernels  22.5 us (20%)
  waiting for transfers between devices  5.89 us (5%)
  matrix products  4.5 us (4%)
  local copies, waits for them, and re-layouts  3.33 us (3%)
  other arithmetic  2.57 us (2%)
    all_to_all x1, blocking collectives, by_head(): back = lax.all_to_all(back, 'res', 0, 0, tiled=True)  21.3 us
    all_gather x1, blocking collectives, by_head(): lax.all_gather(homolog_embedding, 'res', axis=0, axis_index_groups=lines)  17.1 us
    ppermute x10, starting transfers between devices, exchange(): return lax.ppermute(value, axis, [(i, i ^ offset) for i in range(size)])  10.5 us
    pallas_call x1, Pallas kernels, by_head(): pl.pallas_call(functools.partial(attention_kernel, n_res, n_seq, width, t...  9.9 us
    all_to_all x1, starting transfers between devices, by_head(): ready = lax.all_to_all(ready, 'res', 0, 0, tiled=True)  7.28 us
    all_gather x1, blocking collectives, by_head(): lax.all_gather(ready[:, :own].reshape(total, part), 'seq', axis=0)  7.22 us
    pallas_call x1, Pallas kernels, by_head(): pl.pallas_call(functools.partial(gradient_kernel, n_res, width), in_specs...  4.54 us
    ppermute x10, waiting for transfers between devices, exchange(): return lax.ppermute(value, axis, [(i, i ^ offset) for i in range(size)])  4.44 us
  transfers between devices with their start and end apart: 13, of which 5 were waited for; matrix products, arithmetic and copies ran while one was open for 4% of the time, Pallas kernels for 19%

profile of v4, /device:TPU:0, one launch (start us, length us, event | category | flops | bytes accessed | tf_op | source)
XLA Modules:
  0.0 110.6 jit_solution(2102070711081438900)
XLA Ops:
  0.6 0.0 copy-start
  0.7 0.0 copy-start.4
  0.7 0.6 copy-done
  1.3 2.3 %fusion.2 = bf16[8,64,128]{2,0,1:T(8,128)(2,1)S(1)} fusion(bf16[64,128,128]{2,1,0:T(8,128)(2,1)} %rows_ref.1, bf16[128,8]{0,1:T(8,128)(2,1)S(1)} %copy-done), kind=kOutput, calls=%fused_computation.7 | convolution fusion | flops 16777216 | bytes 2230272 | tf_op jit(solution)/shard_map/ijc,ch->hij/dot_general | solution.py:271
  3.7 1.2 %ready.1 = bf16[8,128,128]{2,1,0:T(8,128)(2,1)} custom-call(bf16[4,64,256]{2,1,0:T(8,128)(2,1)S(1)} %copy-done.2, bf16[4,64,256]{2,1,0:T(8,128)(2,1)S(1)} %copy-done.6, bf16[8,64,128]{2,1,0:T(8,128)(2,1)S(1)} %copy.26.bias_ref, bf16[256,256]{1,0:T(8,128)(2,1)S(1)} %copy-done.7, bf16[256,256]{1,0:T(8,128)(2,1)S(1)} %copy-done.4, f32[1,256]{1,0:T(1,128)S(1)} %bitcast.21), custom_call_target="tpu_custom_call" | custom-call | tf_op jit(solution)/shard_map/ready/pallas_call | solution.py:275
  4.9 7.3 %all-to-all-start = ((bf16[8,128,128]{2,1,0:T(8,128)(2,1)}), bf16[8,128,128]{2,1,0:T(8,128)(2,1)S(1)}, u32[]{:S(2)}, u32[]{:S(2)}) async-start(bf16[8,128,128]{2,1,0:T(8,128)(2,1)} %ready.1), calls=%async_computation | async-start | bytes 524288 | tf_op jit(solution)/shard_map/all_to_all | solution.py:281
  12.2 2.0 %collective-permute-start = (bf16[4,64,256]{2,1,0:T(8,128)(2,1)S(1)}, bf16[4,64,256]{2,1,0:T(8,128)(2,1)S(1)}, u32[]{:S(2)}, u32[]{:S(2)}) collective-permute-start(bf16[4,64,256]{2,1,0:T(8,128)(2,1)S(1)} %copy-done.6), channel_id=1, source_target_pairs={{0,1},{1,0},{2,3},{3,2},{4,5},{5,4},{6,7},{7,6},{8,9},{9,8},{10,11... | collective-permute-start | bytes 393224 | tf_op jit(solution)/shard_map/ppermute | solution.py:16
  14.2 0.2 weights.1.refs_4_.refs_7_
  14.4 17.1 %all-gather = bf16[16,64,256]{2,1,0:T(8,128)(2,1)S(1)} all-gather(bf16[4,64,256]{2,1,0:T(8,128)(2,1)S(1)} %copy-done.2), channel_id=2, replica_groups={{0,2,4,6},{1,3,5,7},{8,10,12,14},{9,11,13,15},{16,18,20,22},{17,19,21,2..., dimensions={0}, use_global_device_ids=true | all-gather | bytes 655360 | tf_op jit(solution)/shard_map/all_gather | solution.py:283
  31.5 0.0 collective-permute-done
  31.6 2.0 %collective-permute-start.1 = (bf16[4,4,64,256]{3,2,1,0:T(8,128)(2,1)S(1)}, bf16[4,4,64,256]{3,2,1,0:T(8,128)(2,1)S(1)}, u32[]{:S(2)}, u32[]{:S(2)}) collective-permute-start(bf16[4,4,64,256]{3,2,1,0:T(8,128)(2,1)S(1)} %bitcast.16), channel_id=1, source_target_pairs={{0,1},{1,0},{2,3},{3,2},{4,5},{5,4},{6,7},{7,6},{8,9},{9,8},{10,11... | collective-permute-start | bytes 1572872 | tf_op jit(solution)/shard_map/ppermute | solution.py:16
  33.5 0.1 pad_add_fusion.where
  33.6 0.0 collective-permute-start.2
  33.6 2.4 %collective-permute-start.3 = (bf16[2,4,64,256]{3,2,1,0:T(8,128)(2,1)S(1)}, bf16[2,4,64,256]{3,2,1,0:T(8,128)(2,1)}, u32[]{:S(2)}, u32[]{:S(2)}) collective-permute-start(bf16[2,4,64,256]{3,2,1,0:T(8,128)(2,1)S(1)} %pad_maximum_fusion.refs_2_), channel_id=1, source_target_pairs={{0,4},{1,5},{2,6},{3,7},{4,0},{5,1},{6,2},{7,3},{8,12},{9,13},{10,... | collective-permute-start | bytes 786440 | tf_op jit(solution)/shard_map/ppermute | solution.py:16
  36.1 2.0 %collective-permute-start.4 = (bf16[2,4,64,256]{3,2,1,0:T(8,128)(2,1)S(1)}, bf16[2,4,64,256]{3,2,1,0:T(8,128)(2,1)}, u32[]{:S(2)}, u32[]{:S(2)}) collective-permute-start(bf16[2,4,64,256]{3,2,1,0:T(8,128)(2,1)S(1)} %pad_maximum_fusion.refs_2_), channel_id=1, source_target_pairs={{0,6},{1,7},{2,4},{3,5},{4,2},{5,3},{6,0},{7,1},{8,14},{9,15},{10,... | collective-permute-start | bytes 786440 | tf_op jit(solution)/shard_map/ppermute | solution.py:16
  38.0 0.0 all-to-all-done
  38.0 7.2 %all_gather.11.refs_2_ = bf16[4,512,128]{2,1,0:T(8,128)(2,1)S(1)} all-gather(bf16[1,512,128]{2,1,0:T(8,128)(2,1)S(1)} %bitcast.25), channel_id=1, replica_groups=mesh['seq'=4,'res'=8] {'seq'}, dimensions={0}, use_global_device_ids=true | all-gather | bytes 655360 | tf_op jit(solution)/shard_map/all_gather | solution.py:288
  45.3 0.0 collective-permute-done.1.refs_1_
  45.3 9.9 %attention.1 = (f32[4,128,512]{2,1,0:T(8,128)S(1)}, bf16[8,192,128]{2,1,0:T(8,128)(2,1)S(1)}, f32[1024,128]{1,0:T(8,128)S(1)}, f32[1024,128]{1,0:T(8,128)}) custom-call(s32[2]{0:T(128)S(1)} %pad_add_fusion.where, bf16[4,4,64,256]{3,2,1,0:T(8,128)(2,1)S(1)} %bitcast.17, bf16[4,4,64,256]{3,2,1,0:T(8,128)(2,1)S(1)} %collective-permute-done.1.refs_1_, ...), custom_call_target="tpu_custom_call" | custom-call | tf_op jit(solution)/shard_map/attention/pallas_call | solution.py:309
  55.2 0.8 copy-done.8
  55.9 0.0 collective-permute-done.2.refs_3_
  55.9 0.0 collective-permute-done.3.refs_4_
  55.9 0.0 collective-permute-done.4.refs_5_
  55.9 0.4 collective-permute-start.5
  56.3 4.1 %all-to-all-start.1 = ((bf16[8,192,128]{2,1,0:T(8,128)(2,1)}), bf16[8,192,128]{2,1,0:T(8,128)(2,1)}, u32[]{:S(2)}, u32[]{:S(2)}) async-start(bf16[8,192,128]{2,1,0:T(8,128)(2,1)} %copy-done.8), calls=%async_computation.1 | async-start | bytes 786432 | tf_op jit(solution)/shard_map/all_to_all | solution.py:356
  60.4 0.0 collective-permute-done.5
  60.4 1.8 %slice_add_fusion = (f32[512,128]{1,0:T(8,128)}, f32[512,128]{1,0:T(8,128)S(1)}) fusion(f32[1024,128]{1,0:T(8,128)} %collective-permute-done.5, f32[1024,128]{1,0:T(8,128)S(1)} %get-tuple-element.46), kind=kLoop, calls=%fused_computation.1 | loop fusion | flops 131072 | bytes 1572864 | tf_op jit(solution)/shard_map/add | solution.py:336
  62.3 0.8 collective-permute-start.7
  63.1 0.9 copy-done.5
  64.0 4.5 %gradients.1 = (bf16[8,64,128]{2,1,0:T(8,128)(2,1)S(1)}, f32[168,128]{1,0:T(8,128)S(1)}, f32[168,128]{1,0:T(8,128)S(1)}) custom-call(s32[2]{0:T(128)S(1)} %pad_add_fusion.where, bf16[4,4,64,256]{3,2,1,0:T(8,128)(2,1)S(1)} %bitcast.18, bf16[4,4,64,256]{3,2,1,0:T(8,128)(2,1)S(1)} %collective-permute-done.1.refs_1_, ...), custom_call_target="tpu_custom_call" | custom-call | tf_op jit(solution)/shard_map/gradients/pallas_call | solution.py:340
  68.5 0.0 copy-start.1
  68.6 0.1 collective-permute-start.6
  68.6 1.3 %collective-permute-done.6 = f32[168,128]{1,0:T(8,128)S(1)} collective-permute-done((f32[168,128]{1,0:T(8,128)S(1)}, f32[168,128]{1,0:T(8,128)S(1)}, u32[]{:S(2)}, u32[]{:S(2)}) %collective-permute-start.6) | collective-permute-done | bytes 86048 | tf_op jit(solution)/shard_map/ppermute | solution.py:16
  69.9 0.7 collective-permute-done.7.pair_come
  70.7 0.8 collective-permute-start.8
  71.5 1.3 %all-to-all-done.1.packed = bf16[8,192,128]{2,1,0:T(8,128)(2,1)} async-done(((bf16[8,192,128]{2,1,0:T(8,128)(2,1)}), bf16[8,192,128]{2,1,0:T(8,128)(2,1)}, u32[]{:S(2)}, u32[]{:S(2)}) %all-to-all-start.1) | async-done | bytes 393248 | tf_op jit(solution)/shard_map/all_to_all | solution.py:356
  72.7 2.4 %collective-permute-done.8.come = f32[168,128]{1,0:T(8,128)S(1)} collective-permute-done((f32[168,128]{1,0:T(8,128)S(1)}, f32[168,128]{1,0:T(8,128)S(1)}, u32[]{:S(2)}, u32[]{:S(2)}) %collective-permute-start.8) | collective-permute-done | bytes 86048 | tf_op jit(solution)/shard_map/ppermute | solution.py:16
  75.2 0.9 copy-done.3
  76.1 0.1 back.1
  76.2 21.3 %all_to_all.20.grad_ref.back.mine = bf16[8,304,128]{2,1,0:T(8,128)(2,1)S(1)} all-to-all(bf16[8,304,128]{2,1,0:T(8,128)(2,1)S(1)} %back.1), channel_id=1, replica_groups=mesh['seq'=4,'res'=8] {'res'}, dimensions={0} | all-to-all | bytes 1245184 | tf_op jit(solution)/shard_map/all_to_all | solution.py:372
  97.5 0.0 collective-permute-start.9
  97.5 1.4 %pair.1 = f32[32,8,128]{2,1,0:T(8,128)} custom-call(bf16[8,304,128]{2,1,0:T(8,128)(2,1)S(1)} %all_to_all.20.grad_ref.back.mine, bf16[64,128,128]{2,1,0:T(8,128)(2,1)S(1)} %copy-done.1), custom_call_target="tpu_custom_call" | custom-call | tf_op jit(solution)/shard_map/pair/pallas_call | solution.py:373
  98.8 3.4 %all-to-all-start.3 = ((f32[32,8,128]{2,1,0:T(8,128)}), f32[32,8,128]{2,1,0:T(8,128)S(1)}, u32[]{:S(2)}, u32[]{:S(2)}) async-start(f32[32,8,128]{2,1,0:T(8,128)} %pair.1), calls=%async_computation.3 | async-start | bytes 262144 | tf_op jit(solution)/shard_map/all_to_all | solution.py:383
  102.2 2.2 %tail.1 = bf16[4,64,256]{2,1,0:T(8,128)(2,1)} custom-call(bf16[8,192,128]{2,1,0:T(8,128)(2,1)} %all-to-all-done.1.packed, bf16[8,304,128]{2,1,0:T(8,128)(2,1)S(1)} %all_to_all.20.grad_ref.back.mine, bf16[4,64,256]{2,1,0:T(8,128)(2,1)S(1)} %copy-done.2, bf16[8,128,256]{2,1,0:T(8,128)(2,1)S(1)} %weights.1.refs_4_.refs_7_, f32[1,256]{1,0:T(1,128)S(1)} %bitcast.24), custom_call_target="tpu_custom_call" | custom-call | tf_op jit(solution)/shard_map/tail/pallas_call | solution.py:388
  104.5 2.2 %convolution_convert_fusion = bf16[64,128,128]{2,1,0:T(8,128)(2,1)} fusion(bf16[8,64,128]{2,1,0:T(8,128)(2,1)S(1)} %slice.32, bf16[128,8]{0,1:T(8,128)(2,1)S(1)} %copy-done), kind=kOutput, calls=%fused_computation | convolution fusion | flops 17825792 | bytes 2230272 | tf_op jit(solution)/shard_map/hij,ch->ijc/dot_general | solution.py:384
  106.7 3.1 %sums.1 = (f32[1,256]{1,0:T(1,128)}, f32[256,256]{1,0:T(8,128)}, f32[256,256]{1,0:T(8,128)}, f32[256,256]{1,0:T(8,128)}, f32[256,256]{1,0:T(8,128)}, /*index=5*/f32[256,256]{1,0:T(8,128)}) custom-call(s32[2]{0:T(128)S(1)} %pad_add_fusion.where, bf16[8,304,128]{2,1,0:T(8,128)(2,1)S(1)} %all_to_all.20.grad_ref.back.mine, ...), custom_call_target="tpu_custom_call" | custom-call | tf_op jit(solution)/shard_map/sums/pallas_call | solution.py:396
  109.8 0.2 all-to-all-done.3
  110.0 0.6 reduce_sum.9
  (25 shorter events, 0.1 us)
Async XLA Ops:
  0.6 0.7 copy-start
  0.7 3.0 %copy-start.2 = (bf16[4,64,256]{2,1,0:T(8,128)(2,1)S(1)}, bf16[4,64,256]{2,1,0:T(8,128)(2,1)}, u32[]{:S(2)}) copy-start(bf16[4,64,256]{2,1,0:T(8,128)(2,1)} %own_ref.2) | copy-start | bytes 393220
  0.7 3.0 %copy-start.6 = (bf16[4,64,256]{2,1,0:T(8,128)(2,1)S(1)}, bf16[4,64,256]{2,1,0:T(8,128)(2,1)}, u32[]{:S(2)}) copy-start(bf16[4,64,256]{2,1,0:T(8,128)(2,1)} %slope_ref.1) | copy-start | bytes 393220
  0.7 3.0 %copy-start.7 = (bf16[256,256]{1,0:T(8,128)(2,1)S(1)}, bf16[256,256]{1,0:T(8,128)(2,1)}, u32[]{:S(2)}) copy-start(bf16[256,256]{1,0:T(8,128)(2,1)} %refs_3_.1) | copy-start | bytes 393220
  0.7 3.0 %copy-start.4 = (bf16[256,256]{1,0:T(8,128)(2,1)S(1)}, bf16[256,256]{1,0:T(8,128)(2,1)}, u32[]{:S(2)}) copy-start(bf16[256,256]{1,0:T(8,128)(2,1)} %out_w.1) | copy-start | bytes 393220
  0.7 3.0 %copy-start.12 = (f32[256]{0:T(256)S(1)}, f32[256]{0:T(256)}, u32[]{:S(2)}) copy-start(f32[256]{0:T(256)} %param.13) | copy-start | bytes 3076
  0.7 13.5 %copy-start.9 = (bf16[256,256]{1,0:T(8,128)(2,1)S(1)}, bf16[256,256]{1,0:T(8,128)(2,1)}, u32[]{:S(2)}) copy-start(bf16[256,256]{1,0:T(8,128)(2,1)} %refs_0_.1) | copy-start | bytes 393220
  0.7 13.5 %copy-start.10 = (bf16[256,256]{1,0:T(8,128)(2,1)S(1)}, bf16[256,256]{1,0:T(8,128)(2,1)}, u32[]{:S(2)}) copy-start(bf16[256,256]{1,0:T(8,128)(2,1)} %refs_1_.1) | copy-start | bytes 393220
  1.3 12.9 %copy-start.11 = (bf16[256,256]{1,0:T(8,128)(2,1)S(1)}, bf16[256,256]{1,0:T(8,128)(2,1)}, u32[]{:S(2)}) copy-start(bf16[256,256]{1,0:T(8,128)(2,1)} %refs_2_.1) | copy-start | bytes 393220
  4.9 33.1 %all-to-all-start = ((bf16[8,128,128]{2,1,0:T(8,128)(2,1)}), bf16[8,128,128]{2,1,0:T(8,128)(2,1)S(1)}, u32[]{:S(2)}, u32[]{:S(2)}) async-start(bf16[8,128,128]{2,1,0:T(8,128)(2,1)} %ready.1), calls=%async_computation | async-start | bytes 524288 | tf_op jit(solution)/shard_map/all_to_all | solution.py:281
  12.2 19.4 %collective-permute-start = (bf16[4,64,256]{2,1,0:T(8,128)(2,1)S(1)}, bf16[4,64,256]{2,1,0:T(8,128)(2,1)S(1)}, u32[]{:S(2)}, u32[]{:S(2)}) collective-permute-start(bf16[4,64,256]{2,1,0:T(8,128)(2,1)S(1)} %copy-done.6), channel_id=1, source_target_pairs={{0,1},{1,0},{2,3},{3,2},{4,5},{5,4},{6,7},{7,6},{8,9},{9,8},{10,11... | collective-permute-start | bytes 393224 | tf_op jit(solution)/shard_map/ppermute | solution.py:16
  31.6 13.7 %collective-permute-start.1 = (bf16[4,4,64,256]{3,2,1,0:T(8,128)(2,1)S(1)}, bf16[4,4,64,256]{3,2,1,0:T(8,128)(2,1)S(1)}, u32[]{:S(2)}, u32[]{:S(2)}) collective-permute-start(bf16[4,4,64,256]{3,2,1,0:T(8,128)(2,1)S(1)} %bitcast.16), channel_id=1, source_target_pairs={{0,1},{1,0},{2,3},{3,2},{4,5},{5,4},{6,7},{7,6},{8,9},{9,8},{10,11... | collective-permute-start | bytes 1572872 | tf_op jit(solution)/shard_map/ppermute | solution.py:16
  33.6 22.3 %collective-permute-start.2 = (bf16[2,4,64,256]{3,2,1,0:T(8,128)(2,1)S(1)}, bf16[2,4,64,256]{3,2,1,0:T(8,128)(2,1)}, u32[]{:S(2)}, u32[]{:S(2)}) collective-permute-start(bf16[2,4,64,256]{3,2,1,0:T(8,128)(2,1)S(1)} %pad_maximum_fusion.refs_2_), channel_id=1, source_target_pairs={{0,2},{1,3},{2,0},{3,1},{4,6},{5,7},{6,4},{7,5},{8,10},{9,11},{10,... | collective-permute-start | bytes 786440 | tf_op jit(solution)/shard_map/ppermute | solution.py:16
  33.6 22.3 %collective-permute-start.3 = (bf16[2,4,64,256]{3,2,1,0:T(8,128)(2,1)S(1)}, bf16[2,4,64,256]{3,2,1,0:T(8,128)(2,1)}, u32[]{:S(2)}, u32[]{:S(2)}) collective-permute-start(bf16[2,4,64,256]{3,2,1,0:T(8,128)(2,1)S(1)} %pad_maximum_fusion.refs_2_), channel_id=1, source_target_pairs={{0,4},{1,5},{2,6},{3,7},{4,0},{5,1},{6,2},{7,3},{8,12},{9,13},{10,... | collective-permute-start | bytes 786440 | tf_op jit(solution)/shard_map/ppermute | solution.py:16
  36.1 19.9 %collective-permute-start.4 = (bf16[2,4,64,256]{3,2,1,0:T(8,128)(2,1)S(1)}, bf16[2,4,64,256]{3,2,1,0:T(8,128)(2,1)}, u32[]{:S(2)}, u32[]{:S(2)}) collective-permute-start(bf16[2,4,64,256]{3,2,1,0:T(8,128)(2,1)S(1)} %pad_maximum_fusion.refs_2_), channel_id=1, source_target_pairs={{0,6},{1,7},{2,4},{3,5},{4,2},{5,3},{6,0},{7,1},{8,14},{9,15},{10,... | collective-permute-start | bytes 786440 | tf_op jit(solution)/shard_map/ppermute | solution.py:16
  55.2 0.8 copy-start.8
  55.9 4.5 %collective-permute-start.5 = (f32[1024,128]{1,0:T(8,128)}, f32[1024,128]{1,0:T(8,128)}, u32[]{:S(2)}, u32[]{:S(2)}) collective-permute-start(f32[1024,128]{1,0:T(8,128)} %get-tuple-element.47), channel_id=1, source_target_pairs={{0,8},{8,0},{16,24},{24,16},{1,9},{9,1},{17,25},{25,17},{2,10},{10... | collective-permute-start | bytes 1572872 | tf_op jit(solution)/shard_map/ppermute | solution.py:16
  56.3 16.4 %all-to-all-start.1 = ((bf16[8,192,128]{2,1,0:T(8,128)(2,1)}), bf16[8,192,128]{2,1,0:T(8,128)(2,1)}, u32[]{:S(2)}, u32[]{:S(2)}) async-start(bf16[8,192,128]{2,1,0:T(8,128)(2,1)} %copy-done.8), calls=%async_computation.1 | async-start | bytes 786432 | tf_op jit(solution)/shard_map/all_to_all | solution.py:356
  62.3 8.4 %collective-permute-start.7 = (f32[512,128]{1,0:T(8,128)S(1)}, f32[512,128]{1,0:T(8,128)S(1)}, u32[]{:S(2)}, u32[]{:S(2)}) collective-permute-start(f32[512,128]{1,0:T(8,128)S(1)} %get-tuple-element.52), channel_id=1, source_target_pairs={{0,16},{8,24},{16,0},{24,8},{1,17},{9,25},{17,1},{25,9},{2,18},{10... | collective-permute-start | bytes 786440 | tf_op jit(solution)/shard_map/ppermute | solution.py:16
  63.1 0.9 copy-start.5
  68.5 28.9 %copy-start.1 = (bf16[64,128,128]{2,1,0:T(8,128)(2,1)S(1)}, bf16[64,128,128]{2,1,0:T(8,128)(2,1)}, u32[]{:S(2)}) copy-start(bf16[64,128,128]{2,1,0:T(8,128)(2,1)} %rows_ref.1) | copy-start | bytes 6291460
  68.6 1.3 %collective-permute-start.6 = (f32[168,128]{1,0:T(8,128)S(1)}, f32[168,128]{1,0:T(8,128)S(1)}, u32[]{:S(2)}, u32[]{:S(2)}) collective-permute-start(f32[168,128]{1,0:T(8,128)S(1)} %get-tuple-element.51), channel_id=1, source_target_pairs={{0,8},{8,0},{16,24},{24,16},{1,9},{9,1},{17,25},{25,17},{2,10},{10... | collective-permute-start | bytes 258056 | tf_op jit(solution)/shard_map/ppermute | solution.py:16
  70.7 4.5 %collective-permute-start.8 = (f32[168,128]{1,0:T(8,128)S(1)}, f32[168,128]{1,0:T(8,128)S(1)}, u32[]{:S(2)}, u32[]{:S(2)}) collective-permute-start(f32[168,128]{1,0:T(8,128)S(1)} %add.10.keep), channel_id=1, source_target_pairs={{0,16},{8,24},{16,0},{24,8},{1,17},{9,25},{17,1},{25,9},{2,18},{10... | collective-permute-start | bytes 258056 | tf_op jit(solution)/shard_map/ppermute | solution.py:16
  75.1 1.0 copy-start.3
  97.5 9.3 %collective-permute-start.9 = (bf16[8,304,128]{2,1,0:T(8,128)(2,1)S(1)}, bf16[8,304,128]{2,1,0:T(8,128)(2,1)}, u32[]{:S(2)}, u32[]{:S(2)}) collective-permute-start(bf16[8,304,128]{2,1,0:T(8,128)(2,1)S(1)} %all_to_all.20.grad_ref.back.mine), channel_id=1, source_target_pairs={{0,8},{8,0},{16,24},{24,16},{1,9},{9,1},{17,25},{25,17},{2,10},{10... | collective-permute-start | bytes 1867784 | tf_op jit(solution)/shard_map/ppermute | solution.py:16
  98.8 11.1 %all-to-all-start.3 = ((f32[32,8,128]{2,1,0:T(8,128)}), f32[32,8,128]{2,1,0:T(8,128)S(1)}, u32[]{:S(2)}, u32[]{:S(2)}) async-start(f32[32,8,128]{2,1,0:T(8,128)} %pair.1), calls=%async_computation.3 | async-start | bytes 262144 | tf_op jit(solution)/shard_map/all_to_all | solution.py:383

commit v5 on v4

--- a/solution.py
+++ b/solution.py
@@ -10,6 +10,7 @@
 
 F32 = jnp.float32
 BF16 = jnp.bfloat16
+LOG2E = 1.0 / math.log(2.0)
 
 
 def exchange(value, axis, size, offset):
@@ -66,7 +67,7 @@
     scale = 1.0 / math.sqrt(width)
 
     for m in range(n_seq):
-        bias_s[:, m * part : (m + 1) * part] = biases[m]
+        bias_s[:, m * part : (m + 1) * part] = biases[m].astype(F32) * LOG2E
     for k in range(n_res):
         for n in range(datts.shape[1] // width):
             block = jnp.transpose(datts[k, n * width : (n + 1) * width, :].astype(F32)).astype(BF16)
@@ -96,9 +97,9 @@
         gqs, atts = [], []
         for c in range(total // span):
             lo, hi = c * span, (c + 1) * span
-            scores = dot(q[lo:hi], k_t) * scale + bias_s[lo:hi, :].astype(F32)
+            scores = dot(q[lo:hi], k_t) * (scale * LOG2E) + bias_s[lo:hi, :]
             top = jnp.max(scores, axis=-1, keepdims=True)
-            e = jnp.exp(scores - top)
+            e = jnp.exp2(scores - top)
             soft = e * (1.0 / jnp.sum(e, axis=-1, keepdims=True))
             half = soft.astype(BF16)
             atts.append(dot(half, v))
@@ -313,7 +314,7 @@
         scratch_shapes=[
             pltpu.VMEM((total, channels), BF16),
             pltpu.VMEM((rows, total, width), BF16),
-            pltpu.VMEM((total, total), BF16),
+            pltpu.VMEM((total, total), F32),
             pltpu.VMEM((total, total), F32),
         ],
         out_shape=[

time: 111 us -> 111 us (level)
  no operation moved by 1% of the time
where the time goes in v5:
time: 111 us
  blocking collectives  45.7 us (41%)
  starting transfers between devices  25.2 us (23%)
  Pallas kernels  22.5 us (20%)
  waiting for transfers between devices  5.89 us (5%)
  matrix products  4.5 us (4%)
  local copies, waits for them, and re-layouts  3.33 us (3%)
  other arithmetic  2.57 us (2%)
    all_to_all x1, blocking collectives, by_head(): back = lax.all_to_all(back, 'res', 0, 0, tiled=True)  21.3 us
    all_gather x1, blocking collectives, by_head(): lax.all_gather(homolog_embedding, 'res', axis=0, axis_index_groups=lines)  17.1 us
    ppermute x10, starting transfers between devices, exchange(): return lax.ppermute(value, axis, [(i, i ^ offset) for i in range(size)])  10.5 us
    pallas_call x1, Pallas kernels, by_head(): pl.pallas_call(functools.partial(attention_kernel, n_res, n_seq, width, t...  9.88 us
    all_to_all x1, starting transfers between devices, by_head(): ready = lax.all_to_all(ready, 'res', 0, 0, tiled=True)  7.28 us
    all_gather x1, blocking collectives, by_head(): lax.all_gather(ready[:, :own].reshape(total, part), 'seq', axis=0)  7.22 us
    pallas_call x1, Pallas kernels, by_head(): pl.pallas_call(functools.partial(gradient_kernel, n_res, width), in_specs...  4.54 us
    ppermute x10, waiting for transfers between devices, exchange(): return lax.ppermute(value, axis, [(i, i ^ offset) for i in range(size)])  4.44 us
  transfers between devices with their start and end apart: 13, of which 5 were waited for; matrix products, arithmetic and copies ran while one was open for 4% of the time, Pallas kernels for 19%

profile of v5, /device:TPU:0, one launch (start us, length us, event | category | flops | bytes accessed | tf_op | source)
XLA Modules:
  0.0 110.6 jit_solution(12483241327454726442)
XLA Ops:
  0.6 0.0 copy-start
  0.7 0.0 copy-start.4
  0.7 0.6 copy-done
  1.3 2.3 %fusion.2 = bf16[8,64,128]{2,0,1:T(8,128)(2,1)S(1)} fusion(bf16[64,128,128]{2,1,0:T(8,128)(2,1)} %rows_ref.1, bf16[128,8]{0,1:T(8,128)(2,1)S(1)} %copy-done), kind=kOutput, calls=%fused_computation.7 | convolution fusion | flops 16777216 | bytes 2230272 | tf_op jit(solution)/shard_map/ijc,ch->hij/dot_general | solution.py:272
  3.7 1.2 %ready.1 = bf16[8,128,128]{2,1,0:T(8,128)(2,1)} custom-call(bf16[4,64,256]{2,1,0:T(8,128)(2,1)S(1)} %copy-done.2, bf16[4,64,256]{2,1,0:T(8,128)(2,1)S(1)} %copy-done.6, bf16[8,64,128]{2,1,0:T(8,128)(2,1)S(1)} %copy.26.bias_ref, bf16[256,256]{1,0:T(8,128)(2,1)S(1)} %copy-done.7, bf16[256,256]{1,0:T(8,128)(2,1)S(1)} %copy-done.4, f32[1,256]{1,0:T(1,128)S(1)} %bitcast.21), custom_call_target="tpu_custom_call" | custom-call | tf_op jit(solution)/shard_map/ready/pallas_call | solution.py:276
  4.9 7.3 %all-to-all-start = ((bf16[8,128,128]{2,1,0:T(8,128)(2,1)}), bf16[8,128,128]{2,1,0:T(8,128)(2,1)S(1)}, u32[]{:S(2)}, u32[]{:S(2)}) async-start(bf16[8,128,128]{2,1,0:T(8,128)(2,1)} %ready.1), calls=%async_computation | async-start | bytes 524288 | tf_op jit(solution)/shard_map/all_to_all | solution.py:282
  12.2 2.0 %collective-permute-start = (bf16[4,64,256]{2,1,0:T(8,128)(2,1)S(1)}, bf16[4,64,256]{2,1,0:T(8,128)(2,1)S(1)}, u32[]{:S(2)}, u32[]{:S(2)}) collective-permute-start(bf16[4,64,256]{2,1,0:T(8,128)(2,1)S(1)} %copy-done.6), channel_id=1, source_target_pairs={{0,1},{1,0},{2,3},{3,2},{4,5},{5,4},{6,7},{7,6},{8,9},{9,8},{10,11... | collective-permute-start | bytes 393224 | tf_op jit(solution)/shard_map/ppermute | solution.py:17
  14.2 0.2 weights.1.refs_4_.refs_7_
  14.4 17.1 %all-gather = bf16[16,64,256]{2,1,0:T(8,128)(2,1)S(1)} all-gather(bf16[4,64,256]{2,1,0:T(8,128)(2,1)S(1)} %copy-done.2), channel_id=2, replica_groups={{0,2,4,6},{1,3,5,7},{8,10,12,14},{9,11,13,15},{16,18,20,22},{17,19,21,2..., dimensions={0}, use_global_device_ids=true | all-gather | bytes 655360 | tf_op jit(solution)/shard_map/all_gather | solution.py:284
  31.5 0.0 collective-permute-done
  31.6 2.0 %collective-permute-start.1 = (bf16[4,4,64,256]{3,2,1,0:T(8,128)(2,1)S(1)}, bf16[4,4,64,256]{3,2,1,0:T(8,128)(2,1)S(1)}, u32[]{:S(2)}, u32[]{:S(2)}) collective-permute-start(bf16[4,4,64,256]{3,2,1,0:T(8,128)(2,1)S(1)} %bitcast.16), channel_id=1, source_target_pairs={{0,1},{1,0},{2,3},{3,2},{4,5},{5,4},{6,7},{7,6},{8,9},{9,8},{10,11... | collective-permute-start | bytes 1572872 | tf_op jit(solution)/shard_map/ppermute | solution.py:17
  33.5 0.1 pad_add_fusion.where
  33.6 0.0 collective-permute-start.2
  33.6 2.4 %collective-permute-start.3 = (bf16[2,4,64,256]{3,2,1,0:T(8,128)(2,1)S(1)}, bf16[2,4,64,256]{3,2,1,0:T(8,128)(2,1)}, u32[]{:S(2)}, u32[]{:S(2)}) collective-permute-start(bf16[2,4,64,256]{3,2,1,0:T(8,128)(2,1)S(1)} %pad_maximum_fusion.refs_2_), channel_id=1, source_target_pairs={{0,4},{1,5},{2,6},{3,7},{4,0},{5,1},{6,2},{7,3},{8,12},{9,13},{10,... | collective-permute-start | bytes 786440 | tf_op jit(solution)/shard_map/ppermute | solution.py:17
  36.1 2.0 %collective-permute-start.4 = (bf16[2,4,64,256]{3,2,1,0:T(8,128)(2,1)S(1)}, bf16[2,4,64,256]{3,2,1,0:T(8,128)(2,1)}, u32[]{:S(2)}, u32[]{:S(2)}) collective-permute-start(bf16[2,4,64,256]{3,2,1,0:T(8,128)(2,1)S(1)} %pad_maximum_fusion.refs_2_), channel_id=1, source_target_pairs={{0,6},{1,7},{2,4},{3,5},{4,2},{5,3},{6,0},{7,1},{8,14},{9,15},{10,... | collective-permute-start | bytes 786440 | tf_op jit(solution)/shard_map/ppermute | solution.py:17
  38.0 0.0 all-to-all-done
  38.0 7.2 %all_gather.11.refs_2_ = bf16[4,512,128]{2,1,0:T(8,128)(2,1)S(1)} all-gather(bf16[1,512,128]{2,1,0:T(8,128)(2,1)S(1)} %bitcast.25), channel_id=1, replica_groups=mesh['seq'=4,'res'=8] {'seq'}, dimensions={0}, use_global_device_ids=true | all-gather | bytes 655360 | tf_op jit(solution)/shard_map/all_gather | solution.py:289
  45.3 0.0 collective-permute-done.1.refs_1_
  45.3 9.9 %attention.1 = (f32[4,128,512]{2,1,0:T(8,128)S(1)}, bf16[8,192,128]{2,1,0:T(8,128)(2,1)S(1)}, f32[1024,128]{1,0:T(8,128)S(1)}, f32[1024,128]{1,0:T(8,128)}) custom-call(s32[2]{0:T(128)S(1)} %pad_add_fusion.where, bf16[4,4,64,256]{3,2,1,0:T(8,128)(2,1)S(1)} %bitcast.17, bf16[4,4,64,256]{3,2,1,0:T(8,128)(2,1)S(1)} %collective-permute-done.1.refs_1_, ...), custom_call_target="tpu_custom_call" | custom-call | tf_op jit(solution)/shard_map/attention/pallas_call | solution.py:310
  55.1 0.8 copy-done.8
  55.9 0.0 collective-permute-done.2.refs_3_
  55.9 0.0 collective-permute-done.3.refs_4_
  55.9 0.0 collective-permute-done.4.refs_5_
  55.9 0.4 collective-permute-start.5
  56.3 4.1 %all-to-all-start.1 = ((bf16[8,192,128]{2,1,0:T(8,128)(2,1)}), bf16[8,192,128]{2,1,0:T(8,128)(2,1)}, u32[]{:S(2)}, u32[]{:S(2)}) async-start(bf16[8,192,128]{2,1,0:T(8,128)(2,1)} %copy-done.8), calls=%async_computation.1 | async-start | bytes 786432 | tf_op jit(solution)/shard_map/all_to_all | solution.py:357
  60.4 0.0 collective-permute-done.5
  60.4 1.8 %slice_add_fusion = (f32[512,128]{1,0:T(8,128)}, f32[512,128]{1,0:T(8,128)S(1)}) fusion(f32[1024,128]{1,0:T(8,128)} %collective-permute-done.5, f32[1024,128]{1,0:T(8,128)S(1)} %get-tuple-element.46), kind=kLoop, calls=%fused_computation.1 | loop fusion | flops 131072 | bytes 1572864 | tf_op jit(solution)/shard_map/add | solution.py:337
  62.2 0.8 collective-permute-start.7
  63.1 0.9 copy-done.5
  64.0 4.5 %gradients.1 = (bf16[8,64,128]{2,1,0:T(8,128)(2,1)S(1)}, f32[168,128]{1,0:T(8,128)S(1)}, f32[168,128]{1,0:T(8,128)S(1)}) custom-call(s32[2]{0:T(128)S(1)} %pad_add_fusion.where, bf16[4,4,64,256]{3,2,1,0:T(8,128)(2,1)S(1)} %bitcast.18, bf16[4,4,64,256]{3,2,1,0:T(8,128)(2,1)S(1)} %collective-permute-done.1.refs_1_, ...), custom_call_target="tpu_custom_call" | custom-call | tf_op jit(solution)/shard_map/gradients/pallas_call | solution.py:341
  68.5 0.0 copy-start.1
  68.5 0.1 collective-permute-start.6
  68.6 1.3 %collective-permute-done.6 = f32[168,128]{1,0:T(8,128)S(1)} collective-permute-done((f32[168,128]{1,0:T(8,128)S(1)}, f32[168,128]{1,0:T(8,128)S(1)}, u32[]{:S(2)}, u32[]{:S(2)}) %collective-permute-start.6) | collective-permute-done | bytes 86048 | tf_op jit(solution)/shard_map/ppermute | solution.py:17
  69.9 0.7 collective-permute-done.7.pair_come
  70.6 0.8 collective-permute-start.8
  71.5 1.3 %all-to-all-done.1.packed = bf16[8,192,128]{2,1,0:T(8,128)(2,1)} async-done(((bf16[8,192,128]{2,1,0:T(8,128)(2,1)}), bf16[8,192,128]{2,1,0:T(8,128)(2,1)}, u32[]{:S(2)}, u32[]{:S(2)}) %all-to-all-start.1) | async-done | bytes 393248 | tf_op jit(solution)/shard_map/all_to_all | solution.py:357
  72.7 2.4 %collective-permute-done.8.come = f32[168,128]{1,0:T(8,128)S(1)} collective-permute-done((f32[168,128]{1,0:T(8,128)S(1)}, f32[168,128]{1,0:T(8,128)S(1)}, u32[]{:S(2)}, u32[]{:S(2)}) %collective-permute-start.8) | collective-permute-done | bytes 86048 | tf_op jit(solution)/shard_map/ppermute | solution.py:17
  75.1 0.9 copy-done.3
  76.1 0.1 back.1
  76.1 21.3 %all_to_all.20.grad_ref.back.mine = bf16[8,304,128]{2,1,0:T(8,128)(2,1)S(1)} all-to-all(bf16[8,304,128]{2,1,0:T(8,128)(2,1)S(1)} %back.1), channel_id=1, replica_groups=mesh['seq'=4,'res'=8] {'res'}, dimensions={0} | all-to-all | bytes 1245184 | tf_op jit(solution)/shard_map/all_to_all | solution.py:373
  97.4 1.4 %pair.1 = f32[32,8,128]{2,1,0:T(8,128)} custom-call(bf16[8,304,128]{2,1,0:T(8,128)(2,1)S(1)} %all_to_all.20.grad_ref.back.mine, bf16[64,128,128]{2,1,0:T(8,128)(2,1)S(1)} %copy-done.1), custom_call_target="tpu_custom_call" | custom-call | tf_op jit(solution)/shard_map/pair/pallas_call | solution.py:374
  98.8 3.4 %all-to-all-start.3 = ((f32[32,8,128]{2,1,0:T(8,128)}), f32[32,8,128]{2,1,0:T(8,128)S(1)}, u32[]{:S(2)}, u32[]{:S(2)}) async-start(f32[32,8,128]{2,1,0:T(8,128)} %pair.1), calls=%async_computation.3 | async-start | bytes 262144 | tf_op jit(solution)/shard_map/all_to_all | solution.py:384
  102.2 2.2 %tail.1 = bf16[4,64,256]{2,1,0:T(8,128)(2,1)} custom-call(bf16[8,192,128]{2,1,0:T(8,128)(2,1)} %all-to-all-done.1.packed, bf16[8,304,128]{2,1,0:T(8,128)(2,1)S(1)} %all_to_all.20.grad_ref.back.mine, bf16[4,64,256]{2,1,0:T(8,128)(2,1)S(1)} %copy-done.2, bf16[8,128,256]{2,1,0:T(8,128)(2,1)S(1)} %weights.1.refs_4_.refs_7_, f32[1,256]{1,0:T(1,128)S(1)} %bitcast.24), custom_call_target="tpu_custom_call" | custom-call | tf_op jit(solution)/shard_map/tail/pallas_call | solution.py:389
  104.5 2.2 %convolution_convert_fusion = bf16[64,128,128]{2,1,0:T(8,128)(2,1)} fusion(bf16[8,64,128]{2,1,0:T(8,128)(2,1)S(1)} %slice.32, bf16[128,8]{0,1:T(8,128)(2,1)S(1)} %copy-done), kind=kOutput, calls=%fused_computation | convolution fusion | flops 17825792 | bytes 2230272 | tf_op jit(solution)/shard_map/hij,ch->ijc/dot_general | solution.py:385
  106.7 0.0 collective-permute-done.9.other
  106.7 3.1 %sums.1 = (f32[1,256]{1,0:T(1,128)}, f32[256,256]{1,0:T(8,128)}, f32[256,256]{1,0:T(8,128)}, f32[256,256]{1,0:T(8,128)}, f32[256,256]{1,0:T(8,128)}, /*index=5*/f32[256,256]{1,0:T(8,128)}) custom-call(s32[2]{0:T(128)S(1)} %pad_add_fusion.where, bf16[8,304,128]{2,1,0:T(8,128)(2,1)S(1)} %all_to_all.20.grad_ref.back.mine, ...), custom_call_target="tpu_custom_call" | custom-call | tf_op jit(solution)/shard_map/sums/pallas_call | solution.py:397
  109.8 0.2 all-to-all-done.3
  109.9 0.6 reduce_sum.9
  (25 shorter events, 0.1 us)
Async XLA Ops:
  0.6 0.7 copy-start
  0.7 3.0 %copy-start.2 = (bf16[4,64,256]{2,1,0:T(8,128)(2,1)S(1)}, bf16[4,64,256]{2,1,0:T(8,128)(2,1)}, u32[]{:S(2)}) copy-start(bf16[4,64,256]{2,1,0:T(8,128)(2,1)} %own_ref.2) | copy-start | bytes 393220
  0.7 3.0 %copy-start.6 = (bf16[4,64,256]{2,1,0:T(8,128)(2,1)S(1)}, bf16[4,64,256]{2,1,0:T(8,128)(2,1)}, u32[]{:S(2)}) copy-start(bf16[4,64,256]{2,1,0:T(8,128)(2,1)} %slope_ref.1) | copy-start | bytes 393220
  0.7 3.0 %copy-start.7 = (bf16[256,256]{1,0:T(8,128)(2,1)S(1)}, bf16[256,256]{1,0:T(8,128)(2,1)}, u32[]{:S(2)}) copy-start(bf16[256,256]{1,0:T(8,128)(2,1)} %refs_3_.1) | copy-start | bytes 393220
  0.7 3.0 %copy-start.4 = (bf16[256,256]{1,0:T(8,128)(2,1)S(1)}, bf16[256,256]{1,0:T(8,128)(2,1)}, u32[]{:S(2)}) copy-start(bf16[256,256]{1,0:T(8,128)(2,1)} %out_w.1) | copy-start | bytes 393220
  0.7 3.0 %copy-start.12 = (f32[256]{0:T(256)S(1)}, f32[256]{0:T(256)}, u32[]{:S(2)}) copy-start(f32[256]{0:T(256)} %param.13) | copy-start | bytes 3076
  0.7 13.5 %copy-start.9 = (bf16[256,256]{1,0:T(8,128)(2,1)S(1)}, bf16[256,256]{1,0:T(8,128)(2,1)}, u32[]{:S(2)}) copy-start(bf16[256,256]{1,0:T(8,128)(2,1)} %refs_0_.1) | copy-start | bytes 393220
  0.7 13.5 %copy-start.10 = (bf16[256,256]{1,0:T(8,128)(2,1)S(1)}, bf16[256,256]{1,0:T(8,128)(2,1)}, u32[]{:S(2)}) copy-start(bf16[256,256]{1,0:T(8,128)(2,1)} %refs_1_.1) | copy-start | bytes 393220
  1.3 12.9 %copy-start.11 = (bf16[256,256]{1,0:T(8,128)(2,1)S(1)}, bf16[256,256]{1,0:T(8,128)(2,1)}, u32[]{:S(2)}) copy-start(bf16[256,256]{1,0:T(8,128)(2,1)} %refs_2_.1) | copy-start | bytes 393220
  4.9 33.1 %all-to-all-start = ((bf16[8,128,128]{2,1,0:T(8,128)(2,1)}), bf16[8,128,128]{2,1,0:T(8,128)(2,1)S(1)}, u32[]{:S(2)}, u32[]{:S(2)}) async-start(bf16[8,128,128]{2,1,0:T(8,128)(2,1)} %ready.1), calls=%async_computation | async-start | bytes 524288 | tf_op jit(solution)/shard_map/all_to_all | solution.py:282
  12.2 19.4 %collective-permute-start = (bf16[4,64,256]{2,1,0:T(8,128)(2,1)S(1)}, bf16[4,64,256]{2,1,0:T(8,128)(2,1)S(1)}, u32[]{:S(2)}, u32[]{:S(2)}) collective-permute-start(bf16[4,64,256]{2,1,0:T(8,128)(2,1)S(1)} %copy-done.6), channel_id=1, source_target_pairs={{0,1},{1,0},{2,3},{3,2},{4,5},{5,4},{6,7},{7,6},{8,9},{9,8},{10,11... | collective-permute-start | bytes 393224 | tf_op jit(solution)/shard_map/ppermute | solution.py:17
  31.6 13.7 %collective-permute-start.1 = (bf16[4,4,64,256]{3,2,1,0:T(8,128)(2,1)S(1)}, bf16[4,4,64,256]{3,2,1,0:T(8,128)(2,1)S(1)}, u32[]{:S(2)}, u32[]{:S(2)}) collective-permute-start(bf16[4,4,64,256]{3,2,1,0:T(8,128)(2,1)S(1)} %bitcast.16), channel_id=1, source_target_pairs={{0,1},{1,0},{2,3},{3,2},{4,5},{5,4},{6,7},{7,6},{8,9},{9,8},{10,11... | collective-permute-start | bytes 1572872 | tf_op jit(solution)/shard_map/ppermute | solution.py:17
  33.6 22.3 %collective-permute-start.2 = (bf16[2,4,64,256]{3,2,1,0:T(8,128)(2,1)S(1)}, bf16[2,4,64,256]{3,2,1,0:T(8,128)(2,1)}, u32[]{:S(2)}, u32[]{:S(2)}) collective-permute-start(bf16[2,4,64,256]{3,2,1,0:T(8,128)(2,1)S(1)} %pad_maximum_fusion.refs_2_), channel_id=1, source_target_pairs={{0,2},{1,3},{2,0},{3,1},{4,6},{5,7},{6,4},{7,5},{8,10},{9,11},{10,... | collective-permute-start | bytes 786440 | tf_op jit(solution)/shard_map/ppermute | solution.py:17
  33.6 22.3 %collective-permute-start.3 = (bf16[2,4,64,256]{3,2,1,0:T(8,128)(2,1)S(1)}, bf16[2,4,64,256]{3,2,1,0:T(8,128)(2,1)}, u32[]{:S(2)}, u32[]{:S(2)}) collective-permute-start(bf16[2,4,64,256]{3,2,1,0:T(8,128)(2,1)S(1)} %pad_maximum_fusion.refs_2_), channel_id=1, source_target_pairs={{0,4},{1,5},{2,6},{3,7},{4,0},{5,1},{6,2},{7,3},{8,12},{9,13},{10,... | collective-permute-start | bytes 786440 | tf_op jit(solution)/shard_map/ppermute | solution.py:17
  36.1 19.9 %collective-permute-start.4 = (bf16[2,4,64,256]{3,2,1,0:T(8,128)(2,1)S(1)}, bf16[2,4,64,256]{3,2,1,0:T(8,128)(2,1)}, u32[]{:S(2)}, u32[]{:S(2)}) collective-permute-start(bf16[2,4,64,256]{3,2,1,0:T(8,128)(2,1)S(1)} %pad_maximum_fusion.refs_2_), channel_id=1, source_target_pairs={{0,6},{1,7},{2,4},{3,5},{4,2},{5,3},{6,0},{7,1},{8,14},{9,15},{10,... | collective-permute-start | bytes 786440 | tf_op jit(solution)/shard_map/ppermute | solution.py:17
  55.1 0.8 copy-start.8
  55.9 4.5 %collective-permute-start.5 = (f32[1024,128]{1,0:T(8,128)}, f32[1024,128]{1,0:T(8,128)}, u32[]{:S(2)}, u32[]{:S(2)}) collective-permute-start(f32[1024,128]{1,0:T(8,128)} %get-tuple-element.47), channel_id=1, source_target_pairs={{0,8},{8,0},{16,24},{24,16},{1,9},{9,1},{17,25},{25,17},{2,10},{10... | collective-permute-start | bytes 1572872 | tf_op jit(solution)/shard_map/ppermute | solution.py:17
  56.3 16.4 %all-to-all-start.1 = ((bf16[8,192,128]{2,1,0:T(8,128)(2,1)}), bf16[8,192,128]{2,1,0:T(8,128)(2,1)}, u32[]{:S(2)}, u32[]{:S(2)}) async-start(bf16[8,192,128]{2,1,0:T(8,128)(2,1)} %copy-done.8), calls=%async_computation.1 | async-start | bytes 786432 | tf_op jit(solution)/shard_map/all_to_all | solution.py:357
  62.2 8.4 %collective-permute-start.7 = (f32[512,128]{1,0:T(8,128)S(1)}, f32[512,128]{1,0:T(8,128)S(1)}, u32[]{:S(2)}, u32[]{:S(2)}) collective-permute-start(f32[512,128]{1,0:T(8,128)S(1)} %get-tuple-element.52), channel_id=1, source_target_pairs={{0,16},{8,24},{16,0},{24,8},{1,17},{9,25},{17,1},{25,9},{2,18},{10... | collective-permute-start | bytes 786440 | tf_op jit(solution)/shard_map/ppermute | solution.py:17
  63.1 0.9 copy-start.5
  68.5 28.9 %copy-start.1 = (bf16[64,128,128]{2,1,0:T(8,128)(2,1)S(1)}, bf16[64,128,128]{2,1,0:T(8,128)(2,1)}, u32[]{:S(2)}) copy-start(bf16[64,128,128]{2,1,0:T(8,128)(2,1)} %rows_ref.1) | copy-start | bytes 6291460
  68.5 1.3 %collective-permute-start.6 = (f32[168,128]{1,0:T(8,128)S(1)}, f32[168,128]{1,0:T(8,128)S(1)}, u32[]{:S(2)}, u32[]{:S(2)}) collective-permute-start(f32[168,128]{1,0:T(8,128)S(1)} %get-tuple-element.51), channel_id=1, source_target_pairs={{0,8},{8,0},{16,24},{24,16},{1,9},{9,1},{17,25},{25,17},{2,10},{10... | collective-permute-start | bytes 258056 | tf_op jit(solution)/shard_map/ppermute | solution.py:17
  70.6 4.5 %collective-permute-start.8 = (f32[168,128]{1,0:T(8,128)S(1)}, f32[168,128]{1,0:T(8,128)S(1)}, u32[]{:S(2)}, u32[]{:S(2)}) collective-permute-start(f32[168,128]{1,0:T(8,128)S(1)} %add.10.keep), channel_id=1, source_target_pairs={{0,16},{8,24},{16,0},{24,8},{1,17},{9,25},{17,1},{25,9},{2,18},{10... | collective-permute-start | bytes 258056 | tf_op jit(solution)/shard_map/ppermute | solution.py:17
  75.1 1.0 copy-start.3
  97.4 9.3 %collective-permute-start.9 = (bf16[8,304,128]{2,1,0:T(8,128)(2,1)S(1)}, bf16[8,304,128]{2,1,0:T(8,128)(2,1)}, u32[]{:S(2)}, u32[]{:S(2)}) collective-permute-start(bf16[8,304,128]{2,1,0:T(8,128)(2,1)S(1)} %all_to_all.20.grad_ref.back.mine), channel_id=1, source_target_pairs={{0,8},{8,0},{16,24},{24,16},{1,9},{9,1},{17,25},{25,17},{2,10},{10... | collective-permute-start | bytes 1867784 | tf_op jit(solution)/shard_map/ppermute | solution.py:17
  98.8 11.1 %all-to-all-start.3 = ((f32[32,8,128]{2,1,0:T(8,128)}), f32[32,8,128]{2,1,0:T(8,128)S(1)}, u32[]{:S(2)}, u32[]{:S(2)}) async-start(f32[32,8,128]{2,1,0:T(8,128)} %pair.1), calls=%async_computation.3 | async-start | bytes 262144 | tf_op jit(solution)/shard_map/all_to_all | solution.py:384
